TPU v7x, 128 devices: a whole 4x4x4 slice. The times are simulated.
128 devices in a mesh: tau: 16 (over z, x_lo, core), aux: 8 (over x_hi, y).
Axes of the slice: x: 4 (x_hi: 2, x_lo: 2; x = x_hi * 2 + x_lo), y: 4, z: 4, core: 2. Of those that a mesh axis runs over, the one named last changes fastest.
Arguments:
- green_tau: bfloat16 [128, 256, 20480], P('tau', None, 'aux'), may hold values from -6 to 6
- fit_matrix: bfloat16 [72, 128], replicated, may hold values from -0.5 to 0.5
- aux_factors: bfloat16 [2048, 20480], P(None, 'aux'), may hold values from -0.0625 to 0.0625
- freq_basis: float32 [240, 72], replicated, may hold values from -0.75 to 0.75
- screened: float32 [120, 2048], P(None, 'aux'), may hold values from 0.5 to 2
- pair_mask: int32 [256, 160], P('tau', 'aux'), may hold values 0 or 1
Outputs:
- sigma: float32 [240, 256, 2048], P(None, 'tau', 'aux')
All inputs are finite; a program needn't handle non-finite values. No bound on the sum of `pair_mask` on one device may be relied on, other than what follows from the above.
Results may differ from a plain program's by a relative error of at most 0.0029.
Values may be sent and summed in bfloat16 or wider, within the bound.
No kernel may reach another device: no remote copies, remote signals or barrier semaphores. Data moves between devices by JAX's collectives and lax.ppermute only.
A program may use at most 128 MiB of HBM per device.

v0:
```python
import jax
import jax.numpy as jnp
from jax import lax
from jax.sharding import PartitionSpec as P

BLOCK = 128


def body(green_tau, fit_matrix, aux_factors, freq_basis, screened, pair_mask):
    row_dev = pair_mask.shape[0]
    tile_cols = green_tau.shape[2]
    n_coef = fit_matrix.shape[0]
    tile_width = aux_factors.shape[0] // lax.axis_size("aux")
    coeff = jnp.einsum(
        "lt,tmb->lmb",
        fit_matrix,
        lax.all_to_all(green_tau, "tau", split_axis=1, concat_axis=0, tiled=True),
        preferred_element_type=jnp.float32,
    )
    keeper = pair_mask.astype(jnp.float32)
    blocked = coeff.reshape(n_coef, row_dev, tile_cols // BLOCK, BLOCK) * keeper[None, :, :, None]
    flat = blocked.astype(jnp.bfloat16).reshape(n_coef * row_dev, tile_cols)
    total = lax.psum(
        jnp.einsum("pb,kb->pk", aux_factors, flat, preferred_element_type=jnp.float32), "aux"
    )
    owned = lax.dynamic_slice_in_dim(total, lax.axis_index("aux") * tile_width, tile_width, 0)
    owned = owned.reshape(tile_width, n_coef, row_dev)
    mixed = jnp.einsum("wl,plm->wmp", freq_basis, owned, precision=lax.Precision.HIGHEST)
    weight = jnp.concatenate([screened, screened], axis=0)
    return mixed * weight[:, None, :]


def solution(mesh):
    return jax.shard_map(
        body,
        mesh=mesh,
        in_specs=(P("tau", None, "aux"), P(), P(None, "aux"), P(), P(None, "aux"), P("tau", "aux")),
        out_specs=P(None, "tau", "aux"),
        check_vma=False,
    )
```

profile of v0, /device:TPU:1, one launch (start us, length us, event | category | flops | bytes accessed | tf_op | source)
XLA Modules:
  0.0 428.1 jit_solution(14544943446789057598)
XLA Ops:
  6.5 0.0 copy-start
  6.5 13.6 %copy.18 = bf16[8,256,2560]{2,0,1:T(8,128)(2,1)} copy(bf16[8,256,2560]{2,1,0:T(8,128)(2,1)} %param.6) | data formatting | bytes 20971520 | tf_op args[0]
  20.1 0.0 copy-start.3
  20.1 7.9 %all-to-all-start = ((bf16[8,256,2560]{2,0,1:T(8,128)(2,1)}), bf16[8,256,2560]{2,0,1:T(8,128)(2,1)}, u32[]{:S(2)}, u32[]{:S(2)}) async-start(bf16[8,256,2560]{2,0,1:T(8,128)(2,1)} %copy.18), calls=%async_computation | async-start | bytes 20971520 | tf_op jit(solution)/shard_map/all_to_all | solution.py:17
  28.0 0.0 all-reduce.2.cloned.1.call-start
  28.1 0.0 copy-done.3
  28.1 117.0 %all-to-all-done = bf16[8,256,2560]{2,0,1:T(8,128)(2,1)} async-done(((bf16[8,256,2560]{2,0,1:T(8,128)(2,1)}), bf16[8,256,2560]{2,0,1:T(8,128)(2,1)}, u32[]{:S(2)}, u32[]{:S(2)}) %all-to-all-start) | async-done | bytes 10485792 | tf_op jit(solution)/shard_map/all_to_all | solution.py:17
  145.1 11.9 %copy.20 = bf16[16,8,16,2560]{3,2,1,0:T(8,128)(2,1)} copy(bf16[16,8,16,2560]{3,1,2,0:T(8,128)(2,1)} %bitcast.4) | data formatting | bytes 20971520 | tf_op jit(solution)/shard_map/all_to_all | solution.py:17
  157.0 0.0 copy-start.2
  157.0 14.6 %copy.21 = bf16[16,2560,128]{2,1,0:T(8,128)(2,1)} copy(bf16[16,2560,128]{1,0,2:T(8,128)(2,1)} %bitcast.28) | data formatting | bytes 20971520 | tf_op jit(solution)/shard_map/lt,tmb->lmb/dot_general | solution.py:14
  171.6 0.0 copy-done.2
  171.6 10.4 %multiply_convert_fusion = bf16[72,16,20,128]{3,0,2,1:T(8,128)(2,1)S(1)} fusion(f32[16,20]{1,0:T(8,128)S(1)} %convert_element_type.6, bf16[16,20,128,128]{3,2,1,0:T(8,128)(2,1)} %bitcast.27, bf16[72,128]{1,0:T(8,128)(2,1)S(1)} %copy-done.2), kind=kOutput, calls=%fused_computation | convolution fusion | flops 760872960 | bytes 16403712 | tf_op jit(solution)/shard_map/lt,tmb->lmb/dot_general | solution.py:14
  182.0 4.7 %copy.22 = bf16[72,16,20,128]{3,2,1,0:T(8,128)(2,1)} copy(bf16[72,16,20,128]{3,0,2,1:T(8,128)(2,1)S(1)} %multiply_convert_fusion) | data formatting | bytes 11796480 | tf_op jit(solution)/shard_map/convert_element_type | solution.py:22
  186.8 19.5 %convolution_bitcast_fusion = f32[2048,1152]{0,1:T(8,128)} fusion(bf16[2048,2560]{1,0:T(8,128)(2,1)} %param.8, bf16[144,8,20,128]{3,2,1,0:T(8,128)(2,1)} %bitcast.29), kind=kOutput, calls=%fused_computation.1 | convolution fusion | flops 12079595520 | bytes 25821184 | tf_op jit(solution)/shard_map/pb,kb->pk/dot_general | solution.py:24
  206.2 0.0 copy-start.1
  206.2 0.0 all-reduce.2.cloned.1.call-update
  206.3 0.9 copy-done.1
  207.2 204.6 %all-reduce.2.cloned.1.call-done = f32[2048,1152]{0,1:T(8,128)} async-done(((f32[2048,1152]{0,1:T(8,128)}), f32[2048,1152]{0,1:T(8,128)}) %all-reduce.2.cloned.1.call-update) | async-done | bytes 9437200 | tf_op jit(solution)/shard_map/psum | solution.py:23
  411.8 1.3 constant_dynamic-slice_fusion
  413.1 0.0 copy-done
  413.1 3.9 bitcast_multiply_fusion
  417.0 4.2 copy.24
  (2 shorter events, 0.0 us)
Async XLA Ops:
  6.5 406.6 %copy-start = (f32[240,72]{0,1:T(8,128)S(1)}, f32[240,72]{0,1:T(8,128)}, u32[]{:S(2)}) copy-start(f32[240,72]{0,1:T(8,128)} %param.9) | copy-start | bytes 207364
  20.1 7.9 %copy-start.3 = (s32[16,20]{1,0:T(8,128)S(1)}, s32[16,20]{1,0:T(8,128)}, u32[]{:S(2)}) copy-start(s32[16,20]{1,0:T(8,128)} %param.11) | copy-start | bytes 3844
  20.1 125.0 %all-to-all-start = ((bf16[8,256,2560]{2,0,1:T(8,128)(2,1)}), bf16[8,256,2560]{2,0,1:T(8,128)(2,1)}, u32[]{:S(2)}, u32[]{:S(2)}) async-start(bf16[8,256,2560]{2,0,1:T(8,128)(2,1)} %copy.18), calls=%async_computation | async-start | bytes 20971520 | tf_op jit(solution)/shard_map/all_to_all | solution.py:17
  28.0 383.7 %all-reduce.2.cloned.1.call-start = ((), (), s32[]{:S(2)}) async-start(), calls=%async_computation.1 | async-start | bytes 18874368 | tf_op jit(solution)/shard_map/psum | solution.py:23
  157.0 14.6 %copy-start.2 = (bf16[72,128]{1,0:T(8,128)(2,1)S(1)}, bf16[72,128]{1,0:T(8,128)(2,1)}, u32[]{:S(2)}) copy-start(bf16[72,128]{1,0:T(8,128)(2,1)} %param.7) | copy-start | bytes 55300
  206.2 0.9 copy-start.1
Sparse Core Ops, SparseCore 0:
  206.4 205.3 all-reduce.1
where the time goes:
time: 429 us; the launch traced here: 428 us
  waiting for transfers between devices  322 us (75%)
  local copies, waits for them, and re-layouts  51.3 us (12%)
  matrix products  33.8 us (8%)
  between operations  13.4 us (3%)
  starting transfers between devices  7.93 us (2%)
    psum x1, waiting for transfers between devices, body(): lax.psum(jnp.einsum('pb,kb->pk', aux_factors, flat, preferred_element_typ...  205 us
    all_to_all x1, waiting for transfers between devices, body(): lax.all_to_all(green_tau, 'tau', split_axis=1, concat_axis=0, tiled=True)  117 us
    dot_general x1, matrix products, body(): jnp.einsum('pb,kb->pk', aux_factors, flat, preferred_element_type=jnp.flo...  19.5 us
    dot_general x1, local copies, waits for them, and re-layouts, body(): jnp.einsum('lt,tmb->lmb', fit_matrix, lax.all_to_all(green_tau, 'tau', sp...  14.6 us
    unnamed x9, local copies, waits for them, and re-layouts  14.5 us
    all_to_all x1, local copies, waits for them, and re-layouts, body(): lax.all_to_all(green_tau, 'tau', split_axis=1, concat_axis=0, tiled=True)  11.9 us
    dot_general x1, matrix products, body(): jnp.einsum('lt,tmb->lmb', fit_matrix, lax.all_to_all(green_tau, 'tau', sp...  10.4 us
  transfers between devices with their start and end apart: 2, of which 2 were waited for; matrix products, arithmetic and copies ran while one was open for 0% of the time, Pallas kernels for 0%

commit v1 on v0

v1 whole, which is shorter than its diff:
```python
import jax
import jax.numpy as jnp
import numpy as np
from jax import lax
from jax.experimental import pallas as pl
from jax.experimental.pallas import tpu as pltpu
from jax.sharding import Mesh, PartitionSpec as P

BLOCK = 128
LANES = 128
AWAY = (2, 1, 3)
PARAMS = pltpu.CompilerParams(vmem_limit_bytes=56 * 2**20)
ANY = pl.BlockSpec(memory_space=pl.ANY)


def fill(g_refs, mask_ref, picks, rows_ref):
    times, _, height, cols = g_refs[0].shape
    for i, g_ref in enumerate(g_refs):
        marks = mask_ref[picks[i]].astype(jnp.float32)
        for k in range(cols // BLOCK):
            keep = jnp.broadcast_to(marks[:, k : k + 1], (height, BLOCK)).astype(jnp.bfloat16)
            at = slice(k * BLOCK, (k + 1) * BLOCK)
            for t in range(times):
                row = (i * times + t) * height
                rows_ref[row : row + height, at] = g_ref[t, 0, :, at] * keep


def product(rows_ref, a):
    return lax.dot_general(rows_ref[...], a, (((1,), (1,)), ((), ())), preferred_element_type=jnp.float32)


def cross_kernel(at, mask_ref, g0, g1, g2, g3, a_ref, b_ref, l_ref, h_ref, o_ref, rows_ref):
    j = pl.program_id(0)

    @pl.when(j == 0)
    def _():
        c = at[2]
        fill((g0, g1, g2, g3), mask_ref, (c, 1 - c, 2 + c, 3 - c), rows_ref)

    part = rows_ref.shape[0] // 4
    width = o_ref.shape[3]

    def put(near_ref, far_ref):
        v = product(rows_ref, a_ref[0])
        for k in range(2):
            for f in range(2):
                at_col = slice(k * width, (k + 1) * width)
                near_ref[f, k] = v[f * part : (f + 1) * part, at_col].astype(near_ref.dtype)
                far_ref[f, k] = v[(2 + f) * part : (3 + f) * part, at_col].astype(far_ref.dtype)

    @pl.when(j < 2)
    def _():
        put(h_ref, b_ref)

    @pl.when(j >= 2)
    def _():
        put(o_ref, l_ref)


def far_kernel(at, mask_ref, g0, g1, g2, g3, a0, a1, after, lo_ref, hi_ref, rows_ref):
    fill((g0, g1, g2, g3), mask_ref, range(4), rows_ref)
    lo_ref[...] = product(rows_ref, a0[0, 0]).astype(jnp.bfloat16)
    hi_ref[...] = product(rows_ref, a1[0, 0]).astype(jnp.bfloat16)


def near_kernel(at, mask_ref, g0, g1, g2, g3, a0, a1, from_up, from_down, after, down_ref, up_ref, rows_ref):
    s = pl.program_id(1)

    @pl.when(s == 0)
    def _():
        fill((g0, g1, g2, g3), mask_ref, range(4), rows_ref)
        down_ref[0, 0] = (product(rows_ref, a0[0, 0]) + from_up[...].astype(jnp.float32)).astype(jnp.bfloat16)
        down_ref[0, 1] = product(rows_ref, a1[0, 0]).astype(jnp.bfloat16)

    @pl.when(s == 1)
    def _():
        up_ref[0, 0] = product(rows_ref, a0[0, 0]).astype(jnp.bfloat16)
        up_ref[0, 1] = (product(rows_ref, a1[0, 0]) + from_down[...].astype(jnp.float32)).astype(jnp.bfloat16)


def own_kernel(at, mask_ref, g0, g1, g2, g3, a0, a1, after, own_ref, rows_ref):
    fill((g0, g1, g2, g3), mask_ref, range(4), rows_ref)
    own_ref[0, 0] = product(rows_ref, a0[0, 0])
    own_ref[0, 1] = product(rows_ref, a1[0, 0])


def final_kernel(w_ref, s_ref, x0_ref, xk_ref, xr_ref, o_ref):
    n_freq, n_time = w_ref.shape
    height = o_ref.shape[0] // n_freq
    part = 8 * height
    w = w_ref[...]
    high = w.astype(jnp.bfloat16)
    low = (w - high.astype(jnp.float32)).astype(jnp.bfloat16)
    twice = jnp.concatenate([high, high], axis=1)
    scale = jnp.concatenate([s_ref[...], s_ref[...]], axis=0)

    def row(m):
        return jnp.concatenate(
            [
                ref[pl.ds(i * part + m, 8, stride=height), :]
                for ref in (x0_ref, xk_ref, xr_ref)
                for i in range(ref.shape[0] // part)
            ],
            axis=0,
        )

    for m in range(0, height, 2):
        x = jnp.concatenate([row(m), row(m + 1)], axis=1)
        x_high = x.astype(jnp.bfloat16)
        x_low = (x - x_high.astype(jnp.float32)).astype(jnp.bfloat16)
        mixed = jnp.dot(
            twice, jnp.concatenate([x_high, x_low], axis=0), preferred_element_type=jnp.float32
        ) + jnp.dot(low, x_high, preferred_element_type=jnp.float32)
        o_ref[pl.ds(m, n_freq, stride=height), :] = mixed[:, :LANES] * scale
        o_ref[pl.ds(m + 1, n_freq, stride=height), :] = mixed[:, LANES:] * scale


def body(green_tau, fit_matrix, aux_factors, freq_basis, screened, pair_mask):
    z, xl, c, xh, y = (lax.axis_index(a) for a in ("z", "xl", "c", "xh", "y"))
    nz, ny = lax.axis_size("z"), lax.axis_size("y")
    times, n_rows, cols = green_tau.shape
    height = pair_mask.shape[0]
    green = green_tau.reshape(times, n_rows // height, height, cols)
    n_aux = aux_factors.shape[0]
    width = n_aux // (2 * ny)
    aux = aux_factors.reshape(2, ny, width, cols)
    part = times * height
    rows = 4 * part
    f32, bf16 = jnp.float32, jnp.bfloat16

    def shift(v, axis, by):
        n = lax.axis_size(axis)
        return lax.ppermute(v, axis, [(i, (i + by) % n) for i in range(n)])

    def flip(v, axis):
        return lax.ppermute(v, axis, [(0, 1), (1, 0)])

    def send(v, d, e, h):
        pairs = [
            (i * 4 + j * 2 + k, (i + d) % nz * 4 + (j ^ e) * 2 + (k ^ h))
            for i in range(nz) for j in (0, 1) for k in (0, 1)
        ]
        return lax.ppermute(v, ("z", "xl", "xh"), pairs)

    pair = jnp.stack([pair_mask, flip(pair_mask, "c")])
    quad = jnp.concatenate([pair, flip(pair, "xl")])
    away = [shift(quad, "z", -d) for d in AWAY]

    owners = [z * 4 + (xl ^ e) * 2 + f for e in (0, 1) for f in (0, 1)]
    owners += [(z + d) % nz * 4 + (xl ^ e) * 2 + (c ^ f) for d in AWAY for e in (0, 1) for f in (0, 1)]
    at = jnp.stack([xh, y, c] + owners).astype(jnp.int32)

    def inputs(first, marks):
        def chunk(g):
            return first + g[0] if first else 0

        def owner(i):
            return lambda *g: (0, g[-1][3 + chunk(g) * 4 + i], 0, 0)

        return [pl.BlockSpec((4, *marks.shape[1:]), lambda *g: (g[0] if first else 0, 0, 0))] + [
            pl.BlockSpec((times, 1, height, cols), owner(i)) for i in range(4)
        ]

    def aux_at(h, target):
        return pl.BlockSpec((1, 1, width, cols), lambda *g: (g[-1][0] ^ h, target(*g), 0, 0))

    def call(kernel, grid, in_specs, out_specs, out_shape, args, columns):
        return pl.pallas_call(
            kernel,
            grid_spec=pltpu.PrefetchScalarGridSpec(
                num_scalar_prefetch=1,
                grid=grid,
                in_specs=in_specs,
                out_specs=out_specs,
                scratch_shapes=[pltpu.VMEM((rows, cols), bf16)],
            ),
            out_shape=out_shape,
            compiler_params=PARAMS,
            cost_estimate=pl.CostEstimate(
                flops=2 * rows * cols * columns, bytes_accessed=2 * cols * (rows + columns), transcendentals=0
            ),
        )(at, *args)

    def many(n):
        return jax.ShapeDtypeStruct((2, ny, part, width), n)

    first = pl.BlockSpec((2, 2, part, width), lambda j, at: (0, jnp.minimum(j, 1), 0, 0))
    second = pl.BlockSpec((2, 2, part, width), lambda j, at: (0, jnp.maximum(j - 2, 0), 0, 0))
    to_both, to_low, to_high, kept = call(
        cross_kernel, (4,),
        inputs(0, quad)
        + [pl.BlockSpec((1, n_aux // 4, cols), lambda j, at: (at[0] ^ (1 - j // 2), j % 2, 0))],
        [first, second, first, second],
        [many(bf16), many(bf16), many(bf16), many(f32)],
        (quad, green, green, green, green, aux_factors.reshape(2, n_aux // 2, cols)), n_aux,
    )
    got_both, got_low, got_high = send(to_both, 0, 1, 1), send(to_low, 0, 1, 0), send(to_high, 0, 0, 1)

    def far(i, n, after):
        marks = jnp.concatenate(away[i : i + n])
        two = lambda q, at: (at[1] + 2) % ny
        out = pl.BlockSpec((rows, width), lambda q, at: (q, 0))
        shape = jax.ShapeDtypeStruct((n * rows, width), bf16)
        lo, hi = call(
            far_kernel, (n,), inputs(1 + i, marks) + [aux_at(0, two), aux_at(1, two), ANY],
            [out, out], [shape, shape], (marks, *[green] * 4, aux, aux, after), 2 * width * n,
        )
        return lo, shift(lo, "y", -1), shift(hi, "y", 1)

    def near(i, n, lo, hi, after):
        marks = jnp.concatenate(away[i : i + n])
        side = lambda q, s, at: (at[1] + ny - 1 + 2 * s) % ny
        got = pl.BlockSpec((rows, width), lambda q, s, at: (q, 0))
        out = pl.BlockSpec((1, 2, rows, width), lambda q, s, at: (q, 0, 0, 0))
        shape = jax.ShapeDtypeStruct((n, 2, rows, width), bf16)
        down, up = call(
            near_kernel, (n, 2), inputs(1 + i, marks) + [aux_at(0, side), aux_at(1, side), got, got, ANY],
            [out, out], [shape, shape], (marks, *[green] * 4, aux, aux, lo, hi, after), 4 * width * n,
        )
        return down, shift(down, "y", -1), shift(up, "y", 1)

    lo_a, up_a, down_a = far(0, 1, kept)
    lo_b, up_b, down_b = far(1, 2, lo_a)
    near_a, from_up_a, from_down_a = near(0, 1, up_a, down_a, lo_b)
    near_b, from_up_b, from_down_b = near(1, 2, up_b, down_b, near_a)
    marks = jnp.concatenate(away)
    here = lambda q, at: at[1]
    own = call(
        own_kernel, (3,), inputs(1, marks) + [aux_at(0, here), aux_at(1, here), ANY],
        pl.BlockSpec((1, 2, rows, width), lambda q, at: (q, 0, 0, 0)),
        jax.ShapeDtypeStruct((3, 2, rows, width), f32), (marks, *[green] * 4, aux, aux, near_b), 6 * width,
    )

    def deliver(d, total):
        quarter = total.reshape(2, 2, 2 * part, width)
        r00 = send(quarter[0, 0], d, 0, 0)
        r01 = send(quarter[0, 1].astype(bf16), d, 1, 0)
        r10 = send(quarter[1, 0].astype(bf16), d, 0, 1)
        r11 = send(quarter[1, 1].astype(bf16), d, 1, 1)
        return r00 + r10.astype(f32), r01.astype(f32) + r11.astype(f32)

    pieces = []
    for k, d in enumerate(AWAY):
        up, down = (from_up_a[0], from_down_a[0]) if k == 0 else (from_up_b[k - 1], from_down_b[k - 1])
        pieces += deliver(d, own[k] + (up.astype(f32) + down.astype(f32)))
    x_kept = jnp.concatenate([v[:part] for v in pieces])
    x_got = flip(jnp.concatenate([v[part:] for v in pieces]), "c")

    zero = kept + got_high.astype(f32)
    one = got_both.astype(f32) + got_low.astype(f32)
    crossing = jnp.stack([zero, one], axis=2).astype(bf16).reshape(2 * ny, 2, part, width)
    crossing, _ = lax.optimization_barrier((crossing, from_up_b))
    crossed = lax.all_to_all(crossing, ("c", "y"), split_axis=0, concat_axis=0, tiled=True)
    x_home = crossed.reshape(2, ny, 2, part, width).astype(f32).sum(axis=1).reshape(4 * part, width)

    order = [z * 4 + (xl ^ e) * 2 + f for f in (0, 1) for e in (0, 1)]
    for side in (c, 1 - c):
        order += [(z + nz - d) % nz * 4 + (xl ^ e) * 2 + side for d in AWAY for e in (0, 1)]
    source = (jnp.stack(order)[:, None] * times + jnp.arange(times)[None, :]).reshape(1, -1)
    n_time = source.shape[1]
    pick = (jnp.arange(n_time)[:, None] == source).astype(f32)
    exact = lax.Precision.HIGHEST
    picked = jnp.dot(fit_matrix.astype(f32), pick, precision=exact)
    weights = jnp.dot(freq_basis, picked, precision=exact)

    n_freq = weights.shape[0]
    lane = lambda v: pl.BlockSpec((v.shape[0], LANES), lambda j: (0, j))
    sigma = pl.pallas_call(
        final_kernel,
        grid=(width // LANES,),
        in_specs=[pl.BlockSpec(weights.shape, lambda j: (0, 0))] + [lane(v) for v in (screened, x_home, x_kept, x_got)],
        out_specs=pl.BlockSpec((n_freq * height, LANES), lambda j: (0, j)),
        out_shape=jax.ShapeDtypeStruct((n_freq * height, width), f32),
        compiler_params=PARAMS,
    )(weights, screened, x_home, x_kept, x_got)
    return sigma.reshape(n_freq, height, width)


def solution(mesh):
    devices = np.array(mesh.devices).reshape(4, 2, 2, 2, 4)
    fine = Mesh(devices, ("z", "xl", "c", "xh", "y"))
    tau, aux = ("z", "xl", "c"), ("xh", "y")
    return jax.shard_map(
        body,
        mesh=fine,
        in_specs=(P(tau, None, aux), P(), P(None, aux), P(), P(None, aux), P(tau, aux)),
        out_specs=P(None, tau, aux),
        check_vma=False,
    )
```

time: 429 us -> 168 us (0.39)
  waiting for transfers between devices: 322 us -> 28.4 us
  Pallas kernels: 0 us -> 58.8 us
  starting transfers between devices: 7.93 us -> 61.8 us
  local copies, waits for them, and re-layouts: 51.3 us -> 9.52 us
  matrix products: 33.8 us -> 1.18 us
  between operations: 13.4 us -> 0.29 us
  other arithmetic: 0.02 us -> 7.18 us
    psum x1 -> x0, waiting for transfers between devices: 205 us -> none  [body(): lax.psum(jnp.einsum('pb,kb->pk', aux_factors, flat, preferred_element_typ...]
    all_to_all x1, waiting for transfers between devices: 117 us -> 0.01 us  [body(): lax.all_to_all(crossing, ('c', 'y'), split_axis=0, concat_axis=0, tiled=T...]
    pallas_call x0 -> x7, Pallas kernels: none -> 58.8 us  [the longest x6 53.9 us: call(): pl.pallas_call(kernel, grid_spec=pltpu.PrefetchScalarGridSpec(num_scalar_...]
    ppermute x0 -> x29, starting transfers between devices: none -> 53.3 us  [the longest x15 31.9 us: send(): return lax.ppermute(v, ('z', 'xl', 'xh'), pairs)]
    dot_general x3 -> x2, matrix products: 33.8 us -> 1.18 us  [the longest x1 1.05 us: body(): weights = jnp.dot(freq_basis, picked, precision=exact)]
    ppermute x0 -> x29, waiting for transfers between devices: none -> 28.3 us  [the longest x11 19.6 us: shift(): return lax.ppermute(v, axis, [(i, (i + by) % n) for i in range(n)])]
    dot_general x1 -> x0, local copies, waits for them, and re-layouts: 14.6 us -> none  [body(): jnp.einsum('lt,tmb->lmb', fit_matrix, lax.all_to_all(green_tau, 'tau', sp...]
    all_to_all x1 -> x0, local copies, waits for them, and re-layouts: 11.9 us -> none  [body(): lax.all_to_all(green_tau, 'tau', split_axis=1, concat_axis=0, tiled=True)]
  transfers between devices with their start and end apart: 2 -> 30, of which waited for: 2 -> 6; matrix products, arithmetic and copies ran while one was open for 0% -> 6% of each run, Pallas kernels for 0% -> 32%
where the time goes in v1:
time: 168 us; the launch traced here: 167 us
  starting transfers between devices  61.8 us (37%)
  Pallas kernels  58.8 us (35%)
  waiting for transfers between devices  28.4 us (17%)
  local copies, waits for them, and re-layouts  9.52 us (6%)
  other arithmetic  7.18 us (4%)
    pallas_call x6, Pallas kernels, call(): pl.pallas_call(kernel, grid_spec=pltpu.PrefetchScalarGridSpec(num_scalar_...  53.9 us
    ppermute x15, starting transfers between devices, send(): return lax.ppermute(v, ('z', 'xl', 'xh'), pairs)  31.9 us
    ppermute x11, waiting for transfers between devices, shift(): return lax.ppermute(v, axis, [(i, (i + by) % n) for i in range(n)])  19.6 us
    ppermute x11, starting transfers between devices, shift(): return lax.ppermute(v, axis, [(i, (i + by) % n) for i in range(n)])  15 us
    all_to_all x1, starting transfers between devices, body(): lax.all_to_all(crossing, ('c', 'y'), split_axis=0, concat_axis=0, tiled=T...  8.43 us
    unnamed x42, local copies, waits for them, and re-layouts  7.19 us
    ppermute x15, waiting for transfers between devices, send(): return lax.ppermute(v, ('z', 'xl', 'xh'), pairs)  7.13 us
    ppermute x3, starting transfers between devices, flip(): return lax.ppermute(v, axis, [(0, 1), (1, 0)])  6.46 us
  transfers between devices with their start and end apart: 30, of which 6 were waited for; matrix products, arithmetic and copies ran while one was open for 6% of the time, Pallas kernels for 32%

profile of v1, /device:TPU:1, one launch (start us, length us, event | category | flops | bytes accessed | tf_op | source)
XLA Modules:
  0.0 167.1 jit_solution(10451554265553612811)
XLA Ops:
  6.5 3.7 %collective-permute-start.7 = (s32[4,16,20]{2,1,0:T(8,128)S(1)}, s32[4,16,20]{2,1,0:T(8,128)S(1)}, u32[]{:S(2)}, u32[]{:S(2)}) collective-permute-start(s32[4,16,20]{2,1,0:T(8,128)S(1)} %pad_add_fusion.1.mask_ref), channel_id=1, source_target_pairs={{0,64},{32,96},{64,0},{96,32},{1,65},{33,97},{65,1},{97,33},{2,66}... | collective-permute-start | bytes 15368 | tf_op jit(solution)/shard_map/ppermute | solution.py:133
  10.9 1.9 %collective-permute-start.5 = (s32[4,16,20]{2,1,0:T(8,128)S(1)}, s32[4,16,20]{2,1,0:T(8,128)S(1)}, u32[]{:S(2)}, u32[]{:S(2)}) collective-permute-start(s32[4,16,20]{2,1,0:T(8,128)S(1)} %pad_add_fusion.1.mask_ref), channel_id=1, source_target_pairs={{0,96},{32,0},{64,32},{96,64},{1,97},{33,1},{65,33},{97,65},{2,98}... | collective-permute-start | bytes 15368 | tf_op jit(solution)/shard_map/ppermute | solution.py:133
  12.8 11.5 %shard_map.64 = (bf16[2,4,128,256]{3,2,1,0:T(8,128)(2,1)}, bf16[2,4,128,256]{3,2,1,0:T(8,128)(2,1)}, bf16[2,4,128,256]{3,2,1,0:T(8,128)(2,1)}, f32[2,4,128,256]{3,2,1,0:T(8,128)}) custom-call(s32[19]{0:T(128)} %stack.135.at, s32[4,16,20]{2,1,0:T(8,128)} %copy-done.12, bf16[8,16,16,2560]{3,2,1,0:T(8,128)(2,1)} %bitcast.73, ...), custom_call_target="tpu_custom_call" | custom-call | flops 5368709120 | bytes 13107200 | tf_op jit(solution)/shard_map/pallas_call | solution.py:168
  25.0 5.6 %shard_map.65 = (bf16[512,256]{1,0:T(8,128)(2,1)}, bf16[512,256]{1,0:T(8,128)(2,1)}) custom-call(s32[19]{0:T(128)} %stack.135.at, s32[4,16,20]{2,1,0:T(8,128)} %copy-done.7, bf16[8,16,16,2560]{3,2,1,0:T(8,128)(2,1)} %bitcast.77, bf16[8,16,16,2560]{3,2,1,0:T(8,128)(2,1)} %bitcast.78, bf16[8,16,16,2560]{3,2,1,0:T(8,128)(2,1)} %bitcast.79, ...), custom_call_target="tpu_custom_call" | custom-call | flops 1342177280 | bytes 5242880 | tf_op jit(solution)/shard_map/pallas_call | solution.py:168
  33.9 7.5 %shard_map.66 = (bf16[1024,256]{1,0:T(8,128)(2,1)}, bf16[1024,256]{1,0:T(8,128)(2,1)}) custom-call(s32[19]{0:T(128)} %stack.135.at, s32[8,16,20]{2,1,0:T(8,128)} %copy-done.6, bf16[8,16,16,2560]{3,2,1,0:T(8,128)(2,1)} %bitcast.84, bf16[8,16,16,2560]{3,2,1,0:T(8,128)(2,1)} %bitcast.82, bf16[8,16,16,2560]{3,2,1,0:T(8,128)(2,1)} %bitcast.83, ...), custom_call_target="tpu_custom_call" | custom-call | flops 2684354560 | bytes 7864320 | tf_op jit(solution)/shard_map/pallas_call | solution.py:168
  41.5 2.7 %collective-permute-start.8 = (bf16[1024,256]{1,0:T(8,128)(2,1)}, bf16[1024,256]{1,0:T(8,128)(2,1)S(1)}, u32[]{:S(2)}, u32[]{:S(2)}) collective-permute-start(bf16[1024,256]{1,0:T(8,128)(2,1)} %get-tuple-element.23.after), channel_id=1, source_target_pairs={{0,3},{1,0},{2,1},{3,2},{4,7},{5,4},{6,5},{7,6},{8,11},{9,8},{10,9... | collective-permute-start | bytes 1572872 | tf_op jit(solution)/shard_map/ppermute | solution.py:133
  44.1 2.7 %collective-permute-start.2 = (bf16[2,4,128,256]{3,2,1,0:T(8,128)(2,1)S(1)}, bf16[2,4,128,256]{3,2,1,0:T(8,128)(2,1)S(1)}, u32[]{:S(2)}, u32[]{:S(2)}) collective-permute-start(bf16[2,4,128,256]{3,2,1,0:T(8,128)(2,1)S(1)} %copy-done.16), channel_id=1, source_target_pairs={{0,4},{4,0},{16,20},{20,16},{32,36},{36,32},{48,52},{52,48},{64,68... | collective-permute-start | bytes 1572872 | tf_op jit(solution)/shard_map/ppermute | solution.py:143
  49.2 7.6 %shard_map.67 = (bf16[1,2,512,256]{3,2,1,0:T(8,128)(2,1)}, bf16[1,2,512,256]{3,2,1,0:T(8,128)(2,1)}) custom-call(s32[19]{0:T(128)} %stack.135.at, s32[4,16,20]{2,1,0:T(8,128)} %copy-done.7, bf16[8,16,16,2560]{3,2,1,0:T(8,128)(2,1)} %bitcast.85, bf16[8,16,16,2560]{3,2,1,0:T(8,128)(2,1)} %bitcast.86, bf16[8,16,16,2560]{3,2,1,0:T(8,128)(2,1)} %bitcast.87, ...), custom_call_target="tpu_custom_call" | custom-call | flops 2684354560 | bytes 7864320 | tf_op jit(solution)/shard_map/pallas_call | solution.py:168
  58.4 12.1 %shard_map.68 = (bf16[2,2,512,256]{3,2,1,0:T(8,128)(2,1)}, bf16[2,2,512,256]{3,2,1,0:T(8,128)(2,1)}) custom-call(s32[19]{0:T(128)} %stack.135.at, s32[8,16,20]{2,1,0:T(8,128)} %copy-done.6, bf16[8,16,16,2560]{3,2,1,0:T(8,128)(2,1)} %bitcast.89, bf16[8,16,16,2560]{3,2,1,0:T(8,128)(2,1)} %bitcast.90, bf16[8,16,16,2560]{3,2,1,0:T(8,128)(2,1)} %bitcast.91, ...), custom_call_target="tpu_custom_call" | custom-call | flops 5368709120 | bytes 13107200 | tf_op jit(solution)/shard_map/pallas_call | solution.py:168
  71.5 1.7 %collective-permute-start.12 = (bf16[2,2,512,256]{3,2,1,0:T(8,128)(2,1)}, bf16[2,2,512,256]{3,2,1,0:T(8,128)(2,1)S(1)}, u32[]{:S(2)}, u32[]{:S(2)}) collective-permute-start(bf16[2,2,512,256]{3,2,1,0:T(8,128)(2,1)} %get-tuple-element.27.after), channel_id=1, source_target_pairs={{0,3},{1,0},{2,1},{3,2},{4,7},{5,4},{6,5},{7,6},{8,11},{9,8},{10,9... | collective-permute-start | bytes 3145736 | tf_op jit(solution)/shard_map/ppermute | solution.py:133
  74.7 9.5 %shard_map.69 = f32[3,2,512,256]{3,2,1,0:T(8,128)} custom-call(s32[19]{0:T(128)} %stack.135.at, s32[12,16,20]{2,1,0:T(8,128)} %pad_add_fusion.mask_ref, bf16[8,16,16,2560]{3,2,1,0:T(8,128)(2,1)} %bitcast.93, bf16[8,16,16,2560]{3,2,1,0:T(8,128)(2,1)} %bitcast.94, bf16[8,16,16,2560]{3,2,1,0:T(8,128)(2,1)} %bitcast.95, bf16[8,16,16,2560]{3,2,1,0:T(8,128)(2,1)} %bitcast.96, ...), custom_call_target="tpu_custom_call" | custom-call | flops 4026531840 | bytes 10485760 | tf_op jit(solution)/shard_map/pallas_call | solution.py:168
  84.2 19.6 %collective-permute-done.14 = bf16[1,2,512,256]{3,2,1,0:T(8,128)(2,1)S(1)} collective-permute-done((bf16[1,2,512,256]{3,2,1,0:T(8,128)(2,1)S(1)}, bf16[1,2,512,256]{3,2,1,0:T(8,128)(2,1)S(1)}, u32[]{:S(2)}, u32[]{:S(2)}) %collective-permute-start.14) | collective-permute-done | bytes 524320 | tf_op jit(solution)/shard_map/ppermute | solution.py:133
  103.8 2.3 %slice_add_fusion = (f32[1,2,512,256]{3,2,1,0:T(8,128)S(1)}, f32[1,2,512,256]{3,2,1,0:T(8,128)S(1)}, f32[1,2,512,256]{3,2,1,0:T(8,128)S(1)}) fusion(f32[3,2,512,256]{3,2,1,0:T(8,128)} %shard_map.69, bf16[2,2,512,256]{3,2,1,0:T(8,128)(2,1)S(1)} %collective-permute-done.19, bf16[2,2,512,256]{3,2,1,0:T(8,128)(2,1)S(1)} %collective-permute-done.12, ...), kind=kLoop, calls=%fused_computation.2 | loop fusion | flops 3145728 | bytes 9437184 | tf_op jit(solution)/shard_map/add | solution.py:245
  107.0 8.4 %all-to-all-start = ((bf16[8,2,128,256]{3,2,1,0:T(8,128)(2,1)}), bf16[8,2,128,256]{3,2,1,0:T(8,128)(2,1)S(1)}, u32[]{:S(2)}, u32[]{:S(2)}) async-start(bf16[8,2,128,256]{3,2,1,0:T(8,128)(2,1)} %pad_maximum_fusion), calls=%async_computation | async-start | bytes 2097152 | tf_op jit(solution)/shard_map/all_to_all | solution.py:253
  118.9 2.0 %collective-permute-start.26 = (bf16[256,256]{1,0:T(8,128)(2,1)S(1)}, bf16[256,256]{1,0:T(8,128)(2,1)S(1)}, u32[]{:S(2)}, u32[]{:S(2)}) collective-permute-start(bf16[256,256]{1,0:T(8,128)(2,1)S(1)} %get-tuple-element.34), channel_id=1, source_target_pairs={{0,112},{4,116},{16,96},{20,100},{32,16},{36,20},{48,0},{52,4},{64... | collective-permute-start | bytes 393224 | tf_op jit(solution)/shard_map/ppermute | solution.py:143
  120.8 3.0 %collective-permute-start.27 = (bf16[256,256]{1,0:T(8,128)(2,1)S(1)}, bf16[256,256]{1,0:T(8,128)(2,1)S(1)}, u32[]{:S(2)}, u32[]{:S(2)}) collective-permute-start(bf16[256,256]{1,0:T(8,128)(2,1)S(1)} %get-tuple-element.35), channel_id=1, source_target_pairs={{0,116},{4,112},{16,100},{20,96},{32,20},{36,16},{48,4},{52,0},{64... | collective-permute-start | bytes 393224 | tf_op jit(solution)/shard_map/ppermute | solution.py:143
  124.0 2.3 %collective-permute-start.25 = (bf16[256,256]{1,0:T(8,128)(2,1)S(1)}, bf16[256,256]{1,0:T(8,128)(2,1)S(1)}, u32[]{:S(2)}, u32[]{:S(2)}) collective-permute-start(bf16[256,256]{1,0:T(8,128)(2,1)S(1)} %get-tuple-element.36), channel_id=1, source_target_pairs={{0,100},{4,96},{16,116},{20,112},{32,4},{36,0},{48,20},{52,16},{64... | collective-permute-start | bytes 393224 | tf_op jit(solution)/shard_map/ppermute | solution.py:143
  127.8 4.1 %collective-permute-start.18 = (bf16[256,256]{1,0:T(8,128)(2,1)S(1)}, bf16[256,256]{1,0:T(8,128)(2,1)S(1)}, u32[]{:S(2)}, u32[]{:S(2)}) collective-permute-start(bf16[256,256]{1,0:T(8,128)(2,1)S(1)} %get-tuple-element.41), channel_id=1, source_target_pairs={{0,84},{4,80},{16,68},{20,64},{32,116},{36,112},{48,100},{52,96},{... | collective-permute-start | bytes 393224 | tf_op jit(solution)/shard_map/ppermute | solution.py:143
  132.0 4.6 %collective-permute-start.15 = (f32[256,256]{1,0:T(8,128)S(1)}, f32[256,256]{1,0:T(8,128)S(1)}, u32[]{:S(2)}, u32[]{:S(2)}) collective-permute-start(f32[256,256]{1,0:T(8,128)S(1)} %slice_bitcast_fusion.2), channel_id=1, source_target_pairs={{0,64},{4,68},{16,80},{20,84},{32,96},{36,100},{48,112},{52,116},{... | collective-permute-start | bytes 786440 | tf_op jit(solution)/shard_map/ppermute | solution.py:143
  136.6 1.7 %collective-permute-start.16 = (bf16[256,256]{1,0:T(8,128)(2,1)S(1)}, bf16[256,256]{1,0:T(8,128)(2,1)S(1)}, u32[]{:S(2)}, u32[]{:S(2)}) collective-permute-start(bf16[256,256]{1,0:T(8,128)(2,1)S(1)} %get-tuple-element.42), channel_id=1, source_target_pairs={{0,68},{4,64},{16,84},{20,80},{32,100},{36,96},{48,116},{52,112},{... | collective-permute-start | bytes 393224 | tf_op jit(solution)/shard_map/ppermute | solution.py:143
  138.4 6.2 %collective-permute-start.24 = (f32[256,256]{1,0:T(8,128)S(1)}, f32[256,256]{1,0:T(8,128)S(1)}, u32[]{:S(2)}, u32[]{:S(2)}) collective-permute-start(f32[256,256]{1,0:T(8,128)S(1)} %slice_bitcast_fusion), channel_id=1, source_target_pairs={{0,96},{4,100},{16,112},{20,116},{32,0},{36,4},{48,16},{52,20},{64... | collective-permute-start | bytes 786440 | tf_op jit(solution)/shard_map/ppermute | solution.py:143
  146.4 4.8 %collective-permute-done.20 = f32[256,256]{1,0:T(8,128)S(1)} collective-permute-done((f32[256,256]{1,0:T(8,128)S(1)}, f32[256,256]{1,0:T(8,128)S(1)}, u32[]{:S(2)}, u32[]{:S(2)}) %collective-permute-start.20) | collective-permute-done | bytes 262176 | tf_op jit(solution)/shard_map/ppermute | solution.py:143
  155.2 3.7 %collective-permute-start.28 = (f32[768,256]{1,0:T(8,128)}, f32[768,256]{1,0:T(8,128)S(1)}, u32[]{:S(2)}, u32[]{:S(2)}) collective-permute-start(f32[768,256]{1,0:T(8,128)} %get-tuple-element.43), channel_id=1, source_target_pairs={{0,8},{8,0},{1,9},{9,1},{2,10},{10,2},{3,11},{11,3},{4,12},{12,4},... | collective-permute-start | bytes 2359304 | tf_op jit(solution)/shard_map/ppermute | solution.py:136
  162.1 5.0 %shard_map.70 = f32[3840,256]{1,0:T(8,128)} custom-call(f32[240,128]{1,0:T(8,128)} %convolution_bitcast_fusion.w_ref, f32[120,256]{1,0:T(8,128)} %s_ref.1, f32[512,256]{1,0:T(8,128)} %bitcast.114, f32[768,256]{1,0:T(8,128)} %copy-done.2, f32[768,256]{1,0:T(8,128)} %copy-done.3), custom_call_target="tpu_custom_call" | custom-call | tf_op jit(solution)/shard_map/pallas_call | solution.py:268
  (117 shorter events, 32.3 us)
Async XLA Ops:
  6.5 17.9 %collective-permute-start.7 = (s32[4,16,20]{2,1,0:T(8,128)S(1)}, s32[4,16,20]{2,1,0:T(8,128)S(1)}, u32[]{:S(2)}, u32[]{:S(2)}) collective-permute-start(s32[4,16,20]{2,1,0:T(8,128)S(1)} %pad_add_fusion.1.mask_ref), channel_id=1, source_target_pairs={{0,64},{32,96},{64,0},{96,32},{1,65},{33,97},{65,1},{97,33},{2,66}... | collective-permute-start | bytes 15368 | tf_op jit(solution)/shard_map/ppermute | solution.py:133
  10.1 23.2 %collective-permute-start.6 = (s32[4,16,20]{2,1,0:T(8,128)S(1)}, s32[4,16,20]{2,1,0:T(8,128)S(1)}, u32[]{:S(2)}, u32[]{:S(2)}) collective-permute-start(s32[4,16,20]{2,1,0:T(8,128)S(1)} %pad_add_fusion.1.mask_ref), channel_id=1, source_target_pairs={{0,32},{32,64},{64,96},{96,0},{1,33},{33,65},{65,97},{97,1},{2,34}... | collective-permute-start | bytes 15368 | tf_op jit(solution)/shard_map/ppermute | solution.py:133
  10.9 22.4 %collective-permute-start.5 = (s32[4,16,20]{2,1,0:T(8,128)S(1)}, s32[4,16,20]{2,1,0:T(8,128)S(1)}, u32[]{:S(2)}, u32[]{:S(2)}) collective-permute-start(s32[4,16,20]{2,1,0:T(8,128)S(1)} %pad_add_fusion.1.mask_ref), channel_id=1, source_target_pairs={{0,96},{32,0},{64,32},{96,64},{1,97},{33,1},{65,33},{97,65},{2,98}... | collective-permute-start | bytes 15368 | tf_op jit(solution)/shard_map/ppermute | solution.py:133
  30.6 17.0 %collective-permute-start.11 = (bf16[512,256]{1,0:T(8,128)(2,1)}, bf16[512,256]{1,0:T(8,128)(2,1)S(1)}, u32[]{:S(2)}, u32[]{:S(2)}) collective-permute-start(bf16[512,256]{1,0:T(8,128)(2,1)} %get-tuple-element.25), channel_id=1, source_target_pairs={{0,1},{1,2},{2,3},{3,0},{4,5},{5,6},{6,7},{7,4},{8,9},{9,10},{10,1... | collective-permute-start | bytes 786440 | tf_op jit(solution)/shard_map/ppermute | solution.py:133
  31.8 16.6 %collective-permute-start.10 = (bf16[512,256]{1,0:T(8,128)(2,1)}, bf16[512,256]{1,0:T(8,128)(2,1)S(1)}, u32[]{:S(2)}, u32[]{:S(2)}) collective-permute-start(bf16[512,256]{1,0:T(8,128)(2,1)} %get-tuple-element.22.after), channel_id=1, source_target_pairs={{0,3},{1,0},{2,1},{3,2},{4,7},{5,4},{6,5},{7,6},{8,11},{9,8},{10,9... | collective-permute-start | bytes 786440 | tf_op jit(solution)/shard_map/ppermute | solution.py:133
  41.4 15.3 %collective-permute-start.9 = (bf16[1024,256]{1,0:T(8,128)(2,1)}, bf16[1024,256]{1,0:T(8,128)(2,1)S(1)}, u32[]{:S(2)}, u32[]{:S(2)}) collective-permute-start(bf16[1024,256]{1,0:T(8,128)(2,1)} %get-tuple-element.24), channel_id=1, source_target_pairs={{0,1},{1,2},{2,3},{3,0},{4,5},{5,6},{6,7},{7,4},{8,9},{9,10},{10,1... | collective-permute-start | bytes 1572872 | tf_op jit(solution)/shard_map/ppermute | solution.py:133
  41.5 15.8 %collective-permute-start.8 = (bf16[1024,256]{1,0:T(8,128)(2,1)}, bf16[1024,256]{1,0:T(8,128)(2,1)S(1)}, u32[]{:S(2)}, u32[]{:S(2)}) collective-permute-start(bf16[1024,256]{1,0:T(8,128)(2,1)} %get-tuple-element.23.after), channel_id=1, source_target_pairs={{0,3},{1,0},{2,1},{3,2},{4,7},{5,4},{6,5},{7,6},{8,11},{9,8},{10,9... | collective-permute-start | bytes 1572872 | tf_op jit(solution)/shard_map/ppermute | solution.py:133
  44.1 27.3 %collective-permute-start.2 = (bf16[2,4,128,256]{3,2,1,0:T(8,128)(2,1)S(1)}, bf16[2,4,128,256]{3,2,1,0:T(8,128)(2,1)S(1)}, u32[]{:S(2)}, u32[]{:S(2)}) collective-permute-start(bf16[2,4,128,256]{3,2,1,0:T(8,128)(2,1)S(1)} %copy-done.16), channel_id=1, source_target_pairs={{0,4},{4,0},{16,20},{20,16},{32,36},{36,32},{48,52},{52,48},{64,68... | collective-permute-start | bytes 1572872 | tf_op jit(solution)/shard_map/ppermute | solution.py:143
  47.5 25.9 %collective-permute-start.3 = (bf16[2,4,128,256]{3,2,1,0:T(8,128)(2,1)S(1)}, bf16[2,4,128,256]{3,2,1,0:T(8,128)(2,1)S(1)}, u32[]{:S(2)}, u32[]{:S(2)}) collective-permute-start(bf16[2,4,128,256]{3,2,1,0:T(8,128)(2,1)S(1)} %copy-done.15), channel_id=1, source_target_pairs={{0,20},{4,16},{16,4},{20,0},{32,52},{36,48},{48,36},{52,32},{64,84... | collective-permute-start | bytes 1572872 | tf_op jit(solution)/shard_map/ppermute | solution.py:143
  48.5 25.0 %collective-permute-start.4 = (bf16[2,4,128,256]{3,2,1,0:T(8,128)(2,1)S(1)}, bf16[2,4,128,256]{3,2,1,0:T(8,128)(2,1)S(1)}, u32[]{:S(2)}, u32[]{:S(2)}) collective-permute-start(bf16[2,4,128,256]{3,2,1,0:T(8,128)(2,1)S(1)} %copy-done.14), channel_id=1, source_target_pairs={{0,16},{4,20},{16,0},{20,4},{32,48},{36,52},{48,32},{52,36},{64,80... | collective-permute-start | bytes 1572872 | tf_op jit(solution)/shard_map/ppermute | solution.py:143
  56.8 47.0 %collective-permute-start.13 = (bf16[1,2,512,256]{3,2,1,0:T(8,128)(2,1)}, bf16[1,2,512,256]{3,2,1,0:T(8,128)(2,1)S(1)}, u32[]{:S(2)}, u32[]{:S(2)}) collective-permute-start(bf16[1,2,512,256]{3,2,1,0:T(8,128)(2,1)} %get-tuple-element.26.after), channel_id=1, source_target_pairs={{0,3},{1,0},{2,1},{3,2},{4,7},{5,4},{6,5},{7,6},{8,11},{9,8},{10,9... | collective-permute-start | bytes 1572872 | tf_op jit(solution)/shard_map/ppermute | solution.py:133
  70.5 33.3 %collective-permute-start.19 = (bf16[2,2,512,256]{3,2,1,0:T(8,128)(2,1)}, bf16[2,2,512,256]{3,2,1,0:T(8,128)(2,1)S(1)}, u32[]{:S(2)}, u32[]{:S(2)}) collective-permute-start(bf16[2,2,512,256]{3,2,1,0:T(8,128)(2,1)} %get-tuple-element.30), channel_id=1, source_target_pairs={{0,1},{1,2},{2,3},{3,0},{4,5},{5,6},{6,7},{7,4},{8,9},{9,10},{10,1... | collective-permute-start | bytes 3145736 | tf_op jit(solution)/shard_map/ppermute | solution.py:133
  71.5 32.4 %collective-permute-start.12 = (bf16[2,2,512,256]{3,2,1,0:T(8,128)(2,1)}, bf16[2,2,512,256]{3,2,1,0:T(8,128)(2,1)S(1)}, u32[]{:S(2)}, u32[]{:S(2)}) collective-permute-start(bf16[2,2,512,256]{3,2,1,0:T(8,128)(2,1)} %get-tuple-element.27.after), channel_id=1, source_target_pairs={{0,3},{1,0},{2,1},{3,2},{4,7},{5,4},{6,5},{7,6},{8,11},{9,8},{10,9... | collective-permute-start | bytes 3145736 | tf_op jit(solution)/shard_map/ppermute | solution.py:133
  73.4 30.4 %collective-permute-start.14 = (bf16[1,2,512,256]{3,2,1,0:T(8,128)(2,1)S(1)}, bf16[1,2,512,256]{3,2,1,0:T(8,128)(2,1)S(1)}, u32[]{:S(2)}, u32[]{:S(2)}) collective-permute-start(bf16[1,2,512,256]{3,2,1,0:T(8,128)(2,1)S(1)} %copy-done.17), channel_id=1, source_target_pairs={{0,1},{1,2},{2,3},{3,0},{4,5},{5,6},{6,7},{7,4},{8,9},{9,10},{10,1... | collective-permute-start | bytes 1572872 | tf_op jit(solution)/shard_map/ppermute | solution.py:133
  107.0 53.3 %all-to-all-start = ((bf16[8,2,128,256]{3,2,1,0:T(8,128)(2,1)}), bf16[8,2,128,256]{3,2,1,0:T(8,128)(2,1)S(1)}, u32[]{:S(2)}, u32[]{:S(2)}) async-start(bf16[8,2,128,256]{3,2,1,0:T(8,128)(2,1)} %pad_maximum_fusion), calls=%async_computation | async-start | bytes 2097152 | tf_op jit(solution)/shard_map/all_to_all | solution.py:253
  115.6 10.7 %collective-permute-start.23 = (bf16[256,256]{1,0:T(8,128)(2,1)S(1)}, bf16[256,256]{1,0:T(8,128)(2,1)S(1)}, u32[]{:S(2)}, u32[]{:S(2)}) collective-permute-start(bf16[256,256]{1,0:T(8,128)(2,1)S(1)} %get-tuple-element.38), channel_id=1, source_target_pairs={{0,52},{4,48},{16,36},{20,32},{32,84},{36,80},{48,68},{52,64},{64,... | collective-permute-start | bytes 393224 | tf_op jit(solution)/shard_map/ppermute | solution.py:143
  117.2 29.2 %collective-permute-start.21 = (bf16[256,256]{1,0:T(8,128)(2,1)S(1)}, bf16[256,256]{1,0:T(8,128)(2,1)S(1)}, u32[]{:S(2)}, u32[]{:S(2)}) collective-permute-start(bf16[256,256]{1,0:T(8,128)(2,1)S(1)} %get-tuple-element.39), channel_id=1, source_target_pairs={{0,36},{4,32},{16,52},{20,48},{32,68},{36,64},{48,84},{52,80},{64,... | collective-permute-start | bytes 393224 | tf_op jit(solution)/shard_map/ppermute | solution.py:143
  118.9 8.9 %collective-permute-start.26 = (bf16[256,256]{1,0:T(8,128)(2,1)S(1)}, bf16[256,256]{1,0:T(8,128)(2,1)S(1)}, u32[]{:S(2)}, u32[]{:S(2)}) collective-permute-start(bf16[256,256]{1,0:T(8,128)(2,1)S(1)} %get-tuple-element.34), channel_id=1, source_target_pairs={{0,112},{4,116},{16,96},{20,100},{32,16},{36,20},{48,0},{52,4},{64... | collective-permute-start | bytes 393224 | tf_op jit(solution)/shard_map/ppermute | solution.py:143
  120.8 11.1 %collective-permute-start.27 = (bf16[256,256]{1,0:T(8,128)(2,1)S(1)}, bf16[256,256]{1,0:T(8,128)(2,1)S(1)}, u32[]{:S(2)}, u32[]{:S(2)}) collective-permute-start(bf16[256,256]{1,0:T(8,128)(2,1)S(1)} %get-tuple-element.35), channel_id=1, source_target_pairs={{0,116},{4,112},{16,100},{20,96},{32,20},{36,16},{48,4},{52,0},{64... | collective-permute-start | bytes 393224 | tf_op jit(solution)/shard_map/ppermute | solution.py:143
  124.0 28.6 %collective-permute-start.25 = (bf16[256,256]{1,0:T(8,128)(2,1)S(1)}, bf16[256,256]{1,0:T(8,128)(2,1)S(1)}, u32[]{:S(2)}, u32[]{:S(2)}) collective-permute-start(bf16[256,256]{1,0:T(8,128)(2,1)S(1)} %get-tuple-element.36), channel_id=1, source_target_pairs={{0,100},{4,96},{16,116},{20,112},{32,4},{36,0},{48,20},{52,16},{64... | collective-permute-start | bytes 393224 | tf_op jit(solution)/shard_map/ppermute | solution.py:143
  126.3 10.3 %collective-permute-start.17 = (bf16[256,256]{1,0:T(8,128)(2,1)S(1)}, bf16[256,256]{1,0:T(8,128)(2,1)S(1)}, u32[]{:S(2)}, u32[]{:S(2)}) collective-permute-start(bf16[256,256]{1,0:T(8,128)(2,1)S(1)} %get-tuple-element.40), channel_id=1, source_target_pairs={{0,80},{4,84},{16,64},{20,68},{32,112},{36,116},{48,96},{52,100},{... | collective-permute-start | bytes 393224 | tf_op jit(solution)/shard_map/ppermute | solution.py:143
  127.8 10.6 %collective-permute-start.18 = (bf16[256,256]{1,0:T(8,128)(2,1)S(1)}, bf16[256,256]{1,0:T(8,128)(2,1)S(1)}, u32[]{:S(2)}, u32[]{:S(2)}) collective-permute-start(bf16[256,256]{1,0:T(8,128)(2,1)S(1)} %get-tuple-element.41), channel_id=1, source_target_pairs={{0,84},{4,80},{16,68},{20,64},{32,116},{36,112},{48,100},{52,96},{... | collective-permute-start | bytes 393224 | tf_op jit(solution)/shard_map/ppermute | solution.py:143
  132.0 13.0 %collective-permute-start.15 = (f32[256,256]{1,0:T(8,128)S(1)}, f32[256,256]{1,0:T(8,128)S(1)}, u32[]{:S(2)}, u32[]{:S(2)}) collective-permute-start(f32[256,256]{1,0:T(8,128)S(1)} %slice_bitcast_fusion.2), channel_id=1, source_target_pairs={{0,64},{4,68},{16,80},{20,84},{32,96},{36,100},{48,112},{52,116},{... | collective-permute-start | bytes 786440 | tf_op jit(solution)/shard_map/ppermute | solution.py:143
  138.4 15.4 %collective-permute-start.24 = (f32[256,256]{1,0:T(8,128)S(1)}, f32[256,256]{1,0:T(8,128)S(1)}, u32[]{:S(2)}, u32[]{:S(2)}) collective-permute-start(f32[256,256]{1,0:T(8,128)S(1)} %slice_bitcast_fusion), channel_id=1, source_target_pairs={{0,96},{4,100},{16,112},{20,116},{32,0},{36,4},{48,16},{52,20},{64... | collective-permute-start | bytes 786440 | tf_op jit(solution)/shard_map/ppermute | solution.py:143
  (24 other events, 360.0 us)

commit v2 on v0

v2 whole, which is shorter than its diff:
```python
import functools

import jax
import jax.numpy as jnp
import numpy as np
from jax import lax
from jax.experimental import pallas as pl
from jax.experimental.pallas import tpu as pltpu
from jax.sharding import Mesh, PartitionSpec as P

BLOCK = 128
LANES = 128
ANY = pl.BlockSpec(memory_space=pl.ANY)
WHOLE = pl.BlockSpec(memory_space=pltpu.VMEM)
SMALL = pltpu.CompilerParams(vmem_limit_bytes=14 * 2**20)
COST = pl.CostEstimate(flops=4 * 10**9, bytes_accessed=2 * 10**7, transcendentals=0)
LITTLE = pl.CostEstimate(flops=10**6, bytes_accessed=10**5, transcendentals=0)
LONG = pl.CostEstimate(flops=10**11, bytes_accessed=10**6, transcendentals=0)


def stage_kernel(source, after, held, sem):
    copy = pltpu.make_async_copy(source, held, sem)
    copy.start()
    copy.wait()


def join_kernel(a, b, c, d, out):
    for i, v in enumerate((a, b, c, d)):
        out[i] = v[...]


def fill(at, chunk, green_ref, mask_ref, rows_ref):
    times, _, height, cols = green_ref.shape
    base = lax.rem(at[2] + chunk, 4) * 4
    for i in range(4):
        marks = mask_ref[i ^ at[1]].astype(jnp.float32)
        for k in range(cols // BLOCK):
            keep = jnp.broadcast_to(marks[:, k : k + 1], (height, BLOCK)).astype(jnp.bfloat16)
            lanes = slice(k * BLOCK, (k + 1) * BLOCK)
            for t in range(times):
                row = (i * times + t) * height
                rows_ref[row : row + height, lanes] = green_ref[t, base + i, :, lanes] * keep


def product(rows_ref, a):
    return lax.dot_general(rows_ref[...], a, (((1,), (1,)), ((), ())), preferred_element_type=jnp.float32)


def put(out_ref, h, v):
    part = out_ref.shape[2]
    for i in range(4):
        out_ref[i, h] = v[i * part : (i + 1) * part].astype(out_ref.dtype)


def far_kernel(chunks, at, green_ref, aux_ref, after, *refs):
    mask_refs, (lo_ref, hi_ref, rows_ref) = refs[: len(chunks)], refs[len(chunks) :]
    target = lax.rem(at[0] + 2, aux_ref.shape[1])
    for q, chunk in enumerate(chunks):
        fill(at, chunk, green_ref, mask_refs[q], rows_ref)
        lo_ref[q] = product(rows_ref, aux_ref[0, target]).astype(jnp.bfloat16)
        hi_ref[q] = product(rows_ref, aux_ref[1, target]).astype(jnp.bfloat16)


def near_kernel(chunk, at, green_ref, aux_ref, after, mask_ref, from_up, from_down, *refs):
    down_ref, up_ref, rows_ref = refs[-3:]
    n = aux_ref.shape[1]
    fill(at, chunk, green_ref, mask_ref, rows_ref)
    below, above = lax.rem(at[0] + n - 1, n), lax.rem(at[0] + 1, n)
    put(down_ref, 0, product(rows_ref, aux_ref[0, below]) + from_up[0].astype(jnp.float32))
    put(down_ref, 1, product(rows_ref, aux_ref[1, below]))
    put(up_ref, 0, product(rows_ref, aux_ref[0, above]))
    put(up_ref, 1, product(rows_ref, aux_ref[1, above]) + from_down[0].astype(jnp.float32))


def own_kernel(at, green_ref, aux_ref, after, mask_refs, out_ref, rows_ref):
    chunk = pl.program_id(0)
    fill(at, chunk, green_ref, mask_refs, rows_ref)
    for h in range(2):
        put(out_ref.at[0], h, product(rows_ref, aux_ref[h, at[0]]))


def sum_kernel(own_ref, from_up, from_down, after, out_ref):
    for i in range(4):
        for h in range(2):
            others = from_up[i, h].astype(jnp.float32) + from_down[i, h].astype(jnp.float32)
            out_ref[i, h] = (own_ref[0, i, h] + others).astype(out_ref.dtype)


def gather_kernel(got_ref, after, out_ref):
    part = got_ref.shape[1]
    for i in range(got_ref.shape[0] // 2):
        both = got_ref[2 * i].astype(jnp.float32) + got_ref[2 * i + 1].astype(jnp.float32)
        out_ref[i * part : (i + 1) * part] = both


def final_kernel(w_ref, s_ref, *refs):
    x_refs, o_ref = refs[:-1], refs[-1]
    n_freq, _ = w_ref.shape
    height = o_ref.shape[0] // n_freq
    part = 8 * height
    w = w_ref[...]
    high = w.astype(jnp.bfloat16)
    low = (w - high.astype(jnp.float32)).astype(jnp.bfloat16)
    twice = jnp.concatenate([high, high], axis=1)
    scale = jnp.concatenate([s_ref[...], s_ref[...]], axis=0)

    def row(m):
        return jnp.concatenate(
            [ref[pl.ds(i * part + m, 8, stride=height), :] for ref in x_refs for i in range(ref.shape[0] // part)],
            axis=0,
        )

    for m in range(0, height, 2):
        x = jnp.concatenate([row(m), row(m + 1)], axis=1)
        x_high = x.astype(jnp.bfloat16)
        x_low = (x - x_high.astype(jnp.float32)).astype(jnp.bfloat16)
        mixed = jnp.dot(
            twice, jnp.concatenate([x_high, x_low], axis=0), preferred_element_type=jnp.float32
        ) + jnp.dot(low, x_high, preferred_element_type=jnp.float32)
        o_ref[pl.ds(m, n_freq, stride=height), :] = mixed[:, :LANES] * scale
        o_ref[pl.ds(m + 1, n_freq, stride=height), :] = mixed[:, LANES:] * scale


def body(green_tau, fit_matrix, aux_factors, freq_basis, screened, pair_mask):
    z, xl, c, y = (lax.axis_index(a) for a in ("z", "xl", "c", "y"))
    nz, ny = lax.axis_size("z"), lax.axis_size("y")
    times, n_rows, cols = green_tau.shape
    height, blocks = pair_mask.shape
    width = aux_factors.shape[0] // (2 * ny)
    part = times * height
    rows = 4 * part
    f32, bf16 = jnp.float32, jnp.bfloat16
    shape = jax.ShapeDtypeStruct

    def shift(v, axis, by):
        n = lax.axis_size(axis)
        return lax.ppermute(v, axis, [(i, (i + by) % n) for i in range(n)])

    exact = lax.Precision.HIGHEST
    order = jnp.stack([(z + nz - d) % nz for d in range(nz)])
    source = (order[:, None] * (4 * times) + jnp.arange(4 * times)[None, :]).reshape(1, -1)
    n_time = source.shape[1]
    pick = (jnp.arange(n_time)[:, None] == source).astype(f32)
    picked = jnp.dot(fit_matrix.astype(f32), pick, precision=exact)
    weights = jnp.dot(freq_basis, picked, precision=exact)
    at = jnp.stack([y, xl * 2 + c, z]).astype(jnp.int32)

    def stage(v, after):
        out = pl.pallas_call(
            stage_kernel,
            in_specs=[pl.BlockSpec(memory_space=pltpu.HBM), ANY],
            out_specs=WHOLE,
            out_shape=pltpu.VMEM(v.shape, v.dtype),
            scratch_shapes=[pltpu.SemaphoreType.DMA],
            compiler_params=SMALL,
            cost_estimate=COST,
        )(v, after)
        return pltpu.with_memory_space_constraint(out, pltpu.VMEM)

    def swap(v, e, f):
        pairs = [(i * 2 + j, (i ^ e) * 2 + (j ^ f)) for i in (0, 1) for j in (0, 1)]
        return lax.ppermute(v, ("xl", "c"), pairs)

    aux = stage(aux_factors.reshape(2, ny, width, cols), at)
    quad = pl.pallas_call(
        join_kernel,
        out_shape=shape((4, height, blocks), pair_mask.dtype),
        compiler_params=SMALL,
        cost_estimate=LITTLE,
    )(pair_mask, swap(pair_mask, 0, 1), swap(pair_mask, 1, 0), swap(pair_mask, 1, 1))
    marks = [quad if d == 0 else shift(quad, "z", -d) for d in range(nz)]
    green = stage(green_tau.reshape(times, n_rows // height, height, cols), quad)

    def call(kernel, after, extra, extra_specs, out_shape, cost=COST):
        fixed = lambda s: pl.BlockSpec(s.shape, lambda j, at: (0,) * len(s.shape))
        outs = out_shape if isinstance(out_shape, list) else [out_shape]
        got = pl.pallas_call(
            kernel,
            grid_spec=pltpu.PrefetchScalarGridSpec(
                num_scalar_prefetch=1,
                grid=(1,),
                in_specs=[WHOLE, WHOLE, ANY] + [s or fixed(v) for s, v in zip(extra_specs, extra, strict=True)],
                out_specs=[fixed(s) for s in outs],
                scratch_shapes=[pltpu.VMEM((rows, cols), bf16)],
            ),
            out_shape=outs,
            compiler_params=SMALL,
            cost_estimate=cost,
        )(at, green, aux, after, *extra)
        return got if isinstance(out_shape, list) else got[0]

    step1 = {}

    def far(chunks, after):
        out = shape((len(chunks), rows, width), bf16)
        lo, hi = call(
            functools.partial(far_kernel, chunks), after, [marks[d] for d in chunks], [None] * len(chunks), [out, out]
        )
        got = shift(lo, "y", -1), shift(hi, "y", 1)
        for q, d in enumerate(chunks):
            step1[d] = q, got
        return lo

    message = (4, 2, part, width)
    step2 = {}

    def near(d, after, arrived=(), cost=COST):
        q, got = step1[d]
        spec = pl.BlockSpec((1, rows, width), lambda j, at: (q, 0, 0))
        down, up = call(
            functools.partial(near_kernel, d), after, [marks[d], *got, *arrived],
            [None, spec, spec] + [ANY] * len(arrived),
            [shape(message, bf16), shape(message, bf16)], cost,
        )
        step2[d] = shift(down, "y", -1), shift(up, "y", 1)
        return down

    def own(after):
        joined = jnp.concatenate(marks)
        out = shape((nz, *message), f32)
        return pl.pallas_call(
            own_kernel,
            grid_spec=pltpu.PrefetchScalarGridSpec(
                num_scalar_prefetch=1,
                grid=(nz,),
                in_specs=[WHOLE, WHOLE, ANY, pl.BlockSpec((4, height, blocks), lambda j, at: (j, 0, 0))],
                out_specs=pl.BlockSpec((1, *message), lambda j, at: (j, 0, 0, 0, 0)),
                scratch_shapes=[pltpu.VMEM((rows, cols), bf16)],
            ),
            out_shape=out,
            compiler_params=SMALL,
            cost_estimate=COST,
        )(at, green, aux, after, joined)

    crossed = {}

    def cross(d, after, kind, cost=LITTLE):
        fixed = pl.BlockSpec(message, lambda j: (0, 0, 0, 0))
        total = pl.pallas_call(
            sum_kernel,
            grid=(1,),
            in_specs=[pl.BlockSpec((1, *message), lambda j: (d, 0, 0, 0, 0)), fixed, fixed, ANY],
            out_specs=fixed,
            out_shape=shape(message, kind),
            compiler_params=SMALL,
            cost_estimate=cost,
        )(mine, *step2[d], after)
        crossed[d] = lax.all_to_all(
            total.reshape(8, part, width), ("xl", "c", "xh"), split_axis=0, concat_axis=0, tiled=True
        )
        return total

    pieces = {}

    def gather(d, after):
        got = crossed[d]
        out = pl.pallas_call(
            gather_kernel,
            in_specs=[pl.BlockSpec(got.shape, lambda: (0, 0, 0)), ANY],
            out_shape=shape((rows, width), f32),
            compiler_params=SMALL,
            cost_estimate=LITTLE,
        )(got, after)
        pieces[d] = out if d == 0 else shift(out, "z", d)
        return out

    last = far((2, 0), quad)
    last = far((1, 3), last)
    last = near(2, last)
    last = mine = own(last)
    last = near(1, last)
    last = near(3, last, cost=LITTLE)
    last = near(0, last, step2[2], LITTLE)
    last = cross(2, last, f32)
    last = cross(1, last, bf16, LONG)
    last = gather(2, last)
    last = cross(3, last, bf16)
    last = gather(1, last)
    last = cross(0, last, bf16)
    last = gather(3, last)
    gather(0, last)

    n_freq = weights.shape[0]
    lane = lambda v: pl.BlockSpec((v.shape[0], LANES), lambda j: (0, j))
    held = [pieces[d] for d in range(nz)]
    sigma = pl.pallas_call(
        final_kernel,
        grid=(width // LANES,),
        in_specs=[pl.BlockSpec(weights.shape, lambda j: (0, 0))] + [lane(v) for v in (screened, *held)],
        out_specs=pl.BlockSpec((n_freq * height, LANES), lambda j: (0, j)),
        out_shape=shape((n_freq * height, width), f32),
        compiler_params=pltpu.CompilerParams(vmem_limit_bytes=28 * 2**20),
    )(weights, screened, *held)
    return sigma.reshape(n_freq, height, width)


def solution(mesh):
    devices = np.array(mesh.devices).reshape(4, 2, 2, 2, 4)
    fine = Mesh(devices, ("z", "xl", "c", "xh", "y"))
    tau, aux = ("z", "xl", "c"), ("xh", "y")
    return jax.shard_map(
        body,
        mesh=fine,
        in_specs=(P(tau, None, aux), P(), P(None, aux), P(), P(None, aux), P(tau, aux)),
        out_specs=P(None, tau, aux),
        check_vma=False,
    )
```

time: 429 us -> 141 us (0.33)
  waiting for transfers between devices: 322 us -> 36.3 us
  Pallas kernels: 0 us -> 44.1 us
  local copies, waits for them, and re-layouts: 51.3 us -> 10.6 us
  starting transfers between devices: 7.93 us -> 47.9 us
  matrix products: 33.8 us -> 0.57 us
  between operations: 13.4 us -> 0.3 us
    psum x1 -> x0, waiting for transfers between devices: 205 us -> none  [body(): lax.psum(jnp.einsum('pb,kb->pk', aux_factors, flat, preferred_element_typ...]
    all_to_all x1 -> x4, waiting for transfers between devices: 117 us -> 23.5 us  [cross(): lax.all_to_all(total.reshape(8, part, width), ('xl', 'c', 'xh'), split_ax...]
    pallas_call x0 -> x19, Pallas kernels: none -> 44.1 us  [the longest x6 23.4 us: call(): pl.pallas_call(kernel, grid_spec=pltpu.PrefetchScalarGridSpec(num_scalar_...]
    dot_general x3 -> x2, matrix products: 33.8 us -> 0.57 us  [the longest x1 0.38 us: body(): weights = jnp.dot(freq_basis, picked, precision=exact)]
    ppermute x0 -> x21, starting transfers between devices: none -> 26.8 us  [the longest x18 23.8 us: shift(): return lax.ppermute(v, axis, [(i, (i + by) % n) for i in range(n)])]
    dot_general x1 -> x0, local copies, waits for them, and re-layouts: 14.6 us -> none  [body(): jnp.einsum('lt,tmb->lmb', fit_matrix, lax.all_to_all(green_tau, 'tau', sp...]
    all_to_all x1 -> x4, starting transfers between devices: 7.89 us -> 21.1 us  [cross(): lax.all_to_all(total.reshape(8, part, width), ('xl', 'c', 'xh'), split_ax...]
    ppermute x0 -> x21, waiting for transfers between devices: none -> 12.8 us  [the longest x18 12.8 us: shift(): return lax.ppermute(v, axis, [(i, (i + by) % n) for i in range(n)])]
  transfers between devices with their start and end apart: 2 -> 25, of which waited for: 2 -> 11; matrix products, arithmetic and copies ran while one was open for 0% -> 1% of each run, Pallas kernels for 0% -> 25%
where the time goes in v2:
time: 141 us; the launch traced here: 140 us
  starting transfers between devices  47.9 us (34%)
  Pallas kernels  44.1 us (31%)
  waiting for transfers between devices  36.3 us (26%)
  local copies, waits for them, and re-layouts  10.6 us (8%)
    ppermute x18, starting transfers between devices, shift(): return lax.ppermute(v, axis, [(i, (i + by) % n) for i in range(n)])  23.8 us
    all_to_all x4, waiting for transfers between devices, cross(): lax.all_to_all(total.reshape(8, part, width), ('xl', 'c', 'xh'), split_ax...  23.5 us
    pallas_call x6, Pallas kernels, call(): pl.pallas_call(kernel, grid_spec=pltpu.PrefetchScalarGridSpec(num_scalar_...  23.4 us
    all_to_all x4, starting transfers between devices, cross(): lax.all_to_all(total.reshape(8, part, width), ('xl', 'c', 'xh'), split_ax...  21.1 us
    ppermute x18, waiting for transfers between devices, shift(): return lax.ppermute(v, axis, [(i, (i + by) % n) for i in range(n)])  12.8 us
    unnamed x20, local copies, waits for them, and re-layouts  10.6 us
    pallas_call x1, Pallas kernels, own(): pl.pallas_call(own_kernel, grid_spec=pltpu.PrefetchScalarGridSpec(num_sca...  7.19 us
    pallas_call x4, Pallas kernels, cross(): pl.pallas_call(sum_kernel, grid=(1,), in_specs=[pl.BlockSpec((1, *message...  7.14 us
  transfers between devices with their start and end apart: 25, of which 11 were waited for; matrix products, arithmetic and copies ran while one was open for 1% of the time, Pallas kernels for 25%

profile of v2, /device:TPU:1, one launch (start us, length us, event | category | flops | bytes accessed | tf_op | source)
XLA Modules:
  0.0 140.0 jit_solution(17483885596500948246)
XLA Ops:
  3.1 4.0 %copy-done.5 = bf16[2048,2560]{1,0:T(8,128)(2,1)S(1)} copy-done((bf16[2048,2560]{1,0:T(8,128)(2,1)S(1)}, bf16[2048,2560]{1,0:T(8,128)(2,1)}, u32[]{:S(2)}) %copy-start.5) | copy-done | bytes 10485784
  7.9 3.8 %collective-permute-start.3 = (s32[4,16,20]{2,1,0:T(8,128)S(1)}, s32[4,16,20]{2,1,0:T(8,128)S(1)}, u32[]{:S(2)}, u32[]{:S(2)}) collective-permute-start(s32[4,16,20]{2,1,0:T(8,128)S(1)} %shard_map.64.after.refs_1_.mask_ref), channel_id=1, source_target_pairs={{0,64},{32,96},{64,0},{96,32},{1,65},{33,97},{65,1},{97,33},{2,66}... | collective-permute-start | bytes 15368 | tf_op jit(solution)/shard_map/ppermute | solution.py:137
  13.3 3.7 %shard_map.67 = (bf16[2,512,256]{2,1,0:T(8,128)(2,1)S(1)}, bf16[2,512,256]{2,1,0:T(8,128)(2,1)S(1)}) custom-call(s32[3]{0:T(128)S(1)} %pad_add_fusion.1.after.at, bf16[8,16,16,2560]{3,2,1,0:T(8,128)(2,1)S(1)} %shard_map.65.green_ref, bf16[2,4,256,2560]{3,2,1,0:T(8,128)(2,1)S(1)} %shard_map.66.aux_ref, s32[4,16,20]{2,1,0:T(8,128)S(1)} %shard_map.64.after.refs_1_.mask_ref, ...), custom_call_target="tpu_custom_call" | custom-call | flops 4000000000 | bytes 20000000 | tf_op jit(solution)/shard_map/pallas_call | solution.py:177
  17.1 2.8 %collective-permute-start.6 = (bf16[2,512,256]{2,1,0:T(8,128)(2,1)S(1)}, bf16[2,512,256]{2,1,0:T(8,128)(2,1)S(1)}, u32[]{:S(2)}, u32[]{:S(2)}) collective-permute-start(bf16[2,512,256]{2,1,0:T(8,128)(2,1)S(1)} %get-tuple-element.17.after), channel_id=1, source_target_pairs={{0,3},{1,0},{2,1},{3,2},{4,7},{5,4},{6,5},{7,6},{8,11},{9,8},{10,9... | collective-permute-start | bytes 1572872 | tf_op jit(solution)/shard_map/ppermute | solution.py:137
  19.9 2.8 %collective-permute-start.4 = (s32[4,16,20]{2,1,0:T(8,128)S(1)}, s32[4,16,20]{2,1,0:T(8,128)S(1)}, u32[]{:S(2)}, u32[]{:S(2)}) collective-permute-start(s32[4,16,20]{2,1,0:T(8,128)S(1)} %shard_map.64.after.refs_1_.mask_ref), channel_id=1, source_target_pairs={{0,96},{32,0},{64,32},{96,64},{1,97},{33,1},{65,33},{97,65},{2,98}... | collective-permute-start | bytes 15368 | tf_op jit(solution)/shard_map/ppermute | solution.py:137
  23.7 3.2 %collective-permute-done.5.refs_1_.mask_ref = s32[4,16,20]{2,1,0:T(8,128)S(1)} collective-permute-done((s32[4,16,20]{2,1,0:T(8,128)S(1)}, s32[4,16,20]{2,1,0:T(8,128)S(1)}, u32[]{:S(2)}, u32[]{:S(2)}) %collective-permute-start.5) | collective-permute-done | bytes 5152 | tf_op jit(solution)/shard_map/ppermute | solution.py:137
  27.0 3.7 %shard_map.68 = (bf16[2,512,256]{2,1,0:T(8,128)(2,1)S(1)}, bf16[2,512,256]{2,1,0:T(8,128)(2,1)S(1)}) custom-call(s32[3]{0:T(128)S(1)} %pad_add_fusion.1.after.at, bf16[8,16,16,2560]{3,2,1,0:T(8,128)(2,1)S(1)} %shard_map.65.green_ref, bf16[2,4,256,2560]{3,2,1,0:T(8,128)(2,1)S(1)} %shard_map.66.aux_ref, bf16[2,512,256]{2,1,0:T(8,128)(2,1)S(1)} %get-tuple-element.17.after, ...), custom_call_target="tpu_custom_call" | custom-call | flops 4000000000 | bytes 20000000 | tf_op jit(solution)/shard_map/pallas_call | solution.py:177
  30.7 2.7 %collective-permute-start.8 = (bf16[2,512,256]{2,1,0:T(8,128)(2,1)S(1)}, bf16[2,512,256]{2,1,0:T(8,128)(2,1)S(1)}, u32[]{:S(2)}, u32[]{:S(2)}) collective-permute-start(bf16[2,512,256]{2,1,0:T(8,128)(2,1)S(1)} %get-tuple-element.18.after), channel_id=1, source_target_pairs={{0,3},{1,0},{2,1},{3,2},{4,7},{5,4},{6,5},{7,6},{8,11},{9,8},{10,9... | collective-permute-start | bytes 1572872 | tf_op jit(solution)/shard_map/ppermute | solution.py:137
  33.5 3.6 %shard_map.69 = (bf16[4,2,128,256]{3,2,1,0:T(8,128)(2,1)S(1)}, bf16[4,2,128,256]{3,2,1,0:T(8,128)(2,1)S(1)}) custom-call(s32[3]{0:T(128)S(1)} %pad_add_fusion.1.after.at, bf16[8,16,16,2560]{3,2,1,0:T(8,128)(2,1)S(1)} %shard_map.65.green_ref, bf16[2,4,256,2560]{3,2,1,0:T(8,128)(2,1)S(1)} %shard_map.66.aux_ref, ...), custom_call_target="tpu_custom_call" | custom-call | flops 4000000000 | bytes 20000000 | tf_op jit(solution)/shard_map/pallas_call | solution.py:177
  37.1 2.8 %collective-permute-start.10 = (bf16[4,2,128,256]{3,2,1,0:T(8,128)(2,1)S(1)}, bf16[4,2,128,256]{3,2,1,0:T(8,128)(2,1)S(1)}, u32[]{:S(2)}, u32[]{:S(2)}) collective-permute-start(bf16[4,2,128,256]{3,2,1,0:T(8,128)(2,1)S(1)} %get-tuple-element.20.after), channel_id=1, source_target_pairs={{0,3},{1,0},{2,1},{3,2},{4,7},{5,4},{6,5},{7,6},{8,11},{9,8},{10,9... | collective-permute-start | bytes 1572872 | tf_op jit(solution)/shard_map/ppermute | solution.py:137
  39.8 7.2 %shard_map.70.after.own_ref = f32[4,4,2,128,256]{4,3,2,1,0:T(8,128)S(1)} custom-call(s32[3]{0:T(128)S(1)} %pad_add_fusion.1.after.at, bf16[8,16,16,2560]{3,2,1,0:T(8,128)(2,1)S(1)} %shard_map.65.green_ref, bf16[2,4,256,2560]{3,2,1,0:T(8,128)(2,1)S(1)} %shard_map.66.aux_ref, bf16[4,2,128,256]{3,2,1,0:T(8,128)(2,1)S(1)} %get-tuple-element.20.after, ...), custom_call_target="tpu_custom_call" | custom-call | flops 4000000000 | bytes 20000000 | tf_op jit(solution)/shard_map/pallas_call | solution.py:221
  47.1 3.6 %shard_map.71 = (bf16[4,2,128,256]{3,2,1,0:T(8,128)(2,1)S(1)}, bf16[4,2,128,256]{3,2,1,0:T(8,128)(2,1)S(1)}) custom-call(s32[3]{0:T(128)S(1)} %pad_add_fusion.1.after.at, bf16[8,16,16,2560]{3,2,1,0:T(8,128)(2,1)S(1)} %shard_map.65.green_ref, bf16[2,4,256,2560]{3,2,1,0:T(8,128)(2,1)S(1)} %shard_map.66.aux_ref, ...), custom_call_target="tpu_custom_call" | custom-call | flops 4000000000 | bytes 20000000 | tf_op jit(solution)/shard_map/pallas_call | solution.py:177
  50.7 2.7 %collective-permute-start.14 = (bf16[4,2,128,256]{3,2,1,0:T(8,128)(2,1)S(1)}, bf16[4,2,128,256]{3,2,1,0:T(8,128)(2,1)S(1)}, u32[]{:S(2)}, u32[]{:S(2)}) collective-permute-start(bf16[4,2,128,256]{3,2,1,0:T(8,128)(2,1)S(1)} %get-tuple-element.22.after), channel_id=1, source_target_pairs={{0,3},{1,0},{2,1},{3,2},{4,7},{5,4},{6,5},{7,6},{8,11},{9,8},{10,9... | collective-permute-start | bytes 1572872 | tf_op jit(solution)/shard_map/ppermute | solution.py:137
  53.4 4.4 %shard_map.72 = (bf16[4,2,128,256]{3,2,1,0:T(8,128)(2,1)}, bf16[4,2,128,256]{3,2,1,0:T(8,128)(2,1)}) custom-call(s32[3]{0:T(128)S(1)} %pad_add_fusion.1.after.at, bf16[8,16,16,2560]{3,2,1,0:T(8,128)(2,1)S(1)} %shard_map.65.green_ref, bf16[2,4,256,2560]{3,2,1,0:T(8,128)(2,1)S(1)} %shard_map.66.aux_ref, bf16[4,2,128,256]{3,2,1,0:T(8,128)(2,1)S(1)} %get-tuple-element.22.after, ...), custom_call_target="tpu_custom_call" | custom-call | flops 1000000 | bytes 100000 | tf_op jit(solution)/shard_map/pallas_call | solution.py:177
  60.4 4.4 %shard_map.73 = (bf16[4,2,128,256]{3,2,1,0:T(8,128)(2,1)}, bf16[4,2,128,256]{3,2,1,0:T(8,128)(2,1)}) custom-call(s32[3]{0:T(128)S(1)} %pad_add_fusion.1.after.at, bf16[8,16,16,2560]{3,2,1,0:T(8,128)(2,1)S(1)} %shard_map.65.green_ref, bf16[2,4,256,2560]{3,2,1,0:T(8,128)(2,1)S(1)} %shard_map.66.aux_ref, bf16[4,2,128,256]{3,2,1,0:T(8,128)(2,1)} %get-tuple-element.23.after, ...), custom_call_target="tpu_custom_call" | custom-call | flops 1000000 | bytes 100000 | tf_op jit(solution)/shard_map/pallas_call | solution.py:177
  66.0 9.3 %all-to-all-start.1 = ((f32[8,128,256]{2,1,0:T(8,128)}), f32[8,128,256]{2,1,0:T(8,128)S(1)}, u32[]{:S(2)}, u32[]{:S(2)}) async-start(f32[8,128,256]{2,1,0:T(8,128)} %bitcast.11), calls=%async_computation.1 | async-start | bytes 2097152 | tf_op jit(solution)/shard_map/all_to_all | solution.py:248
  79.5 10.7 %all-to-all-done.1.got_ref = f32[8,128,256]{2,1,0:T(8,128)S(1)} async-done(((f32[8,128,256]{2,1,0:T(8,128)}), f32[8,128,256]{2,1,0:T(8,128)S(1)}, u32[]{:S(2)}, u32[]{:S(2)}) %all-to-all-start.1) | async-done | bytes 1048608 | tf_op jit(solution)/shard_map/all_to_all | solution.py:248
  90.3 3.9 %all-to-all-start = ((bf16[8,128,256]{2,1,0:T(8,128)(2,1)}), bf16[8,128,256]{2,1,0:T(8,128)(2,1)S(1)}, u32[]{:S(2)}, u32[]{:S(2)}) async-start(bf16[8,128,256]{2,1,0:T(8,128)(2,1)} %bitcast.10), calls=%async_computation | async-start | bytes 1048576 | tf_op jit(solution)/shard_map/all_to_all | solution.py:248
  94.2 2.9 %collective-permute-start.12 = (bf16[4,2,128,256]{3,2,1,0:T(8,128)(2,1)}, bf16[4,2,128,256]{3,2,1,0:T(8,128)(2,1)S(1)}, u32[]{:S(2)}, u32[]{:S(2)}) collective-permute-start(bf16[4,2,128,256]{3,2,1,0:T(8,128)(2,1)} %get-tuple-element.25.after), channel_id=1, source_target_pairs={{0,3},{1,0},{2,1},{3,2},{4,7},{5,4},{6,5},{7,6},{8,11},{9,8},{10,9... | collective-permute-start | bytes 1572872 | tf_op jit(solution)/shard_map/ppermute | solution.py:137
  103.9 3.4 %all-to-all-start.3 = ((bf16[8,128,256]{2,1,0:T(8,128)(2,1)}), bf16[8,128,256]{2,1,0:T(8,128)(2,1)S(1)}, u32[]{:S(2)}, u32[]{:S(2)}) async-start(bf16[8,128,256]{2,1,0:T(8,128)(2,1)} %bitcast.13), calls=%async_computation.3 | async-start | bytes 1048576 | tf_op jit(solution)/shard_map/all_to_all | solution.py:248
  108.6 3.1 %collective-permute-done.13.from_down = bf16[4,2,128,256]{3,2,1,0:T(8,128)(2,1)} collective-permute-done((bf16[4,2,128,256]{3,2,1,0:T(8,128)(2,1)}, bf16[4,2,128,256]{3,2,1,0:T(8,128)(2,1)}, u32[]{:S(2)}, u32[]{:S(2)}) %collective-permute-start.13) | collective-permute-done | bytes 524320 | tf_op jit(solution)/shard_map/ppermute | solution.py:137
  117.1 4.5 %all-to-all-start.2 = ((bf16[8,128,256]{2,1,0:T(8,128)(2,1)}), bf16[8,128,256]{2,1,0:T(8,128)(2,1)S(1)}, u32[]{:S(2)}, u32[]{:S(2)}) async-start(bf16[8,128,256]{2,1,0:T(8,128)(2,1)} %bitcast.12), calls=%async_computation.2 | async-start | bytes 1048576 | tf_op jit(solution)/shard_map/all_to_all | solution.py:248
  122.5 8.9 %all-to-all-done.2.got_ref = bf16[8,128,256]{2,1,0:T(8,128)(2,1)S(1)} async-done(((bf16[8,128,256]{2,1,0:T(8,128)(2,1)}), bf16[8,128,256]{2,1,0:T(8,128)(2,1)S(1)}, u32[]{:S(2)}, u32[]{:S(2)}) %all-to-all-start.2) | async-done | bytes 524320 | tf_op jit(solution)/shard_map/all_to_all | solution.py:248
  135.3 4.7 %shard_map.82 = f32[3840,256]{1,0:T(8,128)} custom-call(f32[240,128]{1,0:T(8,128)S(1)} %convolution_bitcast_fusion.w_ref, f32[120,256]{1,0:T(8,128)S(1)} %copy-done.7, f32[512,256]{1,0:T(8,128)S(1)} %shard_map.81.refs_0_, f32[512,256]{1,0:T(8,128)} %collective-permute-done.18.refs_1_, f32[512,256]{1,0:T(8,128)} %collective-permute-done.19.refs_2_, ...), custom_call_target="tpu_custom_call" | custom-call | tf_op jit(solution)/shard_map/pallas_call | solution.py:286
  (72 shorter events, 32.7 us)
Async XLA Ops:
  0.0 7.8 %collective-permute-start = (s32[16,20]{1,0:T(8,128)}, s32[16,20]{1,0:T(8,128)S(1)}, u32[]{:S(2)}, u32[]{:S(2)}) collective-permute-start(s32[16,20]{1,0:T(8,128)} %a.1), channel_id=1, source_target_pairs={{0,8},{8,0},{16,24},{24,16},{1,9},{9,1},{17,25},{25,17},{2,10},{10... | collective-permute-start | bytes 3848 | tf_op jit(solution)/shard_map/ppermute | solution.py:162
  1.4 6.4 %collective-permute-start.1 = (s32[16,20]{1,0:T(8,128)}, s32[16,20]{1,0:T(8,128)S(1)}, u32[]{:S(2)}, u32[]{:S(2)}) collective-permute-start(s32[16,20]{1,0:T(8,128)} %a.1), channel_id=1, source_target_pairs={{0,16},{8,24},{16,0},{24,8},{1,17},{9,25},{17,1},{25,9},{2,18},{10... | collective-permute-start | bytes 3848 | tf_op jit(solution)/shard_map/ppermute | solution.py:162
  2.7 5.1 %collective-permute-start.2 = (s32[16,20]{1,0:T(8,128)}, s32[16,20]{1,0:T(8,128)S(1)}, u32[]{:S(2)}, u32[]{:S(2)}) collective-permute-start(s32[16,20]{1,0:T(8,128)} %a.1), channel_id=1, source_target_pairs={{0,24},{8,16},{16,8},{24,0},{1,25},{9,17},{17,9},{25,1},{2,26},{10... | collective-permute-start | bytes 3848 | tf_op jit(solution)/shard_map/ppermute | solution.py:162
  7.9 5.5 %collective-permute-start.3 = (s32[4,16,20]{2,1,0:T(8,128)S(1)}, s32[4,16,20]{2,1,0:T(8,128)S(1)}, u32[]{:S(2)}, u32[]{:S(2)}) collective-permute-start(s32[4,16,20]{2,1,0:T(8,128)S(1)} %shard_map.64.after.refs_1_.mask_ref), channel_id=1, source_target_pairs={{0,64},{32,96},{64,0},{96,32},{1,65},{33,97},{65,1},{97,33},{2,66}... | collective-permute-start | bytes 15368 | tf_op jit(solution)/shard_map/ppermute | solution.py:137
  17.1 16.4 %collective-permute-start.6 = (bf16[2,512,256]{2,1,0:T(8,128)(2,1)S(1)}, bf16[2,512,256]{2,1,0:T(8,128)(2,1)S(1)}, u32[]{:S(2)}, u32[]{:S(2)}) collective-permute-start(bf16[2,512,256]{2,1,0:T(8,128)(2,1)S(1)} %get-tuple-element.17.after), channel_id=1, source_target_pairs={{0,3},{1,0},{2,1},{3,2},{4,7},{5,4},{6,5},{7,6},{8,11},{9,8},{10,9... | collective-permute-start | bytes 1572872 | tf_op jit(solution)/shard_map/ppermute | solution.py:137
  19.9 13.6 %collective-permute-start.7 = (bf16[2,512,256]{2,1,0:T(8,128)(2,1)S(1)}, bf16[2,512,256]{2,1,0:T(8,128)(2,1)S(1)}, u32[]{:S(2)}, u32[]{:S(2)}) collective-permute-start(bf16[2,512,256]{2,1,0:T(8,128)(2,1)S(1)} %get-tuple-element.19), channel_id=1, source_target_pairs={{0,1},{1,2},{2,3},{3,0},{4,5},{5,6},{6,7},{7,4},{8,9},{9,10},{10,1... | collective-permute-start | bytes 1572872 | tf_op jit(solution)/shard_map/ppermute | solution.py:137
  22.7 4.3 %collective-permute-start.5 = (s32[4,16,20]{2,1,0:T(8,128)S(1)}, s32[4,16,20]{2,1,0:T(8,128)S(1)}, u32[]{:S(2)}, u32[]{:S(2)}) collective-permute-start(s32[4,16,20]{2,1,0:T(8,128)S(1)} %shard_map.64.after.refs_1_.mask_ref), channel_id=1, source_target_pairs={{0,32},{32,64},{64,96},{96,0},{1,33},{33,65},{65,97},{97,1},{2,34}... | collective-permute-start | bytes 15368 | tf_op jit(solution)/shard_map/ppermute | solution.py:137
  30.7 16.3 %collective-permute-start.8 = (bf16[2,512,256]{2,1,0:T(8,128)(2,1)S(1)}, bf16[2,512,256]{2,1,0:T(8,128)(2,1)S(1)}, u32[]{:S(2)}, u32[]{:S(2)}) collective-permute-start(bf16[2,512,256]{2,1,0:T(8,128)(2,1)S(1)} %get-tuple-element.18.after), channel_id=1, source_target_pairs={{0,3},{1,0},{2,1},{3,2},{4,7},{5,4},{6,5},{7,6},{8,11},{9,8},{10,9... | collective-permute-start | bytes 1572872 | tf_op jit(solution)/shard_map/ppermute | solution.py:137
  33.5 13.6 %collective-permute-start.9 = (bf16[2,512,256]{2,1,0:T(8,128)(2,1)S(1)}, bf16[2,512,256]{2,1,0:T(8,128)(2,1)S(1)}, u32[]{:S(2)}, u32[]{:S(2)}) collective-permute-start(bf16[2,512,256]{2,1,0:T(8,128)(2,1)S(1)} %get-tuple-element.21), channel_id=1, source_target_pairs={{0,1},{1,2},{2,3},{3,0},{4,5},{5,6},{6,7},{7,4},{8,9},{9,10},{10,1... | collective-permute-start | bytes 1572872 | tf_op jit(solution)/shard_map/ppermute | solution.py:137
  37.1 23.4 %collective-permute-start.10 = (bf16[4,2,128,256]{3,2,1,0:T(8,128)(2,1)S(1)}, bf16[4,2,128,256]{3,2,1,0:T(8,128)(2,1)S(1)}, u32[]{:S(2)}, u32[]{:S(2)}) collective-permute-start(bf16[4,2,128,256]{3,2,1,0:T(8,128)(2,1)S(1)} %get-tuple-element.20.after), channel_id=1, source_target_pairs={{0,3},{1,0},{2,1},{3,2},{4,7},{5,4},{6,5},{7,6},{8,11},{9,8},{10,9... | collective-permute-start | bytes 1572872 | tf_op jit(solution)/shard_map/ppermute | solution.py:137
  39.8 20.6 %collective-permute-start.11 = (bf16[4,2,128,256]{3,2,1,0:T(8,128)(2,1)S(1)}, bf16[4,2,128,256]{3,2,1,0:T(8,128)(2,1)S(1)}, u32[]{:S(2)}, u32[]{:S(2)}) collective-permute-start(bf16[4,2,128,256]{3,2,1,0:T(8,128)(2,1)S(1)} %get-tuple-element.24), channel_id=1, source_target_pairs={{0,1},{1,2},{2,3},{3,0},{4,5},{5,6},{6,7},{7,4},{8,9},{9,10},{10,1... | collective-permute-start | bytes 1572872 | tf_op jit(solution)/shard_map/ppermute | solution.py:137
  50.7 24.6 %collective-permute-start.14 = (bf16[4,2,128,256]{3,2,1,0:T(8,128)(2,1)S(1)}, bf16[4,2,128,256]{3,2,1,0:T(8,128)(2,1)S(1)}, u32[]{:S(2)}, u32[]{:S(2)}) collective-permute-start(bf16[4,2,128,256]{3,2,1,0:T(8,128)(2,1)S(1)} %get-tuple-element.22.after), channel_id=1, source_target_pairs={{0,3},{1,0},{2,1},{3,2},{4,7},{5,4},{6,5},{7,6},{8,11},{9,8},{10,9... | collective-permute-start | bytes 1572872 | tf_op jit(solution)/shard_map/ppermute | solution.py:137
  53.4 21.9 %collective-permute-start.15 = (bf16[4,2,128,256]{3,2,1,0:T(8,128)(2,1)S(1)}, bf16[4,2,128,256]{3,2,1,0:T(8,128)(2,1)}, u32[]{:S(2)}, u32[]{:S(2)}) collective-permute-start(bf16[4,2,128,256]{3,2,1,0:T(8,128)(2,1)S(1)} %get-tuple-element.27), channel_id=1, source_target_pairs={{0,1},{1,2},{2,3},{3,0},{4,5},{5,6},{6,7},{7,4},{8,9},{9,10},{10,1... | collective-permute-start | bytes 1572872 | tf_op jit(solution)/shard_map/ppermute | solution.py:137
  57.8 39.4 %collective-permute-start.16 = (bf16[4,2,128,256]{3,2,1,0:T(8,128)(2,1)}, bf16[4,2,128,256]{3,2,1,0:T(8,128)(2,1)S(1)}, u32[]{:S(2)}, u32[]{:S(2)}) collective-permute-start(bf16[4,2,128,256]{3,2,1,0:T(8,128)(2,1)} %get-tuple-element.23.after), channel_id=1, source_target_pairs={{0,3},{1,0},{2,1},{3,2},{4,7},{5,4},{6,5},{7,6},{8,11},{9,8},{10,9... | collective-permute-start | bytes 1572872 | tf_op jit(solution)/shard_map/ppermute | solution.py:137
  60.4 36.7 %collective-permute-start.17 = (bf16[4,2,128,256]{3,2,1,0:T(8,128)(2,1)}, bf16[4,2,128,256]{3,2,1,0:T(8,128)(2,1)}, u32[]{:S(2)}, u32[]{:S(2)}) collective-permute-start(bf16[4,2,128,256]{3,2,1,0:T(8,128)(2,1)} %get-tuple-element.28), channel_id=1, source_target_pairs={{0,1},{1,2},{2,3},{3,0},{4,5},{5,6},{6,7},{7,4},{8,9},{9,10},{10,1... | collective-permute-start | bytes 1572872 | tf_op jit(solution)/shard_map/ppermute | solution.py:137
  66.0 24.3 %all-to-all-start.1 = ((f32[8,128,256]{2,1,0:T(8,128)}), f32[8,128,256]{2,1,0:T(8,128)S(1)}, u32[]{:S(2)}, u32[]{:S(2)}) async-start(f32[8,128,256]{2,1,0:T(8,128)} %bitcast.11), calls=%async_computation.1 | async-start | bytes 2097152 | tf_op jit(solution)/shard_map/all_to_all | solution.py:248
  90.3 13.7 %all-to-all-start = ((bf16[8,128,256]{2,1,0:T(8,128)(2,1)}), bf16[8,128,256]{2,1,0:T(8,128)(2,1)S(1)}, u32[]{:S(2)}, u32[]{:S(2)}) async-start(bf16[8,128,256]{2,1,0:T(8,128)(2,1)} %bitcast.10), calls=%async_computation | async-start | bytes 1048576 | tf_op jit(solution)/shard_map/all_to_all | solution.py:248
  94.2 14.4 %collective-permute-start.12 = (bf16[4,2,128,256]{3,2,1,0:T(8,128)(2,1)}, bf16[4,2,128,256]{3,2,1,0:T(8,128)(2,1)S(1)}, u32[]{:S(2)}, u32[]{:S(2)}) collective-permute-start(bf16[4,2,128,256]{3,2,1,0:T(8,128)(2,1)} %get-tuple-element.25.after), channel_id=1, source_target_pairs={{0,3},{1,0},{2,1},{3,2},{4,7},{5,4},{6,5},{7,6},{8,11},{9,8},{10,9... | collective-permute-start | bytes 1572872 | tf_op jit(solution)/shard_map/ppermute | solution.py:137
  97.1 14.6 %collective-permute-start.13 = (bf16[4,2,128,256]{3,2,1,0:T(8,128)(2,1)}, bf16[4,2,128,256]{3,2,1,0:T(8,128)(2,1)}, u32[]{:S(2)}, u32[]{:S(2)}) collective-permute-start(bf16[4,2,128,256]{3,2,1,0:T(8,128)(2,1)} %get-tuple-element.26), channel_id=1, source_target_pairs={{0,1},{1,2},{2,3},{3,0},{4,5},{5,6},{6,7},{7,4},{8,9},{9,10},{10,1... | collective-permute-start | bytes 1572872 | tf_op jit(solution)/shard_map/ppermute | solution.py:137
  103.9 13.2 %all-to-all-start.3 = ((bf16[8,128,256]{2,1,0:T(8,128)(2,1)}), bf16[8,128,256]{2,1,0:T(8,128)(2,1)S(1)}, u32[]{:S(2)}, u32[]{:S(2)}) async-start(bf16[8,128,256]{2,1,0:T(8,128)(2,1)} %bitcast.13), calls=%async_computation.3 | async-start | bytes 1048576 | tf_op jit(solution)/shard_map/all_to_all | solution.py:248
  107.5 26.4 %collective-permute-start.19 = (f32[512,256]{1,0:T(8,128)S(1)}, f32[512,256]{1,0:T(8,128)}, u32[]{:S(2)}, u32[]{:S(2)}) collective-permute-start(f32[512,256]{1,0:T(8,128)S(1)} %shard_map.76.after), channel_id=1, source_target_pairs={{0,64},{32,96},{64,0},{96,32},{1,65},{33,97},{65,1},{97,33},{2,66}... | collective-permute-start | bytes 1572872 | tf_op jit(solution)/shard_map/ppermute | solution.py:137
  107.6 26.3 %collective-permute-start.18 = (f32[512,256]{1,0:T(8,128)S(1)}, f32[512,256]{1,0:T(8,128)}, u32[]{:S(2)}, u32[]{:S(2)}) collective-permute-start(f32[512,256]{1,0:T(8,128)S(1)} %shard_map.78.after), channel_id=1, source_target_pairs={{0,32},{32,64},{64,96},{96,0},{1,33},{33,65},{65,97},{97,1},{2,34}... | collective-permute-start | bytes 1572872 | tf_op jit(solution)/shard_map/ppermute | solution.py:137
  117.1 14.2 %all-to-all-start.2 = ((bf16[8,128,256]{2,1,0:T(8,128)(2,1)}), bf16[8,128,256]{2,1,0:T(8,128)(2,1)S(1)}, u32[]{:S(2)}, u32[]{:S(2)}) async-start(bf16[8,128,256]{2,1,0:T(8,128)(2,1)} %bitcast.12), calls=%async_computation.2 | async-start | bytes 1048576 | tf_op jit(solution)/shard_map/all_to_all | solution.py:248
  121.7 13.6 %collective-permute-start.20 = (f32[512,256]{1,0:T(8,128)S(1)}, f32[512,256]{1,0:T(8,128)S(1)}, u32[]{:S(2)}, u32[]{:S(2)}) collective-permute-start(f32[512,256]{1,0:T(8,128)S(1)} %shard_map.80.after), channel_id=1, source_target_pairs={{0,96},{32,0},{64,32},{96,64},{1,97},{33,1},{65,33},{97,65},{2,98}... | collective-permute-start | bytes 1572872 | tf_op jit(solution)/shard_map/ppermute | solution.py:137
  (11 other events, 229.5 us)

commit v3 on v2

--- a/solution.py
+++ b/solution.py
@@ -53,7 +53,7 @@
 
 
 def far_kernel(chunks, at, green_ref, aux_ref, after, *refs):
-    mask_refs, (lo_ref, hi_ref, rows_ref) = refs[: len(chunks)], refs[len(chunks) :]
+    mask_refs, (lo_ref, hi_ref, rows_ref) = refs[: len(chunks)], refs[-3:]
     target = lax.rem(at[0] + 2, aux_ref.shape[1])
     for q, chunk in enumerate(chunks):
         fill(at, chunk, green_ref, mask_refs[q], rows_ref)
@@ -61,15 +61,18 @@
         hi_ref[q] = product(rows_ref, aux_ref[1, target]).astype(jnp.bfloat16)
 
 
-def near_kernel(chunk, at, green_ref, aux_ref, after, mask_ref, from_up, from_down, *refs):
-    down_ref, up_ref, rows_ref = refs[-3:]
+def near_kernel(chunks, at, green_ref, aux_ref, after, *refs):
+    rows_ref = refs[-1]
     n = aux_ref.shape[1]
-    fill(at, chunk, green_ref, mask_ref, rows_ref)
     below, above = lax.rem(at[0] + n - 1, n), lax.rem(at[0] + 1, n)
-    put(down_ref, 0, product(rows_ref, aux_ref[0, below]) + from_up[0].astype(jnp.float32))
-    put(down_ref, 1, product(rows_ref, aux_ref[1, below]))
-    put(up_ref, 0, product(rows_ref, aux_ref[0, above]))
-    put(up_ref, 1, product(rows_ref, aux_ref[1, above]) + from_down[0].astype(jnp.float32))
+    for q, chunk in enumerate(chunks):
+        mask_ref, from_up, from_down = refs[3 * q : 3 * q + 3]
+        down_ref, up_ref = refs[2 * q - 1 - 2 * len(chunks) :][:2]
+        fill(at, chunk, green_ref, mask_ref, rows_ref)
+        put(down_ref, 0, product(rows_ref, aux_ref[0, below]) + from_up[0].astype(jnp.float32))
+        put(down_ref, 1, product(rows_ref, aux_ref[1, below]))
+        put(up_ref, 0, product(rows_ref, aux_ref[0, above]))
+        put(up_ref, 1, product(rows_ref, aux_ref[1, above]) + from_down[0].astype(jnp.float32))
 
 
 def own_kernel(at, green_ref, aux_ref, after, mask_refs, out_ref, rows_ref):
@@ -79,18 +82,22 @@
         put(out_ref.at[0], h, product(rows_ref, aux_ref[h, at[0]]))
 
 
-def sum_kernel(own_ref, from_up, from_down, after, out_ref):
-    for i in range(4):
-        for h in range(2):
-            others = from_up[i, h].astype(jnp.float32) + from_down[i, h].astype(jnp.float32)
-            out_ref[i, h] = (own_ref[0, i, h] + others).astype(out_ref.dtype)
-
-
-def gather_kernel(got_ref, after, out_ref):
-    part = got_ref.shape[1]
-    for i in range(got_ref.shape[0] // 2):
-        both = got_ref[2 * i].astype(jnp.float32) + got_ref[2 * i + 1].astype(jnp.float32)
-        out_ref[i * part : (i + 1) * part] = both
+def sum_kernel(n, *refs):
+    out_ref = refs[-1]
+    for q in range(n):
+        own_ref, from_up, from_down = refs[3 * q : 3 * q + 3]
+        for i in range(4):
+            for h in range(2):
+                others = from_up[i, h].astype(jnp.float32) + from_down[i, h].astype(jnp.float32)
+                out_ref[2 * i + h, q] = (own_ref[0, i, h] + others).astype(out_ref.dtype)
+
+
+def gather_kernel(got_ref, after, *out_refs):
+    part = got_ref.shape[2]
+    for q, out_ref in enumerate(out_refs):
+        for i in range(4):
+            both = got_ref[2 * i, q].astype(jnp.float32) + got_ref[2 * i + 1, q].astype(jnp.float32)
+            out_ref[i * part : (i + 1) * part] = both
 
 
 def final_kernel(w_ref, s_ref, *refs):
@@ -161,7 +168,6 @@
         pairs = [(i * 2 + j, (i ^ e) * 2 + (j ^ f)) for i in (0, 1) for j in (0, 1)]
         return lax.ppermute(v, ("xl", "c"), pairs)
 
-    aux = stage(aux_factors.reshape(2, ny, width, cols), at)
     quad = pl.pallas_call(
         join_kernel,
         out_shape=shape((4, height, blocks), pair_mask.dtype),
@@ -169,6 +175,7 @@
         cost_estimate=LITTLE,
     )(pair_mask, swap(pair_mask, 0, 1), swap(pair_mask, 1, 0), swap(pair_mask, 1, 1))
     marks = [quad if d == 0 else shift(quad, "z", -d) for d in range(nz)]
+    aux = stage(aux_factors.reshape(2, ny, width, cols), quad)
     green = stage(green_tau.reshape(times, n_rows // height, height, cols), quad)
 
     def call(kernel, after, extra, extra_specs, out_shape, cost=COST):
@@ -191,10 +198,11 @@
 
     step1 = {}
 
-    def far(chunks, after):
+    def far(chunks, after, arrived=()):
         out = shape((len(chunks), rows, width), bf16)
         lo, hi = call(
-            functools.partial(far_kernel, chunks), after, [marks[d] for d in chunks], [None] * len(chunks), [out, out]
+            functools.partial(far_kernel, chunks), after,
+            [*(marks[d] for d in chunks), *arrived], [None] * len(chunks) + [ANY] * len(arrived), [out, out],
         )
         got = shift(lo, "y", -1), shift(hi, "y", 1)
         for q, d in enumerate(chunks):
@@ -204,20 +212,23 @@
     message = (4, 2, part, width)
     step2 = {}
 
-    def near(d, after, arrived=(), cost=COST):
-        q, got = step1[d]
-        spec = pl.BlockSpec((1, rows, width), lambda j, at: (q, 0, 0))
-        down, up = call(
-            functools.partial(near_kernel, d), after, [marks[d], *got, *arrived],
-            [None, spec, spec] + [ANY] * len(arrived),
-            [shape(message, bf16), shape(message, bf16)], cost,
+    def near(chunks, after, arrived=(), cost=COST):
+        args, specs = [], []
+        for d in chunks:
+            q, got = step1[d]
+            spec = pl.BlockSpec((1, rows, width), lambda j, at, q=q: (q, 0, 0))
+            args += [marks[d], *got]
+            specs += [None, spec, spec]
+        out = call(
+            functools.partial(near_kernel, chunks), after, args + [*arrived], specs + [ANY] * len(arrived),
+            [shape(message, bf16)] * (2 * len(chunks)), cost,
         )
-        step2[d] = shift(down, "y", -1), shift(up, "y", 1)
-        return down
+        for k, d in enumerate(chunks):
+            step2[d] = shift(out[2 * k], "y", -1), shift(out[2 * k + 1], "y", 1)
+        return out[0]
 
     def own(after):
         joined = jnp.concatenate(marks)
-        out = shape((nz, *message), f32)
         return pl.pallas_call(
             own_kernel,
             grid_spec=pltpu.PrefetchScalarGridSpec(
@@ -227,58 +238,57 @@
                 out_specs=pl.BlockSpec((1, *message), lambda j, at: (j, 0, 0, 0, 0)),
                 scratch_shapes=[pltpu.VMEM((rows, cols), bf16)],
             ),
-            out_shape=out,
+            out_shape=pltpu.HBM((nz, *message), f32),
             compiler_params=SMALL,
             cost_estimate=COST,
         )(at, green, aux, after, joined)
 
     crossed = {}
 
-    def cross(d, after, kind, cost=LITTLE):
+    def cross(chunks, after, kind, cost=LITTLE):
+        n = len(chunks)
         fixed = pl.BlockSpec(message, lambda j: (0, 0, 0, 0))
+        own_of = lambda d: pl.BlockSpec((1, *message), lambda j: (d, 0, 0, 0, 0))
         total = pl.pallas_call(
-            sum_kernel,
+            functools.partial(sum_kernel, n),
             grid=(1,),
-            in_specs=[pl.BlockSpec((1, *message), lambda j: (d, 0, 0, 0, 0)), fixed, fixed, ANY],
-            out_specs=fixed,
-            out_shape=shape(message, kind),
+            in_specs=[v for d in chunks for v in (own_of(d), fixed, fixed)] + [ANY],
+            out_specs=pl.BlockSpec((8, n, part, width), lambda j: (0, 0, 0, 0)),
+            out_shape=shape((8, n, part, width), kind),
             compiler_params=SMALL,
             cost_estimate=cost,
-        )(mine, *step2[d], after)
-        crossed[d] = lax.all_to_all(
-            total.reshape(8, part, width), ("xl", "c", "xh"), split_axis=0, concat_axis=0, tiled=True
-        )
+        )(*[v for d in chunks for v in (mine, *step2[d])], after)
+        crossed[chunks] = lax.all_to_all(total, ("xl", "c", "xh"), split_axis=0, concat_axis=0, tiled=True)
         return total
 
     pieces = {}
 
-    def gather(d, after):
-        got = crossed[d]
-        out = pl.pallas_call(
+    def gather(chunks, after):
+        got = crossed[chunks]
+        outs = pl.pallas_call(
             gather_kernel,
-            in_specs=[pl.BlockSpec(got.shape, lambda: (0, 0, 0)), ANY],
-            out_shape=shape((rows, width), f32),
+            in_specs=[pl.BlockSpec(got.shape, lambda: (0, 0, 0, 0)), ANY],
+            out_shape=[shape((rows, width), f32)] * len(chunks),
             compiler_params=SMALL,
             cost_estimate=LITTLE,
         )(got, after)
-        pieces[d] = out if d == 0 else shift(out, "z", d)
-        return out
-
-    last = far((2, 0), quad)
+        for d, out in zip(chunks, outs, strict=True):
+            pieces[d] = out if d == 0 else shift(out, "z", d)
+        return outs[0]
+
+    last = far((2, 0), quad, (marks[1], marks[3]))
     last = far((1, 3), last)
-    last = near(2, last)
+    last = near((2,), last)
     last = mine = own(last)
-    last = near(1, last)
-    last = near(3, last, cost=LITTLE)
-    last = near(0, last, step2[2], LITTLE)
-    last = cross(2, last, f32)
-    last = cross(1, last, bf16, LONG)
-    last = gather(2, last)
-    last = cross(3, last, bf16)
-    last = gather(1, last)
-    last = cross(0, last, bf16)
-    last = gather(3, last)
-    gather(0, last)
+    mine = pltpu.with_memory_space_constraint(mine, pltpu.HBM)
+    last = near((1,), last)
+    last = near((3, 0), last, cost=LITTLE)
+    last = cross((2,), last, f32)
+    last = cross((1, 3), last, bf16, LONG)
+    last = gather((2,), last)
+    last = cross((0,), last, bf16, LONG)
+    last = gather((1, 3), last)
+    gather((0,), last)
 
     n_freq = weights.shape[0]
     lane = lambda v: pl.BlockSpec((v.shape[0], LANES), lambda j: (0, j))

time: 141 us -> 147 us (1.043)
  waiting for transfers between devices: 36.3 us -> 44.6 us
  starting transfers between devices: 47.9 us -> 45.8 us
    ppermute x18, waiting for transfers between devices: 12.8 us -> 17.8 us  [shift(): return lax.ppermute(v, axis, [(i, (i + by) % n) for i in range(n)])]
    ppermute x3, waiting for transfers between devices: 0.01 us -> 2.88 us  [swap(): return lax.ppermute(v, ('xl', 'c'), pairs)]
    ppermute x18, starting transfers between devices: 23.8 us -> 22 us  [shift(): return lax.ppermute(v, axis, [(i, (i + by) % n) for i in range(n)])]
    pallas_call x6 -> x5, Pallas kernels: 23.4 us -> 21.9 us  [call(): pl.pallas_call(kernel, grid_spec=pltpu.PrefetchScalarGridSpec(num_scalar_...]
    pallas_call x4 -> x3, Pallas kernels: 7.14 us -> 8.28 us  [cross(): pl.pallas_call(functools.partial(sum_kernel, n), grid=(1,), in_specs=[v f...]
    all_to_all x4 -> x3, waiting for transfers between devices: 23.5 us -> 23.9 us  [cross(): lax.all_to_all(total, ('xl', 'c', 'xh'), split_axis=0, concat_axis=0, til...]
    unnamed x20 -> x16, local copies, waits for them, and re-layouts: 10.6 us -> 10.2 us
    all_to_all x4 -> x3, starting transfers between devices: 21.1 us -> 20.8 us  [cross(): lax.all_to_all(total, ('xl', 'c', 'xh'), split_axis=0, concat_axis=0, til...]
  transfers between devices with their start and end apart: 25 -> 24, of which waited for: 11 -> 10; matrix products, arithmetic and copies ran while one was open for 1% -> 1% of each run, Pallas kernels for 25% -> 25%
where the time goes in v3:
time: 147 us
  starting transfers between devices  45.8 us (31%)
  waiting for transfers between devices  44.6 us (30%)
  Pallas kernels  44.6 us (30%)
  local copies, waits for them, and re-layouts  10.3 us (7%)
    all_to_all x3, waiting for transfers between devices, cross(): lax.all_to_all(total, ('xl', 'c', 'xh'), split_axis=0, concat_axis=0, til...  23.9 us
    ppermute x18, starting transfers between devices, shift(): return lax.ppermute(v, axis, [(i, (i + by) % n) for i in range(n)])  22 us
    pallas_call x5, Pallas kernels, call(): pl.pallas_call(kernel, grid_spec=pltpu.PrefetchScalarGridSpec(num_scalar_...  21.9 us
    all_to_all x3, starting transfers between devices, cross(): lax.all_to_all(total, ('xl', 'c', 'xh'), split_axis=0, concat_axis=0, til...  20.8 us
    ppermute x18, waiting for transfers between devices, shift(): return lax.ppermute(v, axis, [(i, (i + by) % n) for i in range(n)])  17.8 us
    unnamed x16, local copies, waits for them, and re-layouts  10.2 us
    pallas_call x3, Pallas kernels, cross(): pl.pallas_call(functools.partial(sum_kernel, n), grid=(1,), in_specs=[v f...  8.28 us
    pallas_call x1, Pallas kernels, own(): pl.pallas_call(own_kernel, grid_spec=pltpu.PrefetchScalarGridSpec(num_sca...  8.2 us
  transfers between devices with their start and end apart: 24, of which 10 were waited for; matrix products, arithmetic and copies ran while one was open for 1% of the time, Pallas kernels for 25%

profile of v3, /device:TPU:1, one launch (start us, length us, event | category | flops | bytes accessed | tf_op | source)
XLA Modules:
  0.0 146.7 jit_solution(891313855040447898)
XLA Ops:
  6.7 3.8 %collective-permute-start.4 = (s32[4,16,20]{2,1,0:T(8,128)S(1)}, s32[4,16,20]{2,1,0:T(8,128)S(1)}, u32[]{:S(2)}, u32[]{:S(2)}) collective-permute-start(s32[4,16,20]{2,1,0:T(8,128)S(1)} %shard_map.64.after.refs_1_.refs_3_), channel_id=1, source_target_pairs={{0,96},{32,0},{64,32},{96,64},{1,97},{33,1},{65,33},{97,65},{2,98}... | collective-permute-start | bytes 15368 | tf_op jit(solution)/shard_map/ppermute | solution.py:144
  11.8 4.0 %copy-done.2 = bf16[8,256,2560]{2,1,0:T(8,128)(2,1)S(1)} copy-done((bf16[8,256,2560]{2,1,0:T(8,128)(2,1)S(1)}, bf16[8,256,2560]{2,1,0:T(8,128)(2,1)}, u32[]{:S(2)}) %copy-start.2) | copy-done | bytes 10485784
  16.5 3.3 %copy-done.3 = bf16[2048,2560]{1,0:T(8,128)(2,1)S(1)} copy-done((bf16[2048,2560]{1,0:T(8,128)(2,1)S(1)}, bf16[2048,2560]{1,0:T(8,128)(2,1)}, u32[]{:S(2)}) %copy-start.3) | copy-done | bytes 10485784
  20.5 3.7 %shard_map.67 = (bf16[2,512,256]{2,1,0:T(8,128)(2,1)S(1)}, bf16[2,512,256]{2,1,0:T(8,128)(2,1)S(1)}) custom-call(s32[3]{0:T(128)S(1)} %pad_add_fusion.1.at, bf16[8,16,16,2560]{3,2,1,0:T(8,128)(2,1)S(1)} %shard_map.65.green_ref, bf16[2,4,256,2560]{3,2,1,0:T(8,128)(2,1)S(1)} %shard_map.66.aux_ref, s32[4,16,20]{2,1,0:T(8,128)S(1)} %shard_map.64.after.refs_1_.refs_3_, ...), custom_call_target="tpu_custom_call" | custom-call | flops 4000000000 | bytes 20000000 | tf_op jit(solution)/shard_map/pallas_call | solution.py:184
  24.2 2.8 %collective-permute-start.6 = (bf16[2,512,256]{2,1,0:T(8,128)(2,1)S(1)}, bf16[2,512,256]{2,1,0:T(8,128)(2,1)S(1)}, u32[]{:S(2)}, u32[]{:S(2)}) collective-permute-start(bf16[2,512,256]{2,1,0:T(8,128)(2,1)S(1)} %get-tuple-element.19.after), channel_id=1, source_target_pairs={{0,3},{1,0},{2,1},{3,2},{4,7},{5,4},{6,5},{7,6},{8,11},{9,8},{10,9... | collective-permute-start | bytes 1572872 | tf_op jit(solution)/shard_map/ppermute | solution.py:144
  27.1 3.7 %shard_map.68 = (bf16[2,512,256]{2,1,0:T(8,128)(2,1)S(1)}, bf16[2,512,256]{2,1,0:T(8,128)(2,1)S(1)}) custom-call(s32[3]{0:T(128)S(1)} %pad_add_fusion.1.at, bf16[8,16,16,2560]{3,2,1,0:T(8,128)(2,1)S(1)} %shard_map.65.green_ref, bf16[2,4,256,2560]{3,2,1,0:T(8,128)(2,1)S(1)} %shard_map.66.aux_ref, bf16[2,512,256]{2,1,0:T(8,128)(2,1)S(1)} %get-tuple-element.19.after, ...), custom_call_target="tpu_custom_call" | custom-call | flops 4000000000 | bytes 20000000 | tf_op jit(solution)/shard_map/pallas_call | solution.py:184
  30.8 2.7 %collective-permute-start.8 = (bf16[2,512,256]{2,1,0:T(8,128)(2,1)S(1)}, bf16[2,512,256]{2,1,0:T(8,128)(2,1)S(1)}, u32[]{:S(2)}, u32[]{:S(2)}) collective-permute-start(bf16[2,512,256]{2,1,0:T(8,128)(2,1)S(1)} %get-tuple-element.20.after), channel_id=1, source_target_pairs={{0,3},{1,0},{2,1},{3,2},{4,7},{5,4},{6,5},{7,6},{8,11},{9,8},{10,9... | collective-permute-start | bytes 1572872 | tf_op jit(solution)/shard_map/ppermute | solution.py:144
  33.6 3.6 %collective-permute-done.6.refs_1_.refs_4_ = bf16[2,512,256]{2,1,0:T(8,128)(2,1)S(1)} collective-permute-done((bf16[2,512,256]{2,1,0:T(8,128)(2,1)S(1)}, bf16[2,512,256]{2,1,0:T(8,128)(2,1)S(1)}, u32[]{:S(2)}, u32[]{:S(2)}) %collective-permute-start.6) | collective-permute-done | bytes 524320 | tf_op jit(solution)/shard_map/ppermute | solution.py:144
  37.1 3.1 %collective-permute-done.7.refs_2_.refs_5_ = bf16[2,512,256]{2,1,0:T(8,128)(2,1)S(1)} collective-permute-done((bf16[2,512,256]{2,1,0:T(8,128)(2,1)S(1)}, bf16[2,512,256]{2,1,0:T(8,128)(2,1)S(1)}, u32[]{:S(2)}, u32[]{:S(2)}) %collective-permute-start.7) | collective-permute-done | bytes 524320 | tf_op jit(solution)/shard_map/ppermute | solution.py:144
  40.3 4.4 %shard_map.69 = (bf16[4,2,128,256]{3,2,1,0:T(8,128)(2,1)S(1)}, bf16[4,2,128,256]{3,2,1,0:T(8,128)(2,1)}) custom-call(s32[3]{0:T(128)S(1)} %pad_add_fusion.1.at, bf16[8,16,16,2560]{3,2,1,0:T(8,128)(2,1)S(1)} %shard_map.65.green_ref, bf16[2,4,256,2560]{3,2,1,0:T(8,128)(2,1)S(1)} %shard_map.66.aux_ref, bf16[2,512,256]{2,1,0:T(8,128)(2,1)S(1)} %get-tuple-element.20.after, ...), custom_call_target="tpu_custom_call" | custom-call | flops 4000000000 | bytes 20000000 | tf_op jit(solution)/shard_map/pallas_call | solution.py:184
  44.9 8.2 %shard_map.70.after.refs_0_.refs_3_ = f32[4,4,2,128,256]{4,3,2,1,0:T(8,128)} custom-call(s32[3]{0:T(128)S(1)} %pad_add_fusion.1.at, bf16[8,16,16,2560]{3,2,1,0:T(8,128)(2,1)S(1)} %shard_map.65.green_ref, bf16[2,4,256,2560]{3,2,1,0:T(8,128)(2,1)S(1)} %shard_map.66.aux_ref, bf16[4,2,128,256]{3,2,1,0:T(8,128)(2,1)S(1)} %get-tuple-element.22.after, ...), custom_call_target="tpu_custom_call" | custom-call | flops 4000000000 | bytes 20000000 | tf_op jit(solution)/shard_map/pallas_call | solution.py:232
  56.5 3.6 %shard_map.71 = (bf16[4,2,128,256]{3,2,1,0:T(8,128)(2,1)S(1)}, bf16[4,2,128,256]{3,2,1,0:T(8,128)(2,1)S(1)}) custom-call(s32[3]{0:T(128)S(1)} %pad_add_fusion.1.at, bf16[8,16,16,2560]{3,2,1,0:T(8,128)(2,1)S(1)} %shard_map.65.green_ref, bf16[2,4,256,2560]{3,2,1,0:T(8,128)(2,1)S(1)} %shard_map.66.aux_ref, f32[4,4,2,128,256]{4,3,2,1,0:T(8,128)S(1)} %copy-done.1, ...), custom_call_target="tpu_custom_call" | custom-call | flops 4000000000 | bytes 20000000 | tf_op jit(solution)/shard_map/pallas_call | solution.py:184
  61.6 6.4 %shard_map.72 = (bf16[4,2,128,256]{3,2,1,0:T(8,128)(2,1)S(1)}, bf16[4,2,128,256]{3,2,1,0:T(8,128)(2,1)}, bf16[4,2,128,256]{3,2,1,0:T(8,128)(2,1)}, bf16[4,2,128,256]{3,2,1,0:T(8,128)(2,1)S(1)}) custom-call(s32[3]{0:T(128)S(1)} %pad_add_fusion.1.at, bf16[8,16,16,2560]{3,2,1,0:T(8,128)(2,1)S(1)} %shard_map.65.green_ref, ...), custom_call_target="tpu_custom_call" | custom-call | flops 1000000 | bytes 100000 | tf_op jit(solution)/shard_map/pallas_call | solution.py:184
  70.3 2.6 %collective-permute-start.10 = (bf16[4,2,128,256]{3,2,1,0:T(8,128)(2,1)}, bf16[4,2,128,256]{3,2,1,0:T(8,128)(2,1)}, u32[]{:S(2)}, u32[]{:S(2)}) collective-permute-start(bf16[4,2,128,256]{3,2,1,0:T(8,128)(2,1)} %get-tuple-element.25), channel_id=1, source_target_pairs={{0,3},{1,0},{2,1},{3,2},{4,7},{5,4},{6,5},{7,6},{8,11},{9,8},{10,9... | collective-permute-start | bytes 1572872 | tf_op jit(solution)/shard_map/ppermute | solution.py:144
  75.3 9.8 %all-to-all-start = ((f32[8,1,128,256]{3,2,1,0:T(8,128)}), f32[8,1,128,256]{3,2,1,0:T(8,128)S(1)}, u32[]{:S(2)}, u32[]{:S(2)}) async-start(f32[8,1,128,256]{3,2,1,0:T(8,128)} %shard_map.73.refs_6_), calls=%async_computation | async-start | bytes 2097152 | tf_op jit(solution)/shard_map/all_to_all | solution.py:261
  85.1 4.7 %collective-permute-done.15.refs_2_ = bf16[4,2,128,256]{3,2,1,0:T(8,128)(2,1)} collective-permute-done((bf16[4,2,128,256]{3,2,1,0:T(8,128)(2,1)S(1)}, bf16[4,2,128,256]{3,2,1,0:T(8,128)(2,1)}, u32[]{:S(2)}, u32[]{:S(2)}) %collective-permute-start.15) | collective-permute-done | bytes 524320 | tf_op jit(solution)/shard_map/ppermute | solution.py:144
  89.8 3.5 %shard_map.74.after = bf16[8,2,128,256]{3,2,1,0:T(8,128)(2,1)} custom-call(f32[4,4,2,128,256]{4,3,2,1,0:T(8,128)} %shard_map.70.after.refs_0_.refs_3_, bf16[4,2,128,256]{3,2,1,0:T(8,128)(2,1)} %collective-permute-done.14.refs_1_, bf16[4,2,128,256]{3,2,1,0:T(8,128)(2,1)} %collective-permute-done.15.refs_2_, ...), custom_call_target="tpu_custom_call" | custom-call | flops 99999997952 | bytes 1000000 | tf_op jit(solution)/shard_map/pallas_call | solution.py:252
  93.3 7.2 %all-to-all-done.got_ref = f32[8,1,128,256]{3,2,1,0:T(8,128)S(1)} async-done(((f32[8,1,128,256]{3,2,1,0:T(8,128)}), f32[8,1,128,256]{3,2,1,0:T(8,128)S(1)}, u32[]{:S(2)}, u32[]{:S(2)}) %all-to-all-start) | async-done | bytes 1048608 | tf_op jit(solution)/shard_map/all_to_all | solution.py:261
  100.5 7.5 %all-to-all-start.2 = ((bf16[8,2,128,256]{3,2,1,0:T(8,128)(2,1)}), bf16[8,2,128,256]{3,2,1,0:T(8,128)(2,1)S(1)}, u32[]{:S(2)}, u32[]{:S(2)}) async-start(bf16[8,2,128,256]{3,2,1,0:T(8,128)(2,1)} %shard_map.74.after), calls=%async_computation.2 | async-start | bytes 2097152 | tf_op jit(solution)/shard_map/all_to_all | solution.py:261
  112.0 11.3 %all-to-all-done.2.got_ref = bf16[8,2,128,256]{3,2,1,0:T(8,128)(2,1)S(1)} async-done(((bf16[8,2,128,256]{3,2,1,0:T(8,128)(2,1)}), bf16[8,2,128,256]{3,2,1,0:T(8,128)(2,1)S(1)}, u32[]{:S(2)}, u32[]{:S(2)}) %all-to-all-start.2) | async-done | bytes 1048608 | tf_op jit(solution)/shard_map/all_to_all | solution.py:261
  123.3 3.5 %all-to-all-start.1 = ((bf16[8,1,128,256]{3,2,1,0:T(8,128)(2,1)}), bf16[8,1,128,256]{3,2,1,0:T(8,128)(2,1)S(1)}, u32[]{:S(2)}, u32[]{:S(2)}) async-start(bf16[8,1,128,256]{3,2,1,0:T(8,128)(2,1)} %shard_map.76.after), calls=%async_computation.1 | async-start | bytes 1048576 | tf_op jit(solution)/shard_map/all_to_all | solution.py:261
  131.0 5.4 %all-to-all-done.1.got_ref = bf16[8,1,128,256]{3,2,1,0:T(8,128)(2,1)S(1)} async-done(((bf16[8,1,128,256]{3,2,1,0:T(8,128)(2,1)}), bf16[8,1,128,256]{3,2,1,0:T(8,128)(2,1)S(1)}, u32[]{:S(2)}, u32[]{:S(2)}) %all-to-all-start.1) | async-done | bytes 524320 | tf_op jit(solution)/shard_map/all_to_all | solution.py:261
  136.5 5.8 %collective-permute-done.18.refs_1_ = f32[512,256]{1,0:T(8,128)S(1)} collective-permute-done((f32[512,256]{1,0:T(8,128)S(1)}, f32[512,256]{1,0:T(8,128)S(1)}, u32[]{:S(2)}, u32[]{:S(2)}) %collective-permute-start.18) | collective-permute-done | bytes 524320 | tf_op jit(solution)/shard_map/ppermute | solution.py:144
  142.9 3.8 %shard_map.79 = f32[3840,256]{1,0:T(8,128)} custom-call(f32[240,128]{1,0:T(8,128)S(1)} %convolution_bitcast_fusion.w_ref, f32[120,256]{1,0:T(8,128)S(1)} %copy-done.4, f32[512,256]{1,0:T(8,128)S(1)} %shard_map.78.refs_0_, f32[512,256]{1,0:T(8,128)S(1)} %collective-permute-done.18.refs_1_, f32[512,256]{1,0:T(8,128)S(1)} %collective-permute-done.19.refs_2_, ...), custom_call_target="tpu_custom_call" | custom-call | tf_op jit(solution)/shard_map/pallas_call | solution.py:296
  (63 shorter events, 28.2 us)
Async XLA Ops:
  0.0 3.1 %collective-permute-start = (s32[16,20]{1,0:T(8,128)}, s32[16,20]{1,0:T(8,128)S(1)}, u32[]{:S(2)}, u32[]{:S(2)}) collective-permute-start(s32[16,20]{1,0:T(8,128)} %a.1), channel_id=1, source_target_pairs={{0,8},{8,0},{16,24},{24,16},{1,9},{9,1},{17,25},{25,17},{2,10},{10... | collective-permute-start | bytes 3848 | tf_op jit(solution)/shard_map/ppermute | solution.py:169
  1.4 2.7 %collective-permute-start.1 = (s32[16,20]{1,0:T(8,128)}, s32[16,20]{1,0:T(8,128)S(1)}, u32[]{:S(2)}, u32[]{:S(2)}) collective-permute-start(s32[16,20]{1,0:T(8,128)} %a.1), channel_id=1, source_target_pairs={{0,16},{8,24},{16,0},{24,8},{1,17},{9,25},{17,1},{25,9},{2,18},{10... | collective-permute-start | bytes 3848 | tf_op jit(solution)/shard_map/ppermute | solution.py:169
  2.7 3.3 %collective-permute-start.2 = (s32[16,20]{1,0:T(8,128)}, s32[16,20]{1,0:T(8,128)S(1)}, u32[]{:S(2)}, u32[]{:S(2)}) collective-permute-start(s32[16,20]{1,0:T(8,128)} %a.1), channel_id=1, source_target_pairs={{0,24},{8,16},{16,8},{24,0},{1,25},{9,17},{17,9},{25,1},{2,26},{10... | collective-permute-start | bytes 3848 | tf_op jit(solution)/shard_map/ppermute | solution.py:169
  6.7 13.8 %collective-permute-start.4 = (s32[4,16,20]{2,1,0:T(8,128)S(1)}, s32[4,16,20]{2,1,0:T(8,128)S(1)}, u32[]{:S(2)}, u32[]{:S(2)}) collective-permute-start(s32[4,16,20]{2,1,0:T(8,128)S(1)} %shard_map.64.after.refs_1_.refs_3_), channel_id=1, source_target_pairs={{0,96},{32,0},{64,32},{96,64},{1,97},{33,1},{65,33},{97,65},{2,98}... | collective-permute-start | bytes 15368 | tf_op jit(solution)/shard_map/ppermute | solution.py:144
  10.5 10.0 %collective-permute-start.5 = (s32[4,16,20]{2,1,0:T(8,128)S(1)}, s32[4,16,20]{2,1,0:T(8,128)S(1)}, u32[]{:S(2)}, u32[]{:S(2)}) collective-permute-start(s32[4,16,20]{2,1,0:T(8,128)S(1)} %shard_map.64.after.refs_1_.refs_3_), channel_id=1, source_target_pairs={{0,32},{32,64},{64,96},{96,0},{1,33},{33,65},{65,97},{97,1},{2,34}... | collective-permute-start | bytes 15368 | tf_op jit(solution)/shard_map/ppermute | solution.py:144
  10.5 10.0 %collective-permute-start.3 = (s32[4,16,20]{2,1,0:T(8,128)S(1)}, s32[4,16,20]{2,1,0:T(8,128)S(1)}, u32[]{:S(2)}, u32[]{:S(2)}) collective-permute-start(s32[4,16,20]{2,1,0:T(8,128)S(1)} %shard_map.64.after.refs_1_.refs_3_), channel_id=1, source_target_pairs={{0,64},{32,96},{64,0},{96,32},{1,65},{33,97},{65,1},{97,33},{2,66}... | collective-permute-start | bytes 15368 | tf_op jit(solution)/shard_map/ppermute | solution.py:144
  24.2 12.9 %collective-permute-start.6 = (bf16[2,512,256]{2,1,0:T(8,128)(2,1)S(1)}, bf16[2,512,256]{2,1,0:T(8,128)(2,1)S(1)}, u32[]{:S(2)}, u32[]{:S(2)}) collective-permute-start(bf16[2,512,256]{2,1,0:T(8,128)(2,1)S(1)} %get-tuple-element.19.after), channel_id=1, source_target_pairs={{0,3},{1,0},{2,1},{3,2},{4,7},{5,4},{6,5},{7,6},{8,11},{9,8},{10,9... | collective-permute-start | bytes 1572872 | tf_op jit(solution)/shard_map/ppermute | solution.py:144
  27.1 13.2 %collective-permute-start.7 = (bf16[2,512,256]{2,1,0:T(8,128)(2,1)S(1)}, bf16[2,512,256]{2,1,0:T(8,128)(2,1)S(1)}, u32[]{:S(2)}, u32[]{:S(2)}) collective-permute-start(bf16[2,512,256]{2,1,0:T(8,128)(2,1)S(1)} %get-tuple-element.21), channel_id=1, source_target_pairs={{0,1},{1,2},{2,3},{3,0},{4,5},{5,6},{6,7},{7,4},{8,9},{9,10},{10,1... | collective-permute-start | bytes 1572872 | tf_op jit(solution)/shard_map/ppermute | solution.py:144
  30.8 23.5 %collective-permute-start.8 = (bf16[2,512,256]{2,1,0:T(8,128)(2,1)S(1)}, bf16[2,512,256]{2,1,0:T(8,128)(2,1)S(1)}, u32[]{:S(2)}, u32[]{:S(2)}) collective-permute-start(bf16[2,512,256]{2,1,0:T(8,128)(2,1)S(1)} %get-tuple-element.20.after), channel_id=1, source_target_pairs={{0,3},{1,0},{2,1},{3,2},{4,7},{5,4},{6,5},{7,6},{8,11},{9,8},{10,9... | collective-permute-start | bytes 1572872 | tf_op jit(solution)/shard_map/ppermute | solution.py:144
  33.5 20.8 %collective-permute-start.9 = (bf16[2,512,256]{2,1,0:T(8,128)(2,1)S(1)}, bf16[2,512,256]{2,1,0:T(8,128)(2,1)S(1)}, u32[]{:S(2)}, u32[]{:S(2)}) collective-permute-start(bf16[2,512,256]{2,1,0:T(8,128)(2,1)S(1)} %get-tuple-element.23), channel_id=1, source_target_pairs={{0,1},{1,2},{2,3},{3,0},{4,5},{5,6},{6,7},{7,4},{8,9},{9,10},{10,1... | collective-permute-start | bytes 1572872 | tf_op jit(solution)/shard_map/ppermute | solution.py:144
  44.6 25.0 %collective-permute-start.12 = (bf16[4,2,128,256]{3,2,1,0:T(8,128)(2,1)S(1)}, bf16[4,2,128,256]{3,2,1,0:T(8,128)(2,1)S(1)}, u32[]{:S(2)}, u32[]{:S(2)}) collective-permute-start(bf16[4,2,128,256]{3,2,1,0:T(8,128)(2,1)S(1)} %get-tuple-element.22.after), channel_id=1, source_target_pairs={{0,3},{1,0},{2,1},{3,2},{4,7},{5,4},{6,5},{7,6},{8,11},{9,8},{10,9... | collective-permute-start | bytes 1572872 | tf_op jit(solution)/shard_map/ppermute | solution.py:144
  53.1 17.2 %collective-permute-start.13 = (bf16[4,2,128,256]{3,2,1,0:T(8,128)(2,1)}, bf16[4,2,128,256]{3,2,1,0:T(8,128)(2,1)S(1)}, u32[]{:S(2)}, u32[]{:S(2)}) collective-permute-start(bf16[4,2,128,256]{3,2,1,0:T(8,128)(2,1)} %get-tuple-element.27), channel_id=1, source_target_pairs={{0,1},{1,2},{2,3},{3,0},{4,5},{5,6},{6,7},{7,4},{8,9},{9,10},{10,1... | collective-permute-start | bytes 1572872 | tf_op jit(solution)/shard_map/ppermute | solution.py:144
  60.1 25.0 %collective-permute-start.14 = (bf16[4,2,128,256]{3,2,1,0:T(8,128)(2,1)S(1)}, bf16[4,2,128,256]{3,2,1,0:T(8,128)(2,1)}, u32[]{:S(2)}, u32[]{:S(2)}) collective-permute-start(bf16[4,2,128,256]{3,2,1,0:T(8,128)(2,1)S(1)} %get-tuple-element.24.after), channel_id=1, source_target_pairs={{0,3},{1,0},{2,1},{3,2},{4,7},{5,4},{6,5},{7,6},{8,11},{9,8},{10,9... | collective-permute-start | bytes 1572872 | tf_op jit(solution)/shard_map/ppermute | solution.py:144
  68.1 17.0 %collective-permute-start.16 = (bf16[4,2,128,256]{3,2,1,0:T(8,128)(2,1)S(1)}, bf16[4,2,128,256]{3,2,1,0:T(8,128)(2,1)}, u32[]{:S(2)}, u32[]{:S(2)}) collective-permute-start(bf16[4,2,128,256]{3,2,1,0:T(8,128)(2,1)S(1)} %get-tuple-element.28.refs_3_), channel_id=1, source_target_pairs={{0,3},{1,0},{2,1},{3,2},{4,7},{5,4},{6,5},{7,6},{8,11},{9,8},{10,9... | collective-permute-start | bytes 1572872 | tf_op jit(solution)/shard_map/ppermute | solution.py:144
  68.2 16.9 %collective-permute-start.17 = (bf16[4,2,128,256]{3,2,1,0:T(8,128)(2,1)}, bf16[4,2,128,256]{3,2,1,0:T(8,128)(2,1)}, u32[]{:S(2)}, u32[]{:S(2)}) collective-permute-start(bf16[4,2,128,256]{3,2,1,0:T(8,128)(2,1)} %get-tuple-element.30), channel_id=1, source_target_pairs={{0,1},{1,2},{2,3},{3,0},{4,5},{5,6},{6,7},{7,4},{8,9},{9,10},{10,1... | collective-permute-start | bytes 1572872 | tf_op jit(solution)/shard_map/ppermute | solution.py:144
  69.6 20.2 %collective-permute-start.15 = (bf16[4,2,128,256]{3,2,1,0:T(8,128)(2,1)S(1)}, bf16[4,2,128,256]{3,2,1,0:T(8,128)(2,1)}, u32[]{:S(2)}, u32[]{:S(2)}) collective-permute-start(bf16[4,2,128,256]{3,2,1,0:T(8,128)(2,1)S(1)} %get-tuple-element.29), channel_id=1, source_target_pairs={{0,1},{1,2},{2,3},{3,0},{4,5},{5,6},{6,7},{7,4},{8,9},{9,10},{10,1... | collective-permute-start | bytes 1572872 | tf_op jit(solution)/shard_map/ppermute | solution.py:144
  70.3 39.2 %collective-permute-start.10 = (bf16[4,2,128,256]{3,2,1,0:T(8,128)(2,1)}, bf16[4,2,128,256]{3,2,1,0:T(8,128)(2,1)}, u32[]{:S(2)}, u32[]{:S(2)}) collective-permute-start(bf16[4,2,128,256]{3,2,1,0:T(8,128)(2,1)} %get-tuple-element.25), channel_id=1, source_target_pairs={{0,3},{1,0},{2,1},{3,2},{4,7},{5,4},{6,5},{7,6},{8,11},{9,8},{10,9... | collective-permute-start | bytes 1572872 | tf_op jit(solution)/shard_map/ppermute | solution.py:144
  75.3 25.2 %all-to-all-start = ((f32[8,1,128,256]{3,2,1,0:T(8,128)}), f32[8,1,128,256]{3,2,1,0:T(8,128)S(1)}, u32[]{:S(2)}, u32[]{:S(2)}) async-start(f32[8,1,128,256]{3,2,1,0:T(8,128)} %shard_map.73.refs_6_), calls=%async_computation | async-start | bytes 2097152 | tf_op jit(solution)/shard_map/all_to_all | solution.py:261
  85.1 24.4 %collective-permute-start.11 = (bf16[4,2,128,256]{3,2,1,0:T(8,128)(2,1)S(1)}, bf16[4,2,128,256]{3,2,1,0:T(8,128)(2,1)}, u32[]{:S(2)}, u32[]{:S(2)}) collective-permute-start(bf16[4,2,128,256]{3,2,1,0:T(8,128)(2,1)S(1)} %get-tuple-element.26), channel_id=1, source_target_pairs={{0,1},{1,2},{2,3},{3,0},{4,5},{5,6},{6,7},{7,4},{8,9},{9,10},{10,1... | collective-permute-start | bytes 1572872 | tf_op jit(solution)/shard_map/ppermute | solution.py:144
  100.5 22.8 %all-to-all-start.2 = ((bf16[8,2,128,256]{3,2,1,0:T(8,128)(2,1)}), bf16[8,2,128,256]{3,2,1,0:T(8,128)(2,1)S(1)}, u32[]{:S(2)}, u32[]{:S(2)}) async-start(bf16[8,2,128,256]{3,2,1,0:T(8,128)(2,1)} %shard_map.74.after), calls=%async_computation.2 | async-start | bytes 2097152 | tf_op jit(solution)/shard_map/all_to_all | solution.py:261
  108.1 34.8 %collective-permute-start.19 = (f32[512,256]{1,0:T(8,128)S(1)}, f32[512,256]{1,0:T(8,128)S(1)}, u32[]{:S(2)}, u32[]{:S(2)}) collective-permute-start(f32[512,256]{1,0:T(8,128)S(1)} %shard_map.75.refs_3_), channel_id=1, source_target_pairs={{0,64},{32,96},{64,0},{96,32},{1,65},{33,97},{65,1},{97,33},{2,66}... | collective-permute-start | bytes 1572872 | tf_op jit(solution)/shard_map/ppermute | solution.py:144
  123.3 13.2 %all-to-all-start.1 = ((bf16[8,1,128,256]{3,2,1,0:T(8,128)(2,1)}), bf16[8,1,128,256]{3,2,1,0:T(8,128)(2,1)S(1)}, u32[]{:S(2)}, u32[]{:S(2)}) async-start(bf16[8,1,128,256]{3,2,1,0:T(8,128)(2,1)} %shard_map.76.after), calls=%async_computation.1 | async-start | bytes 1048576 | tf_op jit(solution)/shard_map/all_to_all | solution.py:261
  127.6 14.7 %collective-permute-start.18 = (f32[512,256]{1,0:T(8,128)S(1)}, f32[512,256]{1,0:T(8,128)S(1)}, u32[]{:S(2)}, u32[]{:S(2)}) collective-permute-start(f32[512,256]{1,0:T(8,128)S(1)} %get-tuple-element.31.after), channel_id=1, source_target_pairs={{0,32},{32,64},{64,96},{96,0},{1,33},{33,65},{65,97},{97,1},{2,34}... | collective-permute-start | bytes 1572872 | tf_op jit(solution)/shard_map/ppermute | solution.py:144
  129.5 13.4 %collective-permute-start.20 = (f32[512,256]{1,0:T(8,128)}, f32[512,256]{1,0:T(8,128)S(1)}, u32[]{:S(2)}, u32[]{:S(2)}) collective-permute-start(f32[512,256]{1,0:T(8,128)} %get-tuple-element.32), channel_id=1, source_target_pairs={{0,96},{32,0},{64,32},{96,64},{1,97},{33,1},{65,33},{97,65},{2,98}... | collective-permute-start | bytes 1572872 | tf_op jit(solution)/shard_map/ppermute | solution.py:144
  (8 other events, 221.0 us)

commit v4 on v3

--- a/solution.py
+++ b/solution.py
@@ -168,6 +168,7 @@
         pairs = [(i * 2 + j, (i ^ e) * 2 + (j ^ f)) for i in (0, 1) for j in (0, 1)]
         return lax.ppermute(v, ("xl", "c"), pairs)
 
+    aux = stage(aux_factors.reshape(2, ny, width, cols), at)
     quad = pl.pallas_call(
         join_kernel,
         out_shape=shape((4, height, blocks), pair_mask.dtype),
@@ -175,7 +176,6 @@
         cost_estimate=LITTLE,
     )(pair_mask, swap(pair_mask, 0, 1), swap(pair_mask, 1, 0), swap(pair_mask, 1, 1))
     marks = [quad if d == 0 else shift(quad, "z", -d) for d in range(nz)]
-    aux = stage(aux_factors.reshape(2, ny, width, cols), quad)
     green = stage(green_tau.reshape(times, n_rows // height, height, cols), quad)
 
     def call(kernel, after, extra, extra_specs, out_shape, cost=COST):
@@ -282,7 +282,7 @@
     last = mine = own(last)
     mine = pltpu.with_memory_space_constraint(mine, pltpu.HBM)
     last = near((1,), last)
-    last = near((3, 0), last, cost=LITTLE)
+    last = near((3, 0), last, step2[2], LITTLE)
     last = cross((2,), last, f32)
     last = cross((1, 3), last, bf16, LONG)
     last = gather((2,), last)

time: 147 us -> 137 us (0.932)
  local copies, waits for them, and re-layouts: 10.3 us -> 6.28 us
  waiting for transfers between devices: 44.6 us -> 41.1 us
  starting transfers between devices: 45.8 us -> 43.7 us
    unnamed x16, local copies, waits for them, and re-layouts: 10.2 us -> 6.19 us
    all_to_all x3, starting transfers between devices: 20.8 us -> 17.6 us  [cross(): lax.all_to_all(total, ('xl', 'c', 'xh'), split_axis=0, concat_axis=0, til...]
    ppermute x3, waiting for transfers between devices: 2.88 us -> 0.01 us  [swap(): return lax.ppermute(v, ('xl', 'c'), pairs)]
    ppermute x18, waiting for transfers between devices: 17.8 us -> 15.8 us  [shift(): return lax.ppermute(v, axis, [(i, (i + by) % n) for i in range(n)])]
  transfers between devices with their start and end apart: 24 -> 24, of which waited for: 10 -> 9; matrix products, arithmetic and copies ran while one was open for 1% -> 1% of each run, Pallas kernels for 25% -> 27%
where the time goes in v4:
time: 137 us
  Pallas kernels  44.4 us (32%)
  starting transfers between devices  43.7 us (32%)
  waiting for transfers between devices  41.1 us (30%)
  local copies, waits for them, and re-layouts  6.28 us (5%)
    all_to_all x3, waiting for transfers between devices, cross(): lax.all_to_all(total, ('xl', 'c', 'xh'), split_axis=0, concat_axis=0, til...  25.3 us
    ppermute x18, starting transfers between devices, shift(): return lax.ppermute(v, axis, [(i, (i + by) % n) for i in range(n)])  23 us
    pallas_call x5, Pallas kernels, call(): pl.pallas_call(kernel, grid_spec=pltpu.PrefetchScalarGridSpec(num_scalar_...  21.9 us
    all_to_all x3, starting transfers between devices, cross(): lax.all_to_all(total, ('xl', 'c', 'xh'), split_axis=0, concat_axis=0, til...  17.6 us
    ppermute x18, waiting for transfers between devices, shift(): return lax.ppermute(v, axis, [(i, (i + by) % n) for i in range(n)])  15.8 us
    pallas_call x1, Pallas kernels, own(): pl.pallas_call(own_kernel, grid_spec=pltpu.PrefetchScalarGridSpec(num_sca...  8.2 us
    pallas_call x3, Pallas kernels, cross(): pl.pallas_call(functools.partial(sum_kernel, n), grid=(1,), in_specs=[v f...  8.13 us
    unnamed x16, local copies, waits for them, and re-layouts  6.19 us
  transfers between devices with their start and end apart: 24, of which 9 were waited for; matrix products, arithmetic and copies ran while one was open for 1% of the time, Pallas kernels for 27%

profile of v4, /device:TPU:1, one launch (start us, length us, event | category | flops | bytes accessed | tf_op | source)
XLA Modules:
  0.0 137.0 jit_solution(1996953336262198262)
XLA Ops:
  3.1 4.0 %copy-done.2 = bf16[2048,2560]{1,0:T(8,128)(2,1)S(1)} copy-done((bf16[2048,2560]{1,0:T(8,128)(2,1)S(1)}, bf16[2048,2560]{1,0:T(8,128)(2,1)}, u32[]{:S(2)}) %copy-start.2) | copy-done | bytes 10485784
  7.9 4.0 %collective-permute-start.4 = (s32[4,16,20]{2,1,0:T(8,128)S(1)}, s32[4,16,20]{2,1,0:T(8,128)S(1)}, u32[]{:S(2)}, u32[]{:S(2)}) collective-permute-start(s32[4,16,20]{2,1,0:T(8,128)S(1)} %shard_map.64.after.refs_1_.refs_3_), channel_id=1, source_target_pairs={{0,96},{32,0},{64,32},{96,64},{1,97},{33,1},{65,33},{97,65},{2,98}... | collective-permute-start | bytes 15368 | tf_op jit(solution)/shard_map/ppermute | solution.py:144
  16.2 3.7 %shard_map.67 = (bf16[2,512,256]{2,1,0:T(8,128)(2,1)S(1)}, bf16[2,512,256]{2,1,0:T(8,128)(2,1)S(1)}) custom-call(s32[3]{0:T(128)S(1)} %pad_add_fusion.1.after.at, bf16[8,16,16,2560]{3,2,1,0:T(8,128)(2,1)S(1)} %shard_map.65.green_ref, bf16[2,4,256,2560]{3,2,1,0:T(8,128)(2,1)S(1)} %shard_map.66.aux_ref, s32[4,16,20]{2,1,0:T(8,128)S(1)} %shard_map.64.after.refs_1_.refs_3_, ...), custom_call_target="tpu_custom_call" | custom-call | flops 4000000000 | bytes 20000000 | tf_op jit(solution)/shard_map/pallas_call | solution.py:184
  19.9 2.8 %collective-permute-start.6 = (bf16[2,512,256]{2,1,0:T(8,128)(2,1)S(1)}, bf16[2,512,256]{2,1,0:T(8,128)(2,1)S(1)}, u32[]{:S(2)}, u32[]{:S(2)}) collective-permute-start(bf16[2,512,256]{2,1,0:T(8,128)(2,1)S(1)} %get-tuple-element.19.after), channel_id=1, source_target_pairs={{0,3},{1,0},{2,1},{3,2},{4,7},{5,4},{6,5},{7,6},{8,11},{9,8},{10,9... | collective-permute-start | bytes 1572872 | tf_op jit(solution)/shard_map/ppermute | solution.py:144
  22.7 3.7 %shard_map.68 = (bf16[2,512,256]{2,1,0:T(8,128)(2,1)S(1)}, bf16[2,512,256]{2,1,0:T(8,128)(2,1)S(1)}) custom-call(s32[3]{0:T(128)S(1)} %pad_add_fusion.1.after.at, bf16[8,16,16,2560]{3,2,1,0:T(8,128)(2,1)S(1)} %shard_map.65.green_ref, bf16[2,4,256,2560]{3,2,1,0:T(8,128)(2,1)S(1)} %shard_map.66.aux_ref, bf16[2,512,256]{2,1,0:T(8,128)(2,1)S(1)} %get-tuple-element.19.after, ...), custom_call_target="tpu_custom_call" | custom-call | flops 4000000000 | bytes 20000000 | tf_op jit(solution)/shard_map/pallas_call | solution.py:184
  26.5 2.7 %collective-permute-start.8 = (bf16[2,512,256]{2,1,0:T(8,128)(2,1)S(1)}, bf16[2,512,256]{2,1,0:T(8,128)(2,1)S(1)}, u32[]{:S(2)}, u32[]{:S(2)}) collective-permute-start(bf16[2,512,256]{2,1,0:T(8,128)(2,1)S(1)} %get-tuple-element.20.after), channel_id=1, source_target_pairs={{0,3},{1,0},{2,1},{3,2},{4,7},{5,4},{6,5},{7,6},{8,11},{9,8},{10,9... | collective-permute-start | bytes 1572872 | tf_op jit(solution)/shard_map/ppermute | solution.py:144
  29.2 3.1 %collective-permute-done.6.refs_1_.refs_4_ = bf16[2,512,256]{2,1,0:T(8,128)(2,1)S(1)} collective-permute-done((bf16[2,512,256]{2,1,0:T(8,128)(2,1)S(1)}, bf16[2,512,256]{2,1,0:T(8,128)(2,1)S(1)}, u32[]{:S(2)}, u32[]{:S(2)}) %collective-permute-start.6) | collective-permute-done | bytes 524320 | tf_op jit(solution)/shard_map/ppermute | solution.py:144
  32.3 3.1 %collective-permute-done.7.refs_2_.refs_5_ = bf16[2,512,256]{2,1,0:T(8,128)(2,1)S(1)} collective-permute-done((bf16[2,512,256]{2,1,0:T(8,128)(2,1)S(1)}, bf16[2,512,256]{2,1,0:T(8,128)(2,1)S(1)}, u32[]{:S(2)}, u32[]{:S(2)}) %collective-permute-start.7) | collective-permute-done | bytes 524320 | tf_op jit(solution)/shard_map/ppermute | solution.py:144
  35.5 3.6 %shard_map.69 = (bf16[4,2,128,256]{3,2,1,0:T(8,128)(2,1)S(1)}, bf16[4,2,128,256]{3,2,1,0:T(8,128)(2,1)S(1)}) custom-call(s32[3]{0:T(128)S(1)} %pad_add_fusion.1.after.at, bf16[8,16,16,2560]{3,2,1,0:T(8,128)(2,1)S(1)} %shard_map.65.green_ref, bf16[2,4,256,2560]{3,2,1,0:T(8,128)(2,1)S(1)} %shard_map.66.aux_ref, ...), custom_call_target="tpu_custom_call" | custom-call | flops 4000000000 | bytes 20000000 | tf_op jit(solution)/shard_map/pallas_call | solution.py:184
  40.6 8.2 %shard_map.70.after.refs_0_.refs_3_ = f32[4,4,2,128,256]{4,3,2,1,0:T(8,128)} custom-call(s32[3]{0:T(128)S(1)} %pad_add_fusion.1.after.at, bf16[8,16,16,2560]{3,2,1,0:T(8,128)(2,1)S(1)} %shard_map.65.green_ref, bf16[2,4,256,2560]{3,2,1,0:T(8,128)(2,1)S(1)} %shard_map.66.aux_ref, bf16[4,2,128,256]{3,2,1,0:T(8,128)(2,1)S(1)} %get-tuple-element.22.after, ...), custom_call_target="tpu_custom_call" | custom-call | flops 4000000000 | bytes 20000000 | tf_op jit(solution)/shard_map/pallas_call | solution.py:232
  51.0 4.4 %shard_map.71 = (bf16[4,2,128,256]{3,2,1,0:T(8,128)(2,1)S(1)}, bf16[4,2,128,256]{3,2,1,0:T(8,128)(2,1)}) custom-call(s32[3]{0:T(128)S(1)} %pad_add_fusion.1.after.at, bf16[8,16,16,2560]{3,2,1,0:T(8,128)(2,1)S(1)} %shard_map.65.green_ref, bf16[2,4,256,2560]{3,2,1,0:T(8,128)(2,1)S(1)} %shard_map.66.aux_ref, f32[4,4,2,128,256]{4,3,2,1,0:T(8,128)S(1)} %copy-done.1, ...), custom_call_target="tpu_custom_call" | custom-call | flops 4000000000 | bytes 20000000 | tf_op jit(solution)/shard_map/pallas_call | solution.py:184
  57.9 6.4 %shard_map.72 = (bf16[4,2,128,256]{3,2,1,0:T(8,128)(2,1)S(1)}, bf16[4,2,128,256]{3,2,1,0:T(8,128)(2,1)}, bf16[4,2,128,256]{3,2,1,0:T(8,128)(2,1)}, bf16[4,2,128,256]{3,2,1,0:T(8,128)(2,1)S(1)}) custom-call(s32[3]{0:T(128)S(1)} %pad_add_fusion.1.after.at, bf16[8,16,16,2560]{3,2,1,0:T(8,128)(2,1)S(1)} %shard_map.65.green_ref, ...), custom_call_target="tpu_custom_call" | custom-call | flops 1000000 | bytes 100000 | tf_op jit(solution)/shard_map/pallas_call | solution.py:184
  69.0 10.6 %all-to-all-start = ((f32[8,1,128,256]{3,2,1,0:T(8,128)}), f32[8,1,128,256]{3,2,1,0:T(8,128)S(1)}, u32[]{:S(2)}, u32[]{:S(2)}) async-start(f32[8,1,128,256]{3,2,1,0:T(8,128)} %shard_map.73.refs_6_), calls=%async_computation | async-start | bytes 2097152 | tf_op jit(solution)/shard_map/all_to_all | solution.py:261
  79.6 3.0 %collective-permute-start.12 = (bf16[4,2,128,256]{3,2,1,0:T(8,128)(2,1)}, bf16[4,2,128,256]{3,2,1,0:T(8,128)(2,1)}, u32[]{:S(2)}, u32[]{:S(2)}) collective-permute-start(bf16[4,2,128,256]{3,2,1,0:T(8,128)(2,1)} %get-tuple-element.26), channel_id=1, source_target_pairs={{0,3},{1,0},{2,1},{3,2},{4,7},{5,4},{6,5},{7,6},{8,11},{9,8},{10,9... | collective-permute-start | bytes 1572872 | tf_op jit(solution)/shard_map/ppermute | solution.py:144
  82.6 3.3 %shard_map.74.after = bf16[8,2,128,256]{3,2,1,0:T(8,128)(2,1)} custom-call(f32[4,4,2,128,256]{4,3,2,1,0:T(8,128)} %shard_map.70.after.refs_0_.refs_3_, bf16[4,2,128,256]{3,2,1,0:T(8,128)(2,1)S(1)} %collective-permute-done.14.refs_1_, bf16[4,2,128,256]{3,2,1,0:T(8,128)(2,1)} %collective-permute-done.15.refs_2_, ...), custom_call_target="tpu_custom_call" | custom-call | flops 99999997952 | bytes 1000000 | tf_op jit(solution)/shard_map/pallas_call | solution.py:252
  85.9 9.1 %all-to-all-done.got_ref = f32[8,1,128,256]{3,2,1,0:T(8,128)S(1)} async-done(((f32[8,1,128,256]{3,2,1,0:T(8,128)}), f32[8,1,128,256]{3,2,1,0:T(8,128)S(1)}, u32[]{:S(2)}, u32[]{:S(2)}) %all-to-all-start) | async-done | bytes 1048608 | tf_op jit(solution)/shard_map/all_to_all | solution.py:261
  95.0 3.5 %all-to-all-start.2 = ((bf16[8,2,128,256]{3,2,1,0:T(8,128)(2,1)}), bf16[8,2,128,256]{3,2,1,0:T(8,128)(2,1)S(1)}, u32[]{:S(2)}, u32[]{:S(2)}) async-start(bf16[8,2,128,256]{3,2,1,0:T(8,128)(2,1)} %shard_map.74.after), calls=%async_computation.2 | async-start | bytes 2097152 | tf_op jit(solution)/shard_map/all_to_all | solution.py:261
  100.2 2.5 %shard_map.76.after = bf16[8,1,128,256]{3,2,1,0:T(8,128)(2,1)} custom-call(f32[4,4,2,128,256]{4,3,2,1,0:T(8,128)} %shard_map.70.after.refs_0_.refs_3_, bf16[4,2,128,256]{3,2,1,0:T(8,128)(2,1)} %collective-permute-done.12.refs_1_, bf16[4,2,128,256]{3,2,1,0:T(8,128)(2,1)} %collective-permute-done.13.refs_2_, f32[512,256]{1,0:T(8,128)S(1)} %shard_map.75.refs_3_), custom_call_target="tpu_custom_call" | custom-call | flops 99999997952 | bytes 1000000 | tf_op jit(solution)/shard_map/pallas_call | solution.py:252
  102.7 11.0 %all-to-all-done.2.got_ref = bf16[8,2,128,256]{3,2,1,0:T(8,128)(2,1)S(1)} async-done(((bf16[8,2,128,256]{3,2,1,0:T(8,128)(2,1)}), bf16[8,2,128,256]{3,2,1,0:T(8,128)(2,1)S(1)}, u32[]{:S(2)}, u32[]{:S(2)}) %all-to-all-start.2) | async-done | bytes 1048608 | tf_op jit(solution)/shard_map/all_to_all | solution.py:261
  113.7 3.5 %all-to-all-start.1 = ((bf16[8,1,128,256]{3,2,1,0:T(8,128)(2,1)}), bf16[8,1,128,256]{3,2,1,0:T(8,128)(2,1)S(1)}, u32[]{:S(2)}, u32[]{:S(2)}) async-start(bf16[8,1,128,256]{3,2,1,0:T(8,128)(2,1)} %shard_map.76.after), calls=%async_computation.1 | async-start | bytes 1048576 | tf_op jit(solution)/shard_map/all_to_all | solution.py:261
  118.3 2.7 %collective-permute-start.20 = (f32[512,256]{1,0:T(8,128)}, f32[512,256]{1,0:T(8,128)S(1)}, u32[]{:S(2)}, u32[]{:S(2)}) collective-permute-start(f32[512,256]{1,0:T(8,128)} %get-tuple-element.32), channel_id=1, source_target_pairs={{0,96},{32,0},{64,32},{96,64},{1,97},{33,1},{65,33},{97,65},{2,98}... | collective-permute-start | bytes 1572872 | tf_op jit(solution)/shard_map/ppermute | solution.py:144
  121.8 5.2 %all-to-all-done.1.got_ref = bf16[8,1,128,256]{3,2,1,0:T(8,128)(2,1)S(1)} async-done(((bf16[8,1,128,256]{3,2,1,0:T(8,128)(2,1)}), bf16[8,1,128,256]{3,2,1,0:T(8,128)(2,1)S(1)}, u32[]{:S(2)}, u32[]{:S(2)}) %all-to-all-start.1) | async-done | bytes 524320 | tf_op jit(solution)/shard_map/all_to_all | solution.py:261
  127.0 6.2 %collective-permute-done.18.refs_1_ = f32[512,256]{1,0:T(8,128)S(1)} collective-permute-done((f32[512,256]{1,0:T(8,128)S(1)}, f32[512,256]{1,0:T(8,128)S(1)}, u32[]{:S(2)}, u32[]{:S(2)}) %collective-permute-start.18) | collective-permute-done | bytes 524320 | tf_op jit(solution)/shard_map/ppermute | solution.py:144
  133.2 3.8 %shard_map.79 = f32[3840,256]{1,0:T(8,128)} custom-call(f32[240,128]{1,0:T(8,128)S(1)} %convolution_bitcast_fusion.w_ref, f32[120,256]{1,0:T(8,128)S(1)} %copy-done.4, f32[512,256]{1,0:T(8,128)S(1)} %shard_map.78.refs_0_, f32[512,256]{1,0:T(8,128)S(1)} %collective-permute-done.18.refs_1_, f32[512,256]{1,0:T(8,128)S(1)} %collective-permute-done.19.refs_2_, ...), custom_call_target="tpu_custom_call" | custom-call | tf_op jit(solution)/shard_map/pallas_call | solution.py:296
  (63 shorter events, 22.6 us)
Async XLA Ops:
  0.0 7.8 %collective-permute-start = (s32[16,20]{1,0:T(8,128)}, s32[16,20]{1,0:T(8,128)S(1)}, u32[]{:S(2)}, u32[]{:S(2)}) collective-permute-start(s32[16,20]{1,0:T(8,128)} %a.1), channel_id=1, source_target_pairs={{0,8},{8,0},{16,24},{24,16},{1,9},{9,1},{17,25},{25,17},{2,10},{10... | collective-permute-start | bytes 3848 | tf_op jit(solution)/shard_map/ppermute | solution.py:169
  1.4 6.4 %collective-permute-start.1 = (s32[16,20]{1,0:T(8,128)}, s32[16,20]{1,0:T(8,128)S(1)}, u32[]{:S(2)}, u32[]{:S(2)}) collective-permute-start(s32[16,20]{1,0:T(8,128)} %a.1), channel_id=1, source_target_pairs={{0,16},{8,24},{16,0},{24,8},{1,17},{9,25},{17,1},{25,9},{2,18},{10... | collective-permute-start | bytes 3848 | tf_op jit(solution)/shard_map/ppermute | solution.py:169
  2.7 5.1 %collective-permute-start.2 = (s32[16,20]{1,0:T(8,128)}, s32[16,20]{1,0:T(8,128)S(1)}, u32[]{:S(2)}, u32[]{:S(2)}) collective-permute-start(s32[16,20]{1,0:T(8,128)} %a.1), channel_id=1, source_target_pairs={{0,24},{8,16},{16,8},{24,0},{1,25},{9,17},{17,9},{25,1},{2,26},{10... | collective-permute-start | bytes 3848 | tf_op jit(solution)/shard_map/ppermute | solution.py:169
  7.9 6.0 %collective-permute-start.4 = (s32[4,16,20]{2,1,0:T(8,128)S(1)}, s32[4,16,20]{2,1,0:T(8,128)S(1)}, u32[]{:S(2)}, u32[]{:S(2)}) collective-permute-start(s32[4,16,20]{2,1,0:T(8,128)S(1)} %shard_map.64.after.refs_1_.refs_3_), channel_id=1, source_target_pairs={{0,96},{32,0},{64,32},{96,64},{1,97},{33,1},{65,33},{97,65},{2,98}... | collective-permute-start | bytes 15368 | tf_op jit(solution)/shard_map/ppermute | solution.py:144
  11.9 4.0 %collective-permute-start.5 = (s32[4,16,20]{2,1,0:T(8,128)S(1)}, s32[4,16,20]{2,1,0:T(8,128)S(1)}, u32[]{:S(2)}, u32[]{:S(2)}) collective-permute-start(s32[4,16,20]{2,1,0:T(8,128)S(1)} %shard_map.64.after.refs_1_.refs_3_), channel_id=1, source_target_pairs={{0,32},{32,64},{64,96},{96,0},{1,33},{33,65},{65,97},{97,1},{2,34}... | collective-permute-start | bytes 15368 | tf_op jit(solution)/shard_map/ppermute | solution.py:144
  11.9 4.3 %collective-permute-start.3 = (s32[4,16,20]{2,1,0:T(8,128)S(1)}, s32[4,16,20]{2,1,0:T(8,128)S(1)}, u32[]{:S(2)}, u32[]{:S(2)}) collective-permute-start(s32[4,16,20]{2,1,0:T(8,128)S(1)} %shard_map.64.after.refs_1_.refs_3_), channel_id=1, source_target_pairs={{0,64},{32,96},{64,0},{96,32},{1,65},{33,97},{65,1},{97,33},{2,66}... | collective-permute-start | bytes 15368 | tf_op jit(solution)/shard_map/ppermute | solution.py:144
  19.9 12.4 %collective-permute-start.6 = (bf16[2,512,256]{2,1,0:T(8,128)(2,1)S(1)}, bf16[2,512,256]{2,1,0:T(8,128)(2,1)S(1)}, u32[]{:S(2)}, u32[]{:S(2)}) collective-permute-start(bf16[2,512,256]{2,1,0:T(8,128)(2,1)S(1)} %get-tuple-element.19.after), channel_id=1, source_target_pairs={{0,3},{1,0},{2,1},{3,2},{4,7},{5,4},{6,5},{7,6},{8,11},{9,8},{10,9... | collective-permute-start | bytes 1572872 | tf_op jit(solution)/shard_map/ppermute | solution.py:144
  22.7 12.7 %collective-permute-start.7 = (bf16[2,512,256]{2,1,0:T(8,128)(2,1)S(1)}, bf16[2,512,256]{2,1,0:T(8,128)(2,1)S(1)}, u32[]{:S(2)}, u32[]{:S(2)}) collective-permute-start(bf16[2,512,256]{2,1,0:T(8,128)(2,1)S(1)} %get-tuple-element.21), channel_id=1, source_target_pairs={{0,1},{1,2},{2,3},{3,0},{4,5},{5,6},{6,7},{7,4},{8,9},{9,10},{10,1... | collective-permute-start | bytes 1572872 | tf_op jit(solution)/shard_map/ppermute | solution.py:144
  26.5 22.4 %collective-permute-start.8 = (bf16[2,512,256]{2,1,0:T(8,128)(2,1)S(1)}, bf16[2,512,256]{2,1,0:T(8,128)(2,1)S(1)}, u32[]{:S(2)}, u32[]{:S(2)}) collective-permute-start(bf16[2,512,256]{2,1,0:T(8,128)(2,1)S(1)} %get-tuple-element.20.after), channel_id=1, source_target_pairs={{0,3},{1,0},{2,1},{3,2},{4,7},{5,4},{6,5},{7,6},{8,11},{9,8},{10,9... | collective-permute-start | bytes 1572872 | tf_op jit(solution)/shard_map/ppermute | solution.py:144
  29.2 19.6 %collective-permute-start.9 = (bf16[2,512,256]{2,1,0:T(8,128)(2,1)S(1)}, bf16[2,512,256]{2,1,0:T(8,128)(2,1)S(1)}, u32[]{:S(2)}, u32[]{:S(2)}) collective-permute-start(bf16[2,512,256]{2,1,0:T(8,128)(2,1)S(1)} %get-tuple-element.23), channel_id=1, source_target_pairs={{0,1},{1,2},{2,3},{3,0},{4,5},{5,6},{6,7},{7,4},{8,9},{9,10},{10,1... | collective-permute-start | bytes 1572872 | tf_op jit(solution)/shard_map/ppermute | solution.py:144
  39.1 17.8 %collective-permute-start.10 = (bf16[4,2,128,256]{3,2,1,0:T(8,128)(2,1)S(1)}, bf16[4,2,128,256]{3,2,1,0:T(8,128)(2,1)S(1)}, u32[]{:S(2)}, u32[]{:S(2)}) collective-permute-start(bf16[4,2,128,256]{3,2,1,0:T(8,128)(2,1)S(1)} %get-tuple-element.22.after), channel_id=1, source_target_pairs={{0,3},{1,0},{2,1},{3,2},{4,7},{5,4},{6,5},{7,6},{8,11},{9,8},{10,9... | collective-permute-start | bytes 1572872 | tf_op jit(solution)/shard_map/ppermute | solution.py:144
  39.4 18.5 %collective-permute-start.11 = (bf16[4,2,128,256]{3,2,1,0:T(8,128)(2,1)S(1)}, bf16[4,2,128,256]{3,2,1,0:T(8,128)(2,1)S(1)}, u32[]{:S(2)}, u32[]{:S(2)}) collective-permute-start(bf16[4,2,128,256]{3,2,1,0:T(8,128)(2,1)S(1)} %get-tuple-element.25), channel_id=1, source_target_pairs={{0,1},{1,2},{2,3},{3,0},{4,5},{5,6},{6,7},{7,4},{8,9},{9,10},{10,1... | collective-permute-start | bytes 1572872 | tf_op jit(solution)/shard_map/ppermute | solution.py:144
  55.4 27.2 %collective-permute-start.14 = (bf16[4,2,128,256]{3,2,1,0:T(8,128)(2,1)S(1)}, bf16[4,2,128,256]{3,2,1,0:T(8,128)(2,1)S(1)}, u32[]{:S(2)}, u32[]{:S(2)}) collective-permute-start(bf16[4,2,128,256]{3,2,1,0:T(8,128)(2,1)S(1)} %get-tuple-element.24.after), channel_id=1, source_target_pairs={{0,3},{1,0},{2,1},{3,2},{4,7},{5,4},{6,5},{7,6},{8,11},{9,8},{10,9... | collective-permute-start | bytes 1572872 | tf_op jit(solution)/shard_map/ppermute | solution.py:144
  56.9 25.7 %collective-permute-start.15 = (bf16[4,2,128,256]{3,2,1,0:T(8,128)(2,1)}, bf16[4,2,128,256]{3,2,1,0:T(8,128)(2,1)}, u32[]{:S(2)}, u32[]{:S(2)}) collective-permute-start(bf16[4,2,128,256]{3,2,1,0:T(8,128)(2,1)} %get-tuple-element.29), channel_id=1, source_target_pairs={{0,1},{1,2},{2,3},{3,0},{4,5},{5,6},{6,7},{7,4},{8,9},{9,10},{10,1... | collective-permute-start | bytes 1572872 | tf_op jit(solution)/shard_map/ppermute | solution.py:144
  64.4 18.2 %collective-permute-start.16 = (bf16[4,2,128,256]{3,2,1,0:T(8,128)(2,1)S(1)}, bf16[4,2,128,256]{3,2,1,0:T(8,128)(2,1)}, u32[]{:S(2)}, u32[]{:S(2)}) collective-permute-start(bf16[4,2,128,256]{3,2,1,0:T(8,128)(2,1)S(1)} %get-tuple-element.28.refs_3_), channel_id=1, source_target_pairs={{0,3},{1,0},{2,1},{3,2},{4,7},{5,4},{6,5},{7,6},{8,11},{9,8},{10,9... | collective-permute-start | bytes 1572872 | tf_op jit(solution)/shard_map/ppermute | solution.py:144
  66.1 16.5 %collective-permute-start.17 = (bf16[4,2,128,256]{3,2,1,0:T(8,128)(2,1)}, bf16[4,2,128,256]{3,2,1,0:T(8,128)(2,1)}, u32[]{:S(2)}, u32[]{:S(2)}) collective-permute-start(bf16[4,2,128,256]{3,2,1,0:T(8,128)(2,1)} %get-tuple-element.30), channel_id=1, source_target_pairs={{0,1},{1,2},{2,3},{3,0},{4,5},{5,6},{6,7},{7,4},{8,9},{9,10},{10,1... | collective-permute-start | bytes 1572872 | tf_op jit(solution)/shard_map/ppermute | solution.py:144
  69.0 26.0 %all-to-all-start = ((f32[8,1,128,256]{3,2,1,0:T(8,128)}), f32[8,1,128,256]{3,2,1,0:T(8,128)S(1)}, u32[]{:S(2)}, u32[]{:S(2)}) async-start(f32[8,1,128,256]{3,2,1,0:T(8,128)} %shard_map.73.refs_6_), calls=%async_computation | async-start | bytes 2097152 | tf_op jit(solution)/shard_map/all_to_all | solution.py:261
  79.6 20.6 %collective-permute-start.12 = (bf16[4,2,128,256]{3,2,1,0:T(8,128)(2,1)}, bf16[4,2,128,256]{3,2,1,0:T(8,128)(2,1)}, u32[]{:S(2)}, u32[]{:S(2)}) collective-permute-start(bf16[4,2,128,256]{3,2,1,0:T(8,128)(2,1)} %get-tuple-element.26), channel_id=1, source_target_pairs={{0,3},{1,0},{2,1},{3,2},{4,7},{5,4},{6,5},{7,6},{8,11},{9,8},{10,9... | collective-permute-start | bytes 1572872 | tf_op jit(solution)/shard_map/ppermute | solution.py:144
  82.6 17.7 %collective-permute-start.13 = (bf16[4,2,128,256]{3,2,1,0:T(8,128)(2,1)S(1)}, bf16[4,2,128,256]{3,2,1,0:T(8,128)(2,1)}, u32[]{:S(2)}, u32[]{:S(2)}) collective-permute-start(bf16[4,2,128,256]{3,2,1,0:T(8,128)(2,1)S(1)} %get-tuple-element.27), channel_id=1, source_target_pairs={{0,1},{1,2},{2,3},{3,0},{4,5},{5,6},{6,7},{7,4},{8,9},{9,10},{10,1... | collective-permute-start | bytes 1572872 | tf_op jit(solution)/shard_map/ppermute | solution.py:144
  95.0 18.7 %all-to-all-start.2 = ((bf16[8,2,128,256]{3,2,1,0:T(8,128)(2,1)}), bf16[8,2,128,256]{3,2,1,0:T(8,128)(2,1)S(1)}, u32[]{:S(2)}, u32[]{:S(2)}) async-start(bf16[8,2,128,256]{3,2,1,0:T(8,128)(2,1)} %shard_map.74.after), calls=%async_computation.2 | async-start | bytes 2097152 | tf_op jit(solution)/shard_map/all_to_all | solution.py:261
  98.6 28.4 %collective-permute-start.19 = (f32[512,256]{1,0:T(8,128)S(1)}, f32[512,256]{1,0:T(8,128)S(1)}, u32[]{:S(2)}, u32[]{:S(2)}) collective-permute-start(f32[512,256]{1,0:T(8,128)S(1)} %shard_map.75.refs_3_), channel_id=1, source_target_pairs={{0,64},{32,96},{64,0},{96,32},{1,65},{33,97},{65,1},{97,33},{2,66}... | collective-permute-start | bytes 1572872 | tf_op jit(solution)/shard_map/ppermute | solution.py:144
  113.7 13.2 %all-to-all-start.1 = ((bf16[8,1,128,256]{3,2,1,0:T(8,128)(2,1)}), bf16[8,1,128,256]{3,2,1,0:T(8,128)(2,1)S(1)}, u32[]{:S(2)}, u32[]{:S(2)}) async-start(bf16[8,1,128,256]{3,2,1,0:T(8,128)(2,1)} %shard_map.76.after), calls=%async_computation.1 | async-start | bytes 1048576 | tf_op jit(solution)/shard_map/all_to_all | solution.py:261
  118.1 15.1 %collective-permute-start.18 = (f32[512,256]{1,0:T(8,128)S(1)}, f32[512,256]{1,0:T(8,128)S(1)}, u32[]{:S(2)}, u32[]{:S(2)}) collective-permute-start(f32[512,256]{1,0:T(8,128)S(1)} %get-tuple-element.31.after), channel_id=1, source_target_pairs={{0,32},{32,64},{64,96},{96,0},{1,33},{33,65},{65,97},{97,1},{2,34}... | collective-permute-start | bytes 1572872 | tf_op jit(solution)/shard_map/ppermute | solution.py:144
  118.3 14.8 %collective-permute-start.20 = (f32[512,256]{1,0:T(8,128)}, f32[512,256]{1,0:T(8,128)S(1)}, u32[]{:S(2)}, u32[]{:S(2)}) collective-permute-start(f32[512,256]{1,0:T(8,128)} %get-tuple-element.32), channel_id=1, source_target_pairs={{0,96},{32,0},{64,32},{96,64},{1,97},{33,1},{65,33},{97,65},{2,98}... | collective-permute-start | bytes 1572872 | tf_op jit(solution)/shard_map/ppermute | solution.py:144
  (8 other events, 213.9 us)

commit v5 on v4

--- a/solution.py
+++ b/solution.py
@@ -75,11 +75,12 @@
         put(up_ref, 1, product(rows_ref, aux_ref[1, above]) + from_down[0].astype(jnp.float32))
 
 
-def own_kernel(at, green_ref, aux_ref, after, mask_refs, out_ref, rows_ref):
-    chunk = pl.program_id(0)
-    fill(at, chunk, green_ref, mask_refs, rows_ref)
-    for h in range(2):
-        put(out_ref.at[0], h, product(rows_ref, aux_ref[h, at[0]]))
+def own_kernel(chunks, at, green_ref, aux_ref, after, *refs):
+    n, rows_ref = len(chunks), refs[-1]
+    for q, chunk in enumerate(chunks):
+        fill(at, chunk, green_ref, refs[q], rows_ref)
+        for h in range(2):
+            put(refs[n + q], h, product(rows_ref, aux_ref[h, at[0]]))
 
 
 def sum_kernel(n, *refs):
@@ -89,7 +90,7 @@
         for i in range(4):
             for h in range(2):
                 others = from_up[i, h].astype(jnp.float32) + from_down[i, h].astype(jnp.float32)
-                out_ref[2 * i + h, q] = (own_ref[0, i, h] + others).astype(out_ref.dtype)
+                out_ref[2 * i + h, q] = (own_ref[i, h] + others).astype(out_ref.dtype)
 
 
 def gather_kernel(got_ref, after, *out_refs):
@@ -228,36 +229,26 @@
         return out[0]
 
     def own(after):
-        joined = jnp.concatenate(marks)
-        return pl.pallas_call(
-            own_kernel,
-            grid_spec=pltpu.PrefetchScalarGridSpec(
-                num_scalar_prefetch=1,
-                grid=(nz,),
-                in_specs=[WHOLE, WHOLE, ANY, pl.BlockSpec((4, height, blocks), lambda j, at: (j, 0, 0))],
-                out_specs=pl.BlockSpec((1, *message), lambda j, at: (j, 0, 0, 0, 0)),
-                scratch_shapes=[pltpu.VMEM((rows, cols), bf16)],
-            ),
-            out_shape=pltpu.HBM((nz, *message), f32),
-            compiler_params=SMALL,
-            cost_estimate=COST,
-        )(at, green, aux, after, joined)
+        chunks = tuple(range(nz))
+        return call(
+            functools.partial(own_kernel, chunks), after, [marks[d] for d in chunks], [None] * nz,
+            [shape(message, f32)] * nz,
+        )
 
     crossed = {}
 
     def cross(chunks, after, kind, cost=LITTLE):
         n = len(chunks)
         fixed = pl.BlockSpec(message, lambda j: (0, 0, 0, 0))
-        own_of = lambda d: pl.BlockSpec((1, *message), lambda j: (d, 0, 0, 0, 0))
         total = pl.pallas_call(
             functools.partial(sum_kernel, n),
             grid=(1,),
-            in_specs=[v for d in chunks for v in (own_of(d), fixed, fixed)] + [ANY],
+            in_specs=[fixed] * (3 * n) + [ANY],
             out_specs=pl.BlockSpec((8, n, part, width), lambda j: (0, 0, 0, 0)),
             out_shape=shape((8, n, part, width), kind),
             compiler_params=SMALL,
             cost_estimate=cost,
-        )(*[v for d in chunks for v in (mine, *step2[d])], after)
+        )(*[v for d in chunks for v in (mine[d], *step2[d])], after)
         crossed[chunks] = lax.all_to_all(total, ("xl", "c", "xh"), split_axis=0, concat_axis=0, tiled=True)
         return total
 
@@ -278,9 +269,8 @@
 
     last = far((2, 0), quad, (marks[1], marks[3]))
     last = far((1, 3), last)
-    last = near((2,), last)
-    last = mine = own(last)
-    mine = pltpu.with_memory_space_constraint(mine, pltpu.HBM)
+    mine = own(last)
+    last = near((2,), mine[0])
     last = near((1,), last)
     last = near((3, 0), last, step2[2], LITTLE)
     last = cross((2,), last, f32)

time: 137 us -> 137 us (level)
  Pallas kernels: 44.4 us -> 41.7 us
  local copies, waits for them, and re-layouts: 6.28 us -> 8.13 us
  waiting for transfers between devices: 41.1 us -> 42.7 us
    pallas_call x4 -> x3, Pallas kernels: 16.3 us -> 6.2 us  [cross(): pl.pallas_call(functools.partial(sum_kernel, n), grid=(1,), in_specs=[fix...]
    pallas_call x5 -> x6, Pallas kernels: 21.9 us -> 28.5 us  [call(): pl.pallas_call(kernel, grid_spec=pltpu.PrefetchScalarGridSpec(num_scalar_...]
    ppermute x18, waiting for transfers between devices: 15.8 us -> 18.4 us  [shift(): return lax.ppermute(v, axis, [(i, (i + by) % n) for i in range(n)])]
    unnamed x16 -> x26, local copies, waits for them, and re-layouts: 6.19 us -> 8.05 us
  transfers between devices with their start and end apart: 24 -> 24, of which waited for: 9 -> 10; matrix products, arithmetic and copies ran while one was open for 1% -> 1% of each run, Pallas kernels for 27% -> 25%
where the time goes in v5:
time: 137 us
  waiting for transfers between devices  42.7 us (31%)
  starting transfers between devices  42.6 us (31%)
  Pallas kernels  41.7 us (30%)
  local copies, waits for them, and re-layouts  8.13 us (6%)
    pallas_call x6, Pallas kernels, call(): pl.pallas_call(kernel, grid_spec=pltpu.PrefetchScalarGridSpec(num_scalar_...  28.5 us
    all_to_all x3, waiting for transfers between devices, cross(): lax.all_to_all(total, ('xl', 'c', 'xh'), split_axis=0, concat_axis=0, til...  24.3 us
    ppermute x18, starting transfers between devices, shift(): return lax.ppermute(v, axis, [(i, (i + by) % n) for i in range(n)])  22.5 us
    ppermute x18, waiting for transfers between devices, shift(): return lax.ppermute(v, axis, [(i, (i + by) % n) for i in range(n)])  18.4 us
    all_to_all x3, starting transfers between devices, cross(): lax.all_to_all(total, ('xl', 'c', 'xh'), split_axis=0, concat_axis=0, til...  17.1 us
    unnamed x26, local copies, waits for them, and re-layouts  8.05 us
    pallas_call x3, Pallas kernels, cross(): pl.pallas_call(functools.partial(sum_kernel, n), grid=(1,), in_specs=[fix...  6.2 us
    pallas_call x1, Pallas kernels, body(): pl.pallas_call(final_kernel, grid=(width // LANES,), in_specs=[pl.BlockSp...  3.83 us
  transfers between devices with their start and end apart: 24, of which 10 were waited for; matrix products, arithmetic and copies ran while one was open for 1% of the time, Pallas kernels for 25%

profile of v5, /device:TPU:1, one launch (start us, length us, event | category | flops | bytes accessed | tf_op | source)
XLA Modules:
  0.0 136.7 jit_solution(1033172952047588604)
XLA Ops:
  3.1 4.0 %copy-done.1 = bf16[2048,2560]{1,0:T(8,128)(2,1)S(1)} copy-done((bf16[2048,2560]{1,0:T(8,128)(2,1)S(1)}, bf16[2048,2560]{1,0:T(8,128)(2,1)}, u32[]{:S(2)}) %copy-start.1) | copy-done | bytes 10485784
  7.9 4.0 %collective-permute-start.4 = (s32[4,16,20]{2,1,0:T(8,128)S(1)}, s32[4,16,20]{2,1,0:T(8,128)S(1)}, u32[]{:S(2)}, u32[]{:S(2)}) collective-permute-start(s32[4,16,20]{2,1,0:T(8,128)S(1)} %shard_map.64.after.refs_1_.refs_0_.refs_3_), channel_id=1, source_target_pairs={{0,96},{32,0},{64,32},{96,64},{1,97},{33,1},{65,33},{97,65},{2,98}... | collective-permute-start | bytes 15368 | tf_op jit(solution)/shard_map/ppermute | solution.py:145
  16.2 3.7 %shard_map.67 = (bf16[2,512,256]{2,1,0:T(8,128)(2,1)S(1)}, bf16[2,512,256]{2,1,0:T(8,128)(2,1)S(1)}) custom-call(s32[3]{0:T(128)S(1)} %pad_add_fusion.after.at, bf16[8,16,16,2560]{3,2,1,0:T(8,128)(2,1)S(1)} %shard_map.65.green_ref, bf16[2,4,256,2560]{3,2,1,0:T(8,128)(2,1)S(1)} %shard_map.66.aux_ref, ...), custom_call_target="tpu_custom_call" | custom-call | flops 4000000000 | bytes 20000000 | tf_op jit(solution)/shard_map/pallas_call | solution.py:185
  19.9 2.8 %collective-permute-start.6 = (bf16[2,512,256]{2,1,0:T(8,128)(2,1)S(1)}, bf16[2,512,256]{2,1,0:T(8,128)(2,1)S(1)}, u32[]{:S(2)}, u32[]{:S(2)}) collective-permute-start(bf16[2,512,256]{2,1,0:T(8,128)(2,1)S(1)} %get-tuple-element.23.after), channel_id=1, source_target_pairs={{0,3},{1,0},{2,1},{3,2},{4,7},{5,4},{6,5},{7,6},{8,11},{9,8},{10,9... | collective-permute-start | bytes 1572872 | tf_op jit(solution)/shard_map/ppermute | solution.py:145
  22.7 3.7 %shard_map.68 = (bf16[2,512,256]{2,1,0:T(8,128)(2,1)S(1)}, bf16[2,512,256]{2,1,0:T(8,128)(2,1)S(1)}) custom-call(s32[3]{0:T(128)S(1)} %pad_add_fusion.after.at, bf16[8,16,16,2560]{3,2,1,0:T(8,128)(2,1)S(1)} %shard_map.65.green_ref, bf16[2,4,256,2560]{3,2,1,0:T(8,128)(2,1)S(1)} %shard_map.66.aux_ref, bf16[2,512,256]{2,1,0:T(8,128)(2,1)S(1)} %get-tuple-element.23.after, ...), custom_call_target="tpu_custom_call" | custom-call | flops 4000000000 | bytes 20000000 | tf_op jit(solution)/shard_map/pallas_call | solution.py:185
  26.5 2.7 %collective-permute-start.8 = (bf16[2,512,256]{2,1,0:T(8,128)(2,1)S(1)}, bf16[2,512,256]{2,1,0:T(8,128)(2,1)S(1)}, u32[]{:S(2)}, u32[]{:S(2)}) collective-permute-start(bf16[2,512,256]{2,1,0:T(8,128)(2,1)S(1)} %get-tuple-element.24.after), channel_id=1, source_target_pairs={{0,3},{1,0},{2,1},{3,2},{4,7},{5,4},{6,5},{7,6},{8,11},{9,8},{10,9... | collective-permute-start | bytes 1572872 | tf_op jit(solution)/shard_map/ppermute | solution.py:145
  29.2 6.6 %shard_map.69 = (f32[4,2,128,256]{3,2,1,0:T(8,128)S(1)}, f32[4,2,128,256]{3,2,1,0:T(8,128)S(1)}, f32[4,2,128,256]{3,2,1,0:T(8,128)S(1)}, f32[4,2,128,256]{3,2,1,0:T(8,128)S(1)}) custom-call(s32[3]{0:T(128)S(1)} %pad_add_fusion.after.at, bf16[8,16,16,2560]{3,2,1,0:T(8,128)(2,1)S(1)} %shard_map.65.green_ref, bf16[2,4,256,2560]{3,2,1,0:T(8,128)(2,1)S(1)} %shard_map.66.aux_ref, ...), custom_call_target="tpu_custom_call" | custom-call | flops 4000000000 | bytes 20000000 | tf_op jit(solution)/shard_map/pallas_call | solution.py:185
  35.8 3.6 %shard_map.70 = (bf16[4,2,128,256]{3,2,1,0:T(8,128)(2,1)S(1)}, bf16[4,2,128,256]{3,2,1,0:T(8,128)(2,1)S(1)}) custom-call(s32[3]{0:T(128)S(1)} %pad_add_fusion.after.at, bf16[8,16,16,2560]{3,2,1,0:T(8,128)(2,1)S(1)} %shard_map.65.green_ref, bf16[2,4,256,2560]{3,2,1,0:T(8,128)(2,1)S(1)} %shard_map.66.aux_ref, ...), custom_call_target="tpu_custom_call" | custom-call | flops 4000000000 | bytes 20000000 | tf_op jit(solution)/shard_map/pallas_call | solution.py:185
  39.4 2.7 %collective-permute-start.10 = (bf16[4,2,128,256]{3,2,1,0:T(8,128)(2,1)S(1)}, bf16[4,2,128,256]{3,2,1,0:T(8,128)(2,1)S(1)}, u32[]{:S(2)}, u32[]{:S(2)}) collective-permute-start(bf16[4,2,128,256]{3,2,1,0:T(8,128)(2,1)S(1)} %get-tuple-element.27.after), channel_id=1, source_target_pairs={{0,3},{1,0},{2,1},{3,2},{4,7},{5,4},{6,5},{7,6},{8,11},{9,8},{10,9... | collective-permute-start | bytes 1572872 | tf_op jit(solution)/shard_map/ppermute | solution.py:145
  43.6 3.1 %collective-permute-done.9.refs_2_ = bf16[2,512,256]{2,1,0:T(8,128)(2,1)S(1)} collective-permute-done((bf16[2,512,256]{2,1,0:T(8,128)(2,1)S(1)}, bf16[2,512,256]{2,1,0:T(8,128)(2,1)S(1)}, u32[]{:S(2)}, u32[]{:S(2)}) %collective-permute-start.9) | collective-permute-done | bytes 524320 | tf_op jit(solution)/shard_map/ppermute | solution.py:145
  46.7 4.4 %shard_map.71 = (bf16[4,2,128,256]{3,2,1,0:T(8,128)(2,1)}, bf16[4,2,128,256]{3,2,1,0:T(8,128)(2,1)}) custom-call(s32[3]{0:T(128)S(1)} %pad_add_fusion.after.at, bf16[8,16,16,2560]{3,2,1,0:T(8,128)(2,1)S(1)} %shard_map.65.green_ref, bf16[2,4,256,2560]{3,2,1,0:T(8,128)(2,1)S(1)} %shard_map.66.aux_ref, bf16[4,2,128,256]{3,2,1,0:T(8,128)(2,1)S(1)} %get-tuple-element.27.after, ...), custom_call_target="tpu_custom_call" | custom-call | flops 4000000000 | bytes 20000000 | tf_op jit(solution)/shard_map/pallas_call | solution.py:185
  52.6 2.2 %collective-permute-done.10.refs_6_.refs_1_ = bf16[4,2,128,256]{3,2,1,0:T(8,128)(2,1)S(1)} collective-permute-done((bf16[4,2,128,256]{3,2,1,0:T(8,128)(2,1)S(1)}, bf16[4,2,128,256]{3,2,1,0:T(8,128)(2,1)S(1)}, u32[]{:S(2)}, u32[]{:S(2)}) %collective-permute-start.10) | collective-permute-done | bytes 524320 | tf_op jit(solution)/shard_map/ppermute | solution.py:145
  54.8 3.1 %collective-permute-done.11.refs_7_.refs_2_ = bf16[4,2,128,256]{3,2,1,0:T(8,128)(2,1)S(1)} collective-permute-done((bf16[4,2,128,256]{3,2,1,0:T(8,128)(2,1)S(1)}, bf16[4,2,128,256]{3,2,1,0:T(8,128)(2,1)S(1)}, u32[]{:S(2)}, u32[]{:S(2)}) %collective-permute-start.11) | collective-permute-done | bytes 524320 | tf_op jit(solution)/shard_map/ppermute | solution.py:145
  58.0 6.4 %shard_map.72 = (bf16[4,2,128,256]{3,2,1,0:T(8,128)(2,1)}, bf16[4,2,128,256]{3,2,1,0:T(8,128)(2,1)}, bf16[4,2,128,256]{3,2,1,0:T(8,128)(2,1)S(1)}, bf16[4,2,128,256]{3,2,1,0:T(8,128)(2,1)S(1)}) custom-call(s32[3]{0:T(128)S(1)} %pad_add_fusion.after.at, bf16[8,16,16,2560]{3,2,1,0:T(8,128)(2,1)S(1)} %shard_map.65.green_ref, ...), custom_call_target="tpu_custom_call" | custom-call | flops 1000000 | bytes 100000 | tf_op jit(solution)/shard_map/pallas_call | solution.py:185
  69.2 10.1 %all-to-all-start = ((f32[8,1,128,256]{3,2,1,0:T(8,128)}), f32[8,1,128,256]{3,2,1,0:T(8,128)S(1)}, u32[]{:S(2)}, u32[]{:S(2)}) async-start(f32[8,1,128,256]{3,2,1,0:T(8,128)} %shard_map.73.refs_6_), calls=%async_computation | async-start | bytes 2097152 | tf_op jit(solution)/shard_map/all_to_all | solution.py:252
  83.2 2.9 %shard_map.74.after = bf16[8,2,128,256]{3,2,1,0:T(8,128)(2,1)} custom-call(f32[4,2,128,256]{3,2,1,0:T(8,128)S(1)} %copy-done.6, bf16[4,2,128,256]{3,2,1,0:T(8,128)(2,1)} %collective-permute-done.14.refs_1_, bf16[4,2,128,256]{3,2,1,0:T(8,128)(2,1)} %collective-permute-done.15.refs_2_, f32[4,2,128,256]{3,2,1,0:T(8,128)S(1)} %copy-done.8, ...), custom_call_target="tpu_custom_call" | custom-call | flops 99999997952 | bytes 1000000 | tf_op jit(solution)/shard_map/pallas_call | solution.py:243
  86.1 8.5 %all-to-all-done.got_ref = f32[8,1,128,256]{3,2,1,0:T(8,128)S(1)} async-done(((f32[8,1,128,256]{3,2,1,0:T(8,128)}), f32[8,1,128,256]{3,2,1,0:T(8,128)S(1)}, u32[]{:S(2)}, u32[]{:S(2)}) %all-to-all-start) | async-done | bytes 1048608 | tf_op jit(solution)/shard_map/all_to_all | solution.py:252
  94.6 3.5 %all-to-all-start.2 = ((bf16[8,2,128,256]{3,2,1,0:T(8,128)(2,1)}), bf16[8,2,128,256]{3,2,1,0:T(8,128)(2,1)S(1)}, u32[]{:S(2)}, u32[]{:S(2)}) async-start(bf16[8,2,128,256]{3,2,1,0:T(8,128)(2,1)} %shard_map.74.after), calls=%async_computation.2 | async-start | bytes 2097152 | tf_op jit(solution)/shard_map/all_to_all | solution.py:252
  102.7 10.6 %all-to-all-done.2.got_ref = bf16[8,2,128,256]{3,2,1,0:T(8,128)(2,1)S(1)} async-done(((bf16[8,2,128,256]{3,2,1,0:T(8,128)(2,1)}), bf16[8,2,128,256]{3,2,1,0:T(8,128)(2,1)S(1)}, u32[]{:S(2)}, u32[]{:S(2)}) %all-to-all-start.2) | async-done | bytes 1048608 | tf_op jit(solution)/shard_map/all_to_all | solution.py:252
  113.3 3.5 %all-to-all-start.1 = ((bf16[8,1,128,256]{3,2,1,0:T(8,128)(2,1)}), bf16[8,1,128,256]{3,2,1,0:T(8,128)(2,1)S(1)}, u32[]{:S(2)}, u32[]{:S(2)}) async-start(bf16[8,1,128,256]{3,2,1,0:T(8,128)(2,1)} %shard_map.76.after), calls=%async_computation.1 | async-start | bytes 1048576 | tf_op jit(solution)/shard_map/all_to_all | solution.py:252
  118.0 2.7 %collective-permute-start.20 = (f32[512,256]{1,0:T(8,128)}, f32[512,256]{1,0:T(8,128)S(1)}, u32[]{:S(2)}, u32[]{:S(2)}) collective-permute-start(f32[512,256]{1,0:T(8,128)} %get-tuple-element.40), channel_id=1, source_target_pairs={{0,96},{32,0},{64,32},{96,64},{1,97},{33,1},{65,33},{97,65},{2,98}... | collective-permute-start | bytes 1572872 | tf_op jit(solution)/shard_map/ppermute | solution.py:145
  121.4 5.1 %all-to-all-done.1.got_ref = bf16[8,1,128,256]{3,2,1,0:T(8,128)(2,1)S(1)} async-done(((bf16[8,1,128,256]{3,2,1,0:T(8,128)(2,1)}), bf16[8,1,128,256]{3,2,1,0:T(8,128)(2,1)S(1)}, u32[]{:S(2)}, u32[]{:S(2)}) %all-to-all-start.1) | async-done | bytes 524320 | tf_op jit(solution)/shard_map/all_to_all | solution.py:252
  126.6 6.2 %collective-permute-done.18.refs_1_ = f32[512,256]{1,0:T(8,128)S(1)} collective-permute-done((f32[512,256]{1,0:T(8,128)S(1)}, f32[512,256]{1,0:T(8,128)S(1)}, u32[]{:S(2)}, u32[]{:S(2)}) %collective-permute-start.18) | collective-permute-done | bytes 524320 | tf_op jit(solution)/shard_map/ppermute | solution.py:145
  132.8 3.8 %shard_map.79 = f32[3840,256]{1,0:T(8,128)} custom-call(f32[240,128]{1,0:T(8,128)S(1)} %convolution_bitcast_fusion.w_ref, f32[120,256]{1,0:T(8,128)S(1)} %copy-done.3, f32[512,256]{1,0:T(8,128)S(1)} %shard_map.78.refs_0_, f32[512,256]{1,0:T(8,128)S(1)} %collective-permute-done.18.refs_1_, f32[512,256]{1,0:T(8,128)S(1)} %collective-permute-done.19.refs_2_, ...), custom_call_target="tpu_custom_call" | custom-call | tf_op jit(solution)/shard_map/pallas_call | solution.py:286
  (72 shorter events, 26.2 us)
Async XLA Ops:
  0.0 7.8 %collective-permute-start = (s32[16,20]{1,0:T(8,128)}, s32[16,20]{1,0:T(8,128)S(1)}, u32[]{:S(2)}, u32[]{:S(2)}) collective-permute-start(s32[16,20]{1,0:T(8,128)} %a.1), channel_id=1, source_target_pairs={{0,8},{8,0},{16,24},{24,16},{1,9},{9,1},{17,25},{25,17},{2,10},{10... | collective-permute-start | bytes 3848 | tf_op jit(solution)/shard_map/ppermute | solution.py:170
  1.4 6.4 %collective-permute-start.1 = (s32[16,20]{1,0:T(8,128)}, s32[16,20]{1,0:T(8,128)S(1)}, u32[]{:S(2)}, u32[]{:S(2)}) collective-permute-start(s32[16,20]{1,0:T(8,128)} %a.1), channel_id=1, source_target_pairs={{0,16},{8,24},{16,0},{24,8},{1,17},{9,25},{17,1},{25,9},{2,18},{10... | collective-permute-start | bytes 3848 | tf_op jit(solution)/shard_map/ppermute | solution.py:170
  2.7 5.1 %collective-permute-start.2 = (s32[16,20]{1,0:T(8,128)}, s32[16,20]{1,0:T(8,128)S(1)}, u32[]{:S(2)}, u32[]{:S(2)}) collective-permute-start(s32[16,20]{1,0:T(8,128)} %a.1), channel_id=1, source_target_pairs={{0,24},{8,16},{16,8},{24,0},{1,25},{9,17},{17,9},{25,1},{2,26},{10... | collective-permute-start | bytes 3848 | tf_op jit(solution)/shard_map/ppermute | solution.py:170
  7.9 6.0 %collective-permute-start.4 = (s32[4,16,20]{2,1,0:T(8,128)S(1)}, s32[4,16,20]{2,1,0:T(8,128)S(1)}, u32[]{:S(2)}, u32[]{:S(2)}) collective-permute-start(s32[4,16,20]{2,1,0:T(8,128)S(1)} %shard_map.64.after.refs_1_.refs_0_.refs_3_), channel_id=1, source_target_pairs={{0,96},{32,0},{64,32},{96,64},{1,97},{33,1},{65,33},{97,65},{2,98}... | collective-permute-start | bytes 15368 | tf_op jit(solution)/shard_map/ppermute | solution.py:145
  11.9 4.0 %collective-permute-start.5 = (s32[4,16,20]{2,1,0:T(8,128)S(1)}, s32[4,16,20]{2,1,0:T(8,128)S(1)}, u32[]{:S(2)}, u32[]{:S(2)}) collective-permute-start(s32[4,16,20]{2,1,0:T(8,128)S(1)} %shard_map.64.after.refs_1_.refs_0_.refs_3_), channel_id=1, source_target_pairs={{0,32},{32,64},{64,96},{96,0},{1,33},{33,65},{65,97},{97,1},{2,34}... | collective-permute-start | bytes 15368 | tf_op jit(solution)/shard_map/ppermute | solution.py:145
  11.9 4.3 %collective-permute-start.3 = (s32[4,16,20]{2,1,0:T(8,128)S(1)}, s32[4,16,20]{2,1,0:T(8,128)S(1)}, u32[]{:S(2)}, u32[]{:S(2)}) collective-permute-start(s32[4,16,20]{2,1,0:T(8,128)S(1)} %shard_map.64.after.refs_1_.refs_0_.refs_3_), channel_id=1, source_target_pairs={{0,64},{32,96},{64,0},{96,32},{1,65},{33,97},{65,1},{97,33},{2,66}... | collective-permute-start | bytes 15368 | tf_op jit(solution)/shard_map/ppermute | solution.py:145
  19.9 15.9 %collective-permute-start.6 = (bf16[2,512,256]{2,1,0:T(8,128)(2,1)S(1)}, bf16[2,512,256]{2,1,0:T(8,128)(2,1)S(1)}, u32[]{:S(2)}, u32[]{:S(2)}) collective-permute-start(bf16[2,512,256]{2,1,0:T(8,128)(2,1)S(1)} %get-tuple-element.23.after), channel_id=1, source_target_pairs={{0,3},{1,0},{2,1},{3,2},{4,7},{5,4},{6,5},{7,6},{8,11},{9,8},{10,9... | collective-permute-start | bytes 1572872 | tf_op jit(solution)/shard_map/ppermute | solution.py:145
  22.7 13.1 %collective-permute-start.7 = (bf16[2,512,256]{2,1,0:T(8,128)(2,1)S(1)}, bf16[2,512,256]{2,1,0:T(8,128)(2,1)S(1)}, u32[]{:S(2)}, u32[]{:S(2)}) collective-permute-start(bf16[2,512,256]{2,1,0:T(8,128)(2,1)S(1)} %get-tuple-element.26), channel_id=1, source_target_pairs={{0,1},{1,2},{2,3},{3,0},{4,5},{5,6},{6,7},{7,4},{8,9},{9,10},{10,1... | collective-permute-start | bytes 1572872 | tf_op jit(solution)/shard_map/ppermute | solution.py:145
  26.5 17.1 %collective-permute-start.8 = (bf16[2,512,256]{2,1,0:T(8,128)(2,1)S(1)}, bf16[2,512,256]{2,1,0:T(8,128)(2,1)S(1)}, u32[]{:S(2)}, u32[]{:S(2)}) collective-permute-start(bf16[2,512,256]{2,1,0:T(8,128)(2,1)S(1)} %get-tuple-element.24.after), channel_id=1, source_target_pairs={{0,3},{1,0},{2,1},{3,2},{4,7},{5,4},{6,5},{7,6},{8,11},{9,8},{10,9... | collective-permute-start | bytes 1572872 | tf_op jit(solution)/shard_map/ppermute | solution.py:145
  29.2 17.5 %collective-permute-start.9 = (bf16[2,512,256]{2,1,0:T(8,128)(2,1)S(1)}, bf16[2,512,256]{2,1,0:T(8,128)(2,1)S(1)}, u32[]{:S(2)}, u32[]{:S(2)}) collective-permute-start(bf16[2,512,256]{2,1,0:T(8,128)(2,1)S(1)} %get-tuple-element.28), channel_id=1, source_target_pairs={{0,1},{1,2},{2,3},{3,0},{4,5},{5,6},{6,7},{7,4},{8,9},{9,10},{10,1... | collective-permute-start | bytes 1572872 | tf_op jit(solution)/shard_map/ppermute | solution.py:145
  39.4 15.4 %collective-permute-start.10 = (bf16[4,2,128,256]{3,2,1,0:T(8,128)(2,1)S(1)}, bf16[4,2,128,256]{3,2,1,0:T(8,128)(2,1)S(1)}, u32[]{:S(2)}, u32[]{:S(2)}) collective-permute-start(bf16[4,2,128,256]{3,2,1,0:T(8,128)(2,1)S(1)} %get-tuple-element.27.after), channel_id=1, source_target_pairs={{0,3},{1,0},{2,1},{3,2},{4,7},{5,4},{6,5},{7,6},{8,11},{9,8},{10,9... | collective-permute-start | bytes 1572872 | tf_op jit(solution)/shard_map/ppermute | solution.py:145
  42.2 15.8 %collective-permute-start.11 = (bf16[4,2,128,256]{3,2,1,0:T(8,128)(2,1)S(1)}, bf16[4,2,128,256]{3,2,1,0:T(8,128)(2,1)S(1)}, u32[]{:S(2)}, u32[]{:S(2)}) collective-permute-start(bf16[4,2,128,256]{3,2,1,0:T(8,128)(2,1)S(1)} %get-tuple-element.30), channel_id=1, source_target_pairs={{0,1},{1,2},{2,3},{3,0},{4,5},{5,6},{6,7},{7,4},{8,9},{9,10},{10,1... | collective-permute-start | bytes 1572872 | tf_op jit(solution)/shard_map/ppermute | solution.py:145
  51.1 29.0 %collective-permute-start.14 = (bf16[4,2,128,256]{3,2,1,0:T(8,128)(2,1)}, bf16[4,2,128,256]{3,2,1,0:T(8,128)(2,1)}, u32[]{:S(2)}, u32[]{:S(2)}) collective-permute-start(bf16[4,2,128,256]{3,2,1,0:T(8,128)(2,1)} %get-tuple-element.29.after), channel_id=1, source_target_pairs={{0,3},{1,0},{2,1},{3,2},{4,7},{5,4},{6,5},{7,6},{8,11},{9,8},{10,9... | collective-permute-start | bytes 1572872 | tf_op jit(solution)/shard_map/ppermute | solution.py:145
  51.4 29.3 %collective-permute-start.15 = (bf16[4,2,128,256]{3,2,1,0:T(8,128)(2,1)}, bf16[4,2,128,256]{3,2,1,0:T(8,128)(2,1)}, u32[]{:S(2)}, u32[]{:S(2)}) collective-permute-start(bf16[4,2,128,256]{3,2,1,0:T(8,128)(2,1)} %get-tuple-element.36), channel_id=1, source_target_pairs={{0,1},{1,2},{2,3},{3,0},{4,5},{5,6},{6,7},{7,4},{8,9},{9,10},{10,1... | collective-permute-start | bytes 1572872 | tf_op jit(solution)/shard_map/ppermute | solution.py:145
  66.0 14.7 %collective-permute-start.16 = (bf16[4,2,128,256]{3,2,1,0:T(8,128)(2,1)}, bf16[4,2,128,256]{3,2,1,0:T(8,128)(2,1)}, u32[]{:S(2)}, u32[]{:S(2)}) collective-permute-start(bf16[4,2,128,256]{3,2,1,0:T(8,128)(2,1)} %get-tuple-element.34.refs_3_), channel_id=1, source_target_pairs={{0,3},{1,0},{2,1},{3,2},{4,7},{5,4},{6,5},{7,6},{8,11},{9,8},{10,9... | collective-permute-start | bytes 1572872 | tf_op jit(solution)/shard_map/ppermute | solution.py:145
  66.3 14.4 %collective-permute-start.17 = (bf16[4,2,128,256]{3,2,1,0:T(8,128)(2,1)}, bf16[4,2,128,256]{3,2,1,0:T(8,128)(2,1)}, u32[]{:S(2)}, u32[]{:S(2)}) collective-permute-start(bf16[4,2,128,256]{3,2,1,0:T(8,128)(2,1)} %get-tuple-element.38), channel_id=1, source_target_pairs={{0,1},{1,2},{2,3},{3,0},{4,5},{5,6},{6,7},{7,4},{8,9},{9,10},{10,1... | collective-permute-start | bytes 1572872 | tf_op jit(solution)/shard_map/ppermute | solution.py:145
  69.2 25.4 %all-to-all-start = ((f32[8,1,128,256]{3,2,1,0:T(8,128)}), f32[8,1,128,256]{3,2,1,0:T(8,128)S(1)}, u32[]{:S(2)}, u32[]{:S(2)}) async-start(f32[8,1,128,256]{3,2,1,0:T(8,128)} %shard_map.73.refs_6_), calls=%async_computation | async-start | bytes 2097152 | tf_op jit(solution)/shard_map/all_to_all | solution.py:252
  79.2 21.3 %collective-permute-start.12 = (bf16[4,2,128,256]{3,2,1,0:T(8,128)(2,1)}, bf16[4,2,128,256]{3,2,1,0:T(8,128)(2,1)}, u32[]{:S(2)}, u32[]{:S(2)}) collective-permute-start(bf16[4,2,128,256]{3,2,1,0:T(8,128)(2,1)} %copy-done.10), channel_id=1, source_target_pairs={{0,3},{1,0},{2,1},{3,2},{4,7},{5,4},{6,5},{7,6},{8,11},{9,8},{10,9... | collective-permute-start | bytes 1572872 | tf_op jit(solution)/shard_map/ppermute | solution.py:145
  80.2 20.4 %collective-permute-start.13 = (bf16[4,2,128,256]{3,2,1,0:T(8,128)(2,1)}, bf16[4,2,128,256]{3,2,1,0:T(8,128)(2,1)}, u32[]{:S(2)}, u32[]{:S(2)}) collective-permute-start(bf16[4,2,128,256]{3,2,1,0:T(8,128)(2,1)} %copy-done.9), channel_id=1, source_target_pairs={{0,1},{1,2},{2,3},{3,0},{4,5},{5,6},{6,7},{7,4},{8,9},{9,10},{10,1... | collective-permute-start | bytes 1572872 | tf_op jit(solution)/shard_map/ppermute | solution.py:145
  94.6 18.7 %all-to-all-start.2 = ((bf16[8,2,128,256]{3,2,1,0:T(8,128)(2,1)}), bf16[8,2,128,256]{3,2,1,0:T(8,128)(2,1)S(1)}, u32[]{:S(2)}, u32[]{:S(2)}) async-start(bf16[8,2,128,256]{3,2,1,0:T(8,128)(2,1)} %shard_map.74.after), calls=%async_computation.2 | async-start | bytes 2097152 | tf_op jit(solution)/shard_map/all_to_all | solution.py:252
  99.0 27.6 %collective-permute-start.19 = (f32[512,256]{1,0:T(8,128)}, f32[512,256]{1,0:T(8,128)S(1)}, u32[]{:S(2)}, u32[]{:S(2)}) collective-permute-start(f32[512,256]{1,0:T(8,128)} %shard_map.75.refs_3_), channel_id=1, source_target_pairs={{0,64},{32,96},{64,0},{96,32},{1,65},{33,97},{65,1},{97,33},{2,66}... | collective-permute-start | bytes 1572872 | tf_op jit(solution)/shard_map/ppermute | solution.py:145
  113.3 13.2 %all-to-all-start.1 = ((bf16[8,1,128,256]{3,2,1,0:T(8,128)(2,1)}), bf16[8,1,128,256]{3,2,1,0:T(8,128)(2,1)S(1)}, u32[]{:S(2)}, u32[]{:S(2)}) async-start(bf16[8,1,128,256]{3,2,1,0:T(8,128)(2,1)} %shard_map.76.after), calls=%async_computation.1 | async-start | bytes 1048576 | tf_op jit(solution)/shard_map/all_to_all | solution.py:252
  117.7 15.1 %collective-permute-start.18 = (f32[512,256]{1,0:T(8,128)S(1)}, f32[512,256]{1,0:T(8,128)S(1)}, u32[]{:S(2)}, u32[]{:S(2)}) collective-permute-start(f32[512,256]{1,0:T(8,128)S(1)} %get-tuple-element.39.after), channel_id=1, source_target_pairs={{0,32},{32,64},{64,96},{96,0},{1,33},{33,65},{65,97},{97,1},{2,34}... | collective-permute-start | bytes 1572872 | tf_op jit(solution)/shard_map/ppermute | solution.py:145
  118.0 14.9 %collective-permute-start.20 = (f32[512,256]{1,0:T(8,128)}, f32[512,256]{1,0:T(8,128)S(1)}, u32[]{:S(2)}, u32[]{:S(2)}) collective-permute-start(f32[512,256]{1,0:T(8,128)} %get-tuple-element.40), channel_id=1, source_target_pairs={{0,96},{32,0},{64,32},{96,64},{1,97},{33,1},{65,33},{97,65},{2,98}... | collective-permute-start | bytes 1572872 | tf_op jit(solution)/shard_map/ppermute | solution.py:145
  (13 other events, 220.5 us)

commit v6 on v5

--- a/solution.py
+++ b/solution.py
@@ -272,7 +272,7 @@
     mine = own(last)
     last = near((2,), mine[0])
     last = near((1,), last)
-    last = near((3, 0), last, step2[2], LITTLE)
+    last = near((3, 0), last, cost=LITTLE)
     last = cross((2,), last, f32)
     last = cross((1, 3), last, bf16, LONG)
     last = gather((2,), last)

time: 137 us -> 140 us (1.022)
  waiting for transfers between devices: 42.7 us -> 34.5 us
  starting transfers between devices: 42.6 us -> 49.7 us
  local copies, waits for them, and re-layouts: 8.13 us -> 10.1 us
  Pallas kernels: 41.7 us -> 43.5 us
    all_to_all x3, waiting for transfers between devices: 24.3 us -> 19.1 us  [cross(): lax.all_to_all(total, ('xl', 'c', 'xh'), split_axis=0, concat_axis=0, til...]
    all_to_all x3, starting transfers between devices: 17.1 us -> 22 us  [cross(): lax.all_to_all(total, ('xl', 'c', 'xh'), split_axis=0, concat_axis=0, til...]
    ppermute x18, waiting for transfers between devices: 18.4 us -> 15.4 us  [shift(): return lax.ppermute(v, axis, [(i, (i + by) % n) for i in range(n)])]
    ppermute x18, starting transfers between devices: 22.5 us -> 24.7 us  [shift(): return lax.ppermute(v, axis, [(i, (i + by) % n) for i in range(n)])]
    unnamed x26, local copies, waits for them, and re-layouts: 8.05 us -> 10 us
  transfers between devices with their start and end apart: 24 -> 24, of which waited for: 10 -> 9; matrix products, arithmetic and copies ran while one was open for 1% -> 1% of each run, Pallas kernels for 25% -> 26%
where the time goes in v6:
time: 140 us; the launch traced here: 139 us
  starting transfers between devices  49.7 us (36%)
  Pallas kernels  43.5 us (31%)
  waiting for transfers between devices  34.5 us (25%)
  local copies, waits for them, and re-layouts  10.1 us (7%)
    pallas_call x6, Pallas kernels, call(): pl.pallas_call(kernel, grid_spec=pltpu.PrefetchScalarGridSpec(num_scalar_...  29.2 us
    ppermute x18, starting transfers between devices, shift(): return lax.ppermute(v, axis, [(i, (i + by) % n) for i in range(n)])  24.7 us
    all_to_all x3, starting transfers between devices, cross(): lax.all_to_all(total, ('xl', 'c', 'xh'), split_axis=0, concat_axis=0, til...  22 us
    all_to_all x3, waiting for transfers between devices, cross(): lax.all_to_all(total, ('xl', 'c', 'xh'), split_axis=0, concat_axis=0, til...  19.1 us
    ppermute x18, waiting for transfers between devices, shift(): return lax.ppermute(v, axis, [(i, (i + by) % n) for i in range(n)])  15.4 us
    unnamed x26, local copies, waits for them, and re-layouts  10 us
    pallas_call x3, Pallas kernels, cross(): pl.pallas_call(functools.partial(sum_kernel, n), grid=(1,), in_specs=[fix...  7.28 us
    pallas_call x1, Pallas kernels, body(): pl.pallas_call(final_kernel, grid=(width // LANES,), in_specs=[pl.BlockSp...  3.85 us
  transfers between devices with their start and end apart: 24, of which 9 were waited for; matrix products, arithmetic and copies ran while one was open for 1% of the time, Pallas kernels for 26%

profile of v6, /device:TPU:1, one launch (start us, length us, event | category | flops | bytes accessed | tf_op | source)
XLA Modules:
  0.0 139.4 jit_solution(9247037074726580284)
XLA Ops:
  3.1 4.0 %copy-done.1 = bf16[2048,2560]{1,0:T(8,128)(2,1)S(1)} copy-done((bf16[2048,2560]{1,0:T(8,128)(2,1)S(1)}, bf16[2048,2560]{1,0:T(8,128)(2,1)}, u32[]{:S(2)}) %copy-start.1) | copy-done | bytes 10485784
  7.9 4.0 %collective-permute-start.4 = (s32[4,16,20]{2,1,0:T(8,128)S(1)}, s32[4,16,20]{2,1,0:T(8,128)S(1)}, u32[]{:S(2)}, u32[]{:S(2)}) collective-permute-start(s32[4,16,20]{2,1,0:T(8,128)S(1)} %shard_map.64.after.refs_1_.refs_0_.refs_3_), channel_id=1, source_target_pairs={{0,96},{32,0},{64,32},{96,64},{1,97},{33,1},{65,33},{97,65},{2,98}... | collective-permute-start | bytes 15368 | tf_op jit(solution)/shard_map/ppermute | solution.py:145
  16.2 3.7 %shard_map.67 = (bf16[2,512,256]{2,1,0:T(8,128)(2,1)S(1)}, bf16[2,512,256]{2,1,0:T(8,128)(2,1)S(1)}) custom-call(s32[3]{0:T(128)S(1)} %pad_add_fusion.after.at, bf16[8,16,16,2560]{3,2,1,0:T(8,128)(2,1)S(1)} %shard_map.65.green_ref, bf16[2,4,256,2560]{3,2,1,0:T(8,128)(2,1)S(1)} %shard_map.66.aux_ref, ...), custom_call_target="tpu_custom_call" | custom-call | flops 4000000000 | bytes 20000000 | tf_op jit(solution)/shard_map/pallas_call | solution.py:185
  19.9 2.8 %collective-permute-start.6 = (bf16[2,512,256]{2,1,0:T(8,128)(2,1)S(1)}, bf16[2,512,256]{2,1,0:T(8,128)(2,1)S(1)}, u32[]{:S(2)}, u32[]{:S(2)}) collective-permute-start(bf16[2,512,256]{2,1,0:T(8,128)(2,1)S(1)} %get-tuple-element.23.after), channel_id=1, source_target_pairs={{0,3},{1,0},{2,1},{3,2},{4,7},{5,4},{6,5},{7,6},{8,11},{9,8},{10,9... | collective-permute-start | bytes 1572872 | tf_op jit(solution)/shard_map/ppermute | solution.py:145
  22.7 3.7 %shard_map.68 = (bf16[2,512,256]{2,1,0:T(8,128)(2,1)S(1)}, bf16[2,512,256]{2,1,0:T(8,128)(2,1)S(1)}) custom-call(s32[3]{0:T(128)S(1)} %pad_add_fusion.after.at, bf16[8,16,16,2560]{3,2,1,0:T(8,128)(2,1)S(1)} %shard_map.65.green_ref, bf16[2,4,256,2560]{3,2,1,0:T(8,128)(2,1)S(1)} %shard_map.66.aux_ref, bf16[2,512,256]{2,1,0:T(8,128)(2,1)S(1)} %get-tuple-element.23.after, ...), custom_call_target="tpu_custom_call" | custom-call | flops 4000000000 | bytes 20000000 | tf_op jit(solution)/shard_map/pallas_call | solution.py:185
  26.5 2.7 %collective-permute-start.8 = (bf16[2,512,256]{2,1,0:T(8,128)(2,1)S(1)}, bf16[2,512,256]{2,1,0:T(8,128)(2,1)S(1)}, u32[]{:S(2)}, u32[]{:S(2)}) collective-permute-start(bf16[2,512,256]{2,1,0:T(8,128)(2,1)S(1)} %get-tuple-element.24.after), channel_id=1, source_target_pairs={{0,3},{1,0},{2,1},{3,2},{4,7},{5,4},{6,5},{7,6},{8,11},{9,8},{10,9... | collective-permute-start | bytes 1572872 | tf_op jit(solution)/shard_map/ppermute | solution.py:145
  29.2 6.6 %shard_map.69 = (f32[4,2,128,256]{3,2,1,0:T(8,128)S(1)}, f32[4,2,128,256]{3,2,1,0:T(8,128)S(1)}, f32[4,2,128,256]{3,2,1,0:T(8,128)S(1)}, f32[4,2,128,256]{3,2,1,0:T(8,128)S(1)}) custom-call(s32[3]{0:T(128)S(1)} %pad_add_fusion.after.at, bf16[8,16,16,2560]{3,2,1,0:T(8,128)(2,1)S(1)} %shard_map.65.green_ref, bf16[2,4,256,2560]{3,2,1,0:T(8,128)(2,1)S(1)} %shard_map.66.aux_ref, ...), custom_call_target="tpu_custom_call" | custom-call | flops 4000000000 | bytes 20000000 | tf_op jit(solution)/shard_map/pallas_call | solution.py:185
  37.8 4.4 %shard_map.70 = (bf16[4,2,128,256]{3,2,1,0:T(8,128)(2,1)S(1)}, bf16[4,2,128,256]{3,2,1,0:T(8,128)(2,1)}) custom-call(s32[3]{0:T(128)S(1)} %pad_add_fusion.after.at, bf16[8,16,16,2560]{3,2,1,0:T(8,128)(2,1)S(1)} %shard_map.65.green_ref, bf16[2,4,256,2560]{3,2,1,0:T(8,128)(2,1)S(1)} %shard_map.66.aux_ref, ...), custom_call_target="tpu_custom_call" | custom-call | flops 4000000000 | bytes 20000000 | tf_op jit(solution)/shard_map/pallas_call | solution.py:185
  42.2 2.7 %collective-permute-start.12 = (bf16[4,2,128,256]{3,2,1,0:T(8,128)(2,1)S(1)}, bf16[4,2,128,256]{3,2,1,0:T(8,128)(2,1)S(1)}, u32[]{:S(2)}, u32[]{:S(2)}) collective-permute-start(bf16[4,2,128,256]{3,2,1,0:T(8,128)(2,1)S(1)} %get-tuple-element.27.after), channel_id=1, source_target_pairs={{0,3},{1,0},{2,1},{3,2},{4,7},{5,4},{6,5},{7,6},{8,11},{9,8},{10,9... | collective-permute-start | bytes 1572872 | tf_op jit(solution)/shard_map/ppermute | solution.py:145
  46.7 4.4 %shard_map.71 = (bf16[4,2,128,256]{3,2,1,0:T(8,128)(2,1)S(1)}, bf16[4,2,128,256]{3,2,1,0:T(8,128)(2,1)}) custom-call(s32[3]{0:T(128)S(1)} %pad_add_fusion.after.at, bf16[8,16,16,2560]{3,2,1,0:T(8,128)(2,1)S(1)} %shard_map.65.green_ref, bf16[2,4,256,2560]{3,2,1,0:T(8,128)(2,1)S(1)} %shard_map.66.aux_ref, ...), custom_call_target="tpu_custom_call" | custom-call | flops 4000000000 | bytes 20000000 | tf_op jit(solution)/shard_map/pallas_call | solution.py:185
  51.9 6.4 %shard_map.72 = (bf16[4,2,128,256]{3,2,1,0:T(8,128)(2,1)}, bf16[4,2,128,256]{3,2,1,0:T(8,128)(2,1)}, bf16[4,2,128,256]{3,2,1,0:T(8,128)(2,1)S(1)}, bf16[4,2,128,256]{3,2,1,0:T(8,128)(2,1)S(1)}) custom-call(s32[3]{0:T(128)S(1)} %pad_add_fusion.after.at, bf16[8,16,16,2560]{3,2,1,0:T(8,128)(2,1)S(1)} %shard_map.65.green_ref, ...), custom_call_target="tpu_custom_call" | custom-call | flops 1000000 | bytes 100000 | tf_op jit(solution)/shard_map/pallas_call | solution.py:185
  64.7 2.2 %shard_map.73.refs_6_ = f32[8,1,128,256]{3,2,1,0:T(8,128)} custom-call(f32[4,2,128,256]{3,2,1,0:T(8,128)S(1)} %get-tuple-element.32.refs_0_, bf16[4,2,128,256]{3,2,1,0:T(8,128)(2,1)S(1)} %collective-permute-done.12.refs_1_, bf16[4,2,128,256]{3,2,1,0:T(8,128)(2,1)} %collective-permute-done.13.refs_2_, bf16[4,2,128,256]{3,2,1,0:T(8,128)(2,1)} %get-tuple-element.34.refs_3_), custom_call_target="tpu_custom_call" | custom-call | flops 1000000 | bytes 100000 | tf_op jit(solution)/shard_map/pallas_call | solution.py:243
  66.9 8.9 %all-to-all-start = ((f32[8,1,128,256]{3,2,1,0:T(8,128)}), f32[8,1,128,256]{3,2,1,0:T(8,128)S(1)}, u32[]{:S(2)}, u32[]{:S(2)}) async-start(f32[8,1,128,256]{3,2,1,0:T(8,128)} %shard_map.73.refs_6_), calls=%async_computation | async-start | bytes 2097152 | tf_op jit(solution)/shard_map/all_to_all | solution.py:252
  78.4 4.3 %collective-permute-done.15.refs_2_ = bf16[4,2,128,256]{3,2,1,0:T(8,128)(2,1)} collective-permute-done((bf16[4,2,128,256]{3,2,1,0:T(8,128)(2,1)}, bf16[4,2,128,256]{3,2,1,0:T(8,128)(2,1)}, u32[]{:S(2)}, u32[]{:S(2)}) %collective-permute-start.15) | collective-permute-done | bytes 524320 | tf_op jit(solution)/shard_map/ppermute | solution.py:145
  85.1 2.9 %shard_map.74.after = bf16[8,2,128,256]{3,2,1,0:T(8,128)(2,1)} custom-call(f32[4,2,128,256]{3,2,1,0:T(8,128)S(1)} %copy-done.6, bf16[4,2,128,256]{3,2,1,0:T(8,128)(2,1)} %collective-permute-done.14.refs_1_, bf16[4,2,128,256]{3,2,1,0:T(8,128)(2,1)} %collective-permute-done.15.refs_2_, f32[4,2,128,256]{3,2,1,0:T(8,128)S(1)} %copy-done.8, ...), custom_call_target="tpu_custom_call" | custom-call | flops 99999997952 | bytes 1000000 | tf_op jit(solution)/shard_map/pallas_call | solution.py:243
  88.1 3.2 %all-to-all-done.got_ref = f32[8,1,128,256]{3,2,1,0:T(8,128)S(1)} async-done(((f32[8,1,128,256]{3,2,1,0:T(8,128)}), f32[8,1,128,256]{3,2,1,0:T(8,128)S(1)}, u32[]{:S(2)}, u32[]{:S(2)}) %all-to-all-start) | async-done | bytes 1048608 | tf_op jit(solution)/shard_map/all_to_all | solution.py:252
  91.3 9.6 %all-to-all-start.2 = ((bf16[8,2,128,256]{3,2,1,0:T(8,128)(2,1)}), bf16[8,2,128,256]{3,2,1,0:T(8,128)(2,1)S(1)}, u32[]{:S(2)}, u32[]{:S(2)}) async-start(bf16[8,2,128,256]{3,2,1,0:T(8,128)(2,1)} %shard_map.74.after), calls=%async_computation.2 | async-start | bytes 2097152 | tf_op jit(solution)/shard_map/all_to_all | solution.py:252
  103.2 2.2 %shard_map.76.after = bf16[8,1,128,256]{3,2,1,0:T(8,128)(2,1)} custom-call(f32[4,2,128,256]{3,2,1,0:T(8,128)S(1)} %get-tuple-element.25.after.refs_0_, bf16[4,2,128,256]{3,2,1,0:T(8,128)(2,1)} %collective-permute-done.10.refs_1_, bf16[4,2,128,256]{3,2,1,0:T(8,128)(2,1)} %collective-permute-done.11.refs_2_, f32[512,256]{1,0:T(8,128)} %shard_map.75.refs_3_), custom_call_target="tpu_custom_call" | custom-call | flops 99999997952 | bytes 1000000 | tf_op jit(solution)/shard_map/pallas_call | solution.py:243
  105.4 10.7 %all-to-all-done.2.got_ref = bf16[8,2,128,256]{3,2,1,0:T(8,128)(2,1)S(1)} async-done(((bf16[8,2,128,256]{3,2,1,0:T(8,128)(2,1)}), bf16[8,2,128,256]{3,2,1,0:T(8,128)(2,1)S(1)}, u32[]{:S(2)}, u32[]{:S(2)}) %all-to-all-start.2) | async-done | bytes 1048608 | tf_op jit(solution)/shard_map/all_to_all | solution.py:252
  116.1 3.5 %all-to-all-start.1 = ((bf16[8,1,128,256]{3,2,1,0:T(8,128)(2,1)}), bf16[8,1,128,256]{3,2,1,0:T(8,128)(2,1)S(1)}, u32[]{:S(2)}, u32[]{:S(2)}) async-start(bf16[8,1,128,256]{3,2,1,0:T(8,128)(2,1)} %shard_map.76.after), calls=%async_computation.1 | async-start | bytes 1048576 | tf_op jit(solution)/shard_map/all_to_all | solution.py:252
  120.7 2.7 %collective-permute-start.20 = (f32[512,256]{1,0:T(8,128)}, f32[512,256]{1,0:T(8,128)S(1)}, u32[]{:S(2)}, u32[]{:S(2)}) collective-permute-start(f32[512,256]{1,0:T(8,128)} %get-tuple-element.40), channel_id=1, source_target_pairs={{0,96},{32,0},{64,32},{96,64},{1,97},{33,1},{65,33},{97,65},{2,98}... | collective-permute-start | bytes 1572872 | tf_op jit(solution)/shard_map/ppermute | solution.py:145
  124.1 5.1 %all-to-all-done.1.got_ref = bf16[8,1,128,256]{3,2,1,0:T(8,128)(2,1)S(1)} async-done(((bf16[8,1,128,256]{3,2,1,0:T(8,128)(2,1)}), bf16[8,1,128,256]{3,2,1,0:T(8,128)(2,1)S(1)}, u32[]{:S(2)}, u32[]{:S(2)}) %all-to-all-start.1) | async-done | bytes 524320 | tf_op jit(solution)/shard_map/all_to_all | solution.py:252
  129.3 6.2 %collective-permute-done.18.refs_1_ = f32[512,256]{1,0:T(8,128)S(1)} collective-permute-done((f32[512,256]{1,0:T(8,128)S(1)}, f32[512,256]{1,0:T(8,128)S(1)}, u32[]{:S(2)}, u32[]{:S(2)}) %collective-permute-start.18) | collective-permute-done | bytes 524320 | tf_op jit(solution)/shard_map/ppermute | solution.py:145
  135.5 3.8 %shard_map.79 = f32[3840,256]{1,0:T(8,128)} custom-call(f32[240,128]{1,0:T(8,128)S(1)} %convolution_bitcast_fusion.w_ref, f32[120,256]{1,0:T(8,128)S(1)} %copy-done.3, f32[512,256]{1,0:T(8,128)S(1)} %shard_map.78.refs_0_, f32[512,256]{1,0:T(8,128)S(1)} %collective-permute-done.18.refs_1_, f32[512,256]{1,0:T(8,128)S(1)} %collective-permute-done.19.refs_2_, ...), custom_call_target="tpu_custom_call" | custom-call | tf_op jit(solution)/shard_map/pallas_call | solution.py:286
  (72 shorter events, 28.5 us)
Async XLA Ops:
  0.0 7.8 %collective-permute-start = (s32[16,20]{1,0:T(8,128)}, s32[16,20]{1,0:T(8,128)S(1)}, u32[]{:S(2)}, u32[]{:S(2)}) collective-permute-start(s32[16,20]{1,0:T(8,128)} %a.1), channel_id=1, source_target_pairs={{0,8},{8,0},{16,24},{24,16},{1,9},{9,1},{17,25},{25,17},{2,10},{10... | collective-permute-start | bytes 3848 | tf_op jit(solution)/shard_map/ppermute | solution.py:170
  1.4 6.4 %collective-permute-start.1 = (s32[16,20]{1,0:T(8,128)}, s32[16,20]{1,0:T(8,128)S(1)}, u32[]{:S(2)}, u32[]{:S(2)}) collective-permute-start(s32[16,20]{1,0:T(8,128)} %a.1), channel_id=1, source_target_pairs={{0,16},{8,24},{16,0},{24,8},{1,17},{9,25},{17,1},{25,9},{2,18},{10... | collective-permute-start | bytes 3848 | tf_op jit(solution)/shard_map/ppermute | solution.py:170
  2.7 5.1 %collective-permute-start.2 = (s32[16,20]{1,0:T(8,128)}, s32[16,20]{1,0:T(8,128)S(1)}, u32[]{:S(2)}, u32[]{:S(2)}) collective-permute-start(s32[16,20]{1,0:T(8,128)} %a.1), channel_id=1, source_target_pairs={{0,24},{8,16},{16,8},{24,0},{1,25},{9,17},{17,9},{25,1},{2,26},{10... | collective-permute-start | bytes 3848 | tf_op jit(solution)/shard_map/ppermute | solution.py:170
  7.9 6.0 %collective-permute-start.4 = (s32[4,16,20]{2,1,0:T(8,128)S(1)}, s32[4,16,20]{2,1,0:T(8,128)S(1)}, u32[]{:S(2)}, u32[]{:S(2)}) collective-permute-start(s32[4,16,20]{2,1,0:T(8,128)S(1)} %shard_map.64.after.refs_1_.refs_0_.refs_3_), channel_id=1, source_target_pairs={{0,96},{32,0},{64,32},{96,64},{1,97},{33,1},{65,33},{97,65},{2,98}... | collective-permute-start | bytes 15368 | tf_op jit(solution)/shard_map/ppermute | solution.py:145
  11.9 4.0 %collective-permute-start.5 = (s32[4,16,20]{2,1,0:T(8,128)S(1)}, s32[4,16,20]{2,1,0:T(8,128)S(1)}, u32[]{:S(2)}, u32[]{:S(2)}) collective-permute-start(s32[4,16,20]{2,1,0:T(8,128)S(1)} %shard_map.64.after.refs_1_.refs_0_.refs_3_), channel_id=1, source_target_pairs={{0,32},{32,64},{64,96},{96,0},{1,33},{33,65},{65,97},{97,1},{2,34}... | collective-permute-start | bytes 15368 | tf_op jit(solution)/shard_map/ppermute | solution.py:145
  11.9 4.3 %collective-permute-start.3 = (s32[4,16,20]{2,1,0:T(8,128)S(1)}, s32[4,16,20]{2,1,0:T(8,128)S(1)}, u32[]{:S(2)}, u32[]{:S(2)}) collective-permute-start(s32[4,16,20]{2,1,0:T(8,128)S(1)} %shard_map.64.after.refs_1_.refs_0_.refs_3_), channel_id=1, source_target_pairs={{0,64},{32,96},{64,0},{96,32},{1,65},{33,97},{65,1},{97,33},{2,66}... | collective-permute-start | bytes 15368 | tf_op jit(solution)/shard_map/ppermute | solution.py:145
  19.9 17.9 %collective-permute-start.6 = (bf16[2,512,256]{2,1,0:T(8,128)(2,1)S(1)}, bf16[2,512,256]{2,1,0:T(8,128)(2,1)S(1)}, u32[]{:S(2)}, u32[]{:S(2)}) collective-permute-start(bf16[2,512,256]{2,1,0:T(8,128)(2,1)S(1)} %get-tuple-element.23.after), channel_id=1, source_target_pairs={{0,3},{1,0},{2,1},{3,2},{4,7},{5,4},{6,5},{7,6},{8,11},{9,8},{10,9... | collective-permute-start | bytes 1572872 | tf_op jit(solution)/shard_map/ppermute | solution.py:145
  22.7 15.1 %collective-permute-start.7 = (bf16[2,512,256]{2,1,0:T(8,128)(2,1)S(1)}, bf16[2,512,256]{2,1,0:T(8,128)(2,1)S(1)}, u32[]{:S(2)}, u32[]{:S(2)}) collective-permute-start(bf16[2,512,256]{2,1,0:T(8,128)(2,1)S(1)} %get-tuple-element.26), channel_id=1, source_target_pairs={{0,1},{1,2},{2,3},{3,0},{4,5},{5,6},{6,7},{7,4},{8,9},{9,10},{10,1... | collective-permute-start | bytes 1572872 | tf_op jit(solution)/shard_map/ppermute | solution.py:145
  26.5 18.4 %collective-permute-start.8 = (bf16[2,512,256]{2,1,0:T(8,128)(2,1)S(1)}, bf16[2,512,256]{2,1,0:T(8,128)(2,1)S(1)}, u32[]{:S(2)}, u32[]{:S(2)}) collective-permute-start(bf16[2,512,256]{2,1,0:T(8,128)(2,1)S(1)} %get-tuple-element.24.after), channel_id=1, source_target_pairs={{0,3},{1,0},{2,1},{3,2},{4,7},{5,4},{6,5},{7,6},{8,11},{9,8},{10,9... | collective-permute-start | bytes 1572872 | tf_op jit(solution)/shard_map/ppermute | solution.py:145
  29.2 17.5 %collective-permute-start.9 = (bf16[2,512,256]{2,1,0:T(8,128)(2,1)S(1)}, bf16[2,512,256]{2,1,0:T(8,128)(2,1)S(1)}, u32[]{:S(2)}, u32[]{:S(2)}) collective-permute-start(bf16[2,512,256]{2,1,0:T(8,128)(2,1)S(1)} %get-tuple-element.28), channel_id=1, source_target_pairs={{0,1},{1,2},{2,3},{3,0},{4,5},{5,6},{6,7},{7,4},{8,9},{9,10},{10,1... | collective-permute-start | bytes 1572872 | tf_op jit(solution)/shard_map/ppermute | solution.py:145
  42.2 19.3 %collective-permute-start.12 = (bf16[4,2,128,256]{3,2,1,0:T(8,128)(2,1)S(1)}, bf16[4,2,128,256]{3,2,1,0:T(8,128)(2,1)S(1)}, u32[]{:S(2)}, u32[]{:S(2)}) collective-permute-start(bf16[4,2,128,256]{3,2,1,0:T(8,128)(2,1)S(1)} %get-tuple-element.27.after), channel_id=1, source_target_pairs={{0,3},{1,0},{2,1},{3,2},{4,7},{5,4},{6,5},{7,6},{8,11},{9,8},{10,9... | collective-permute-start | bytes 1572872 | tf_op jit(solution)/shard_map/ppermute | solution.py:145
  44.8 17.9 %collective-permute-start.13 = (bf16[4,2,128,256]{3,2,1,0:T(8,128)(2,1)}, bf16[4,2,128,256]{3,2,1,0:T(8,128)(2,1)}, u32[]{:S(2)}, u32[]{:S(2)}) collective-permute-start(bf16[4,2,128,256]{3,2,1,0:T(8,128)(2,1)} %get-tuple-element.33), channel_id=1, source_target_pairs={{0,1},{1,2},{2,3},{3,0},{4,5},{5,6},{6,7},{7,4},{8,9},{9,10},{10,1... | collective-permute-start | bytes 1572872 | tf_op jit(solution)/shard_map/ppermute | solution.py:145
  51.1 27.3 %collective-permute-start.14 = (bf16[4,2,128,256]{3,2,1,0:T(8,128)(2,1)S(1)}, bf16[4,2,128,256]{3,2,1,0:T(8,128)(2,1)}, u32[]{:S(2)}, u32[]{:S(2)}) collective-permute-start(bf16[4,2,128,256]{3,2,1,0:T(8,128)(2,1)S(1)} %get-tuple-element.29.after), channel_id=1, source_target_pairs={{0,3},{1,0},{2,1},{3,2},{4,7},{5,4},{6,5},{7,6},{8,11},{9,8},{10,9... | collective-permute-start | bytes 1572872 | tf_op jit(solution)/shard_map/ppermute | solution.py:145
  60.0 16.6 %collective-permute-start.16 = (bf16[4,2,128,256]{3,2,1,0:T(8,128)(2,1)}, bf16[4,2,128,256]{3,2,1,0:T(8,128)(2,1)}, u32[]{:S(2)}, u32[]{:S(2)}) collective-permute-start(bf16[4,2,128,256]{3,2,1,0:T(8,128)(2,1)} %get-tuple-element.34.refs_3_), channel_id=1, source_target_pairs={{0,3},{1,0},{2,1},{3,2},{4,7},{5,4},{6,5},{7,6},{8,11},{9,8},{10,9... | collective-permute-start | bytes 1572872 | tf_op jit(solution)/shard_map/ppermute | solution.py:145
  60.0 18.4 %collective-permute-start.17 = (bf16[4,2,128,256]{3,2,1,0:T(8,128)(2,1)}, bf16[4,2,128,256]{3,2,1,0:T(8,128)(2,1)}, u32[]{:S(2)}, u32[]{:S(2)}) collective-permute-start(bf16[4,2,128,256]{3,2,1,0:T(8,128)(2,1)} %get-tuple-element.38), channel_id=1, source_target_pairs={{0,1},{1,2},{2,3},{3,0},{4,5},{5,6},{6,7},{7,4},{8,9},{9,10},{10,1... | collective-permute-start | bytes 1572872 | tf_op jit(solution)/shard_map/ppermute | solution.py:145
  61.5 21.2 %collective-permute-start.15 = (bf16[4,2,128,256]{3,2,1,0:T(8,128)(2,1)}, bf16[4,2,128,256]{3,2,1,0:T(8,128)(2,1)}, u32[]{:S(2)}, u32[]{:S(2)}) collective-permute-start(bf16[4,2,128,256]{3,2,1,0:T(8,128)(2,1)} %get-tuple-element.36), channel_id=1, source_target_pairs={{0,1},{1,2},{2,3},{3,0},{4,5},{5,6},{6,7},{7,4},{8,9},{9,10},{10,1... | collective-permute-start | bytes 1572872 | tf_op jit(solution)/shard_map/ppermute | solution.py:145
  62.7 40.5 %collective-permute-start.10 = (bf16[4,2,128,256]{3,2,1,0:T(8,128)(2,1)}, bf16[4,2,128,256]{3,2,1,0:T(8,128)(2,1)}, u32[]{:S(2)}, u32[]{:S(2)}) collective-permute-start(bf16[4,2,128,256]{3,2,1,0:T(8,128)(2,1)} %copy-done.10), channel_id=1, source_target_pairs={{0,3},{1,0},{2,1},{3,2},{4,7},{5,4},{6,5},{7,6},{8,11},{9,8},{10,9... | collective-permute-start | bytes 1572872 | tf_op jit(solution)/shard_map/ppermute | solution.py:145
  66.9 24.3 %all-to-all-start = ((f32[8,1,128,256]{3,2,1,0:T(8,128)}), f32[8,1,128,256]{3,2,1,0:T(8,128)S(1)}, u32[]{:S(2)}, u32[]{:S(2)}) async-start(f32[8,1,128,256]{3,2,1,0:T(8,128)} %shard_map.73.refs_6_), calls=%async_computation | async-start | bytes 2097152 | tf_op jit(solution)/shard_map/all_to_all | solution.py:252
  76.6 26.6 %collective-permute-start.11 = (bf16[4,2,128,256]{3,2,1,0:T(8,128)(2,1)}, bf16[4,2,128,256]{3,2,1,0:T(8,128)(2,1)}, u32[]{:S(2)}, u32[]{:S(2)}) collective-permute-start(bf16[4,2,128,256]{3,2,1,0:T(8,128)(2,1)} %copy-done.9), channel_id=1, source_target_pairs={{0,1},{1,2},{2,3},{3,0},{4,5},{5,6},{6,7},{7,4},{8,9},{9,10},{10,1... | collective-permute-start | bytes 1572872 | tf_op jit(solution)/shard_map/ppermute | solution.py:145
  91.3 24.8 %all-to-all-start.2 = ((bf16[8,2,128,256]{3,2,1,0:T(8,128)(2,1)}), bf16[8,2,128,256]{3,2,1,0:T(8,128)(2,1)S(1)}, u32[]{:S(2)}, u32[]{:S(2)}) async-start(bf16[8,2,128,256]{3,2,1,0:T(8,128)(2,1)} %shard_map.74.after), calls=%async_computation.2 | async-start | bytes 2097152 | tf_op jit(solution)/shard_map/all_to_all | solution.py:252
  101.7 33.9 %collective-permute-start.19 = (f32[512,256]{1,0:T(8,128)}, f32[512,256]{1,0:T(8,128)S(1)}, u32[]{:S(2)}, u32[]{:S(2)}) collective-permute-start(f32[512,256]{1,0:T(8,128)} %shard_map.75.refs_3_), channel_id=1, source_target_pairs={{0,64},{32,96},{64,0},{96,32},{1,65},{33,97},{65,1},{97,33},{2,66}... | collective-permute-start | bytes 1572872 | tf_op jit(solution)/shard_map/ppermute | solution.py:145
  116.1 13.2 %all-to-all-start.1 = ((bf16[8,1,128,256]{3,2,1,0:T(8,128)(2,1)}), bf16[8,1,128,256]{3,2,1,0:T(8,128)(2,1)S(1)}, u32[]{:S(2)}, u32[]{:S(2)}) async-start(bf16[8,1,128,256]{3,2,1,0:T(8,128)(2,1)} %shard_map.76.after), calls=%async_computation.1 | async-start | bytes 1048576 | tf_op jit(solution)/shard_map/all_to_all | solution.py:252
  120.4 15.1 %collective-permute-start.18 = (f32[512,256]{1,0:T(8,128)S(1)}, f32[512,256]{1,0:T(8,128)S(1)}, u32[]{:S(2)}, u32[]{:S(2)}) collective-permute-start(f32[512,256]{1,0:T(8,128)S(1)} %get-tuple-element.39.after), channel_id=1, source_target_pairs={{0,32},{32,64},{64,96},{96,0},{1,33},{33,65},{65,97},{97,1},{2,34}... | collective-permute-start | bytes 1572872 | tf_op jit(solution)/shard_map/ppermute | solution.py:145
  120.7 14.8 %collective-permute-start.20 = (f32[512,256]{1,0:T(8,128)}, f32[512,256]{1,0:T(8,128)S(1)}, u32[]{:S(2)}, u32[]{:S(2)}) collective-permute-start(f32[512,256]{1,0:T(8,128)} %get-tuple-element.40), channel_id=1, source_target_pairs={{0,96},{32,0},{64,32},{96,64},{1,97},{33,1},{65,33},{97,65},{2,98}... | collective-permute-start | bytes 1572872 | tf_op jit(solution)/shard_map/ppermute | solution.py:145
  (13 other events, 217.9 us)
